TPU v7x, 128 devices: a whole 4x4x4 slice. The times are simulated.
128 devices in a mesh: ctx: 32 (over z_hi, x, y), fsdp: 4 (over z_lo, core).
Axes of the slice: x: 4, y: 4, z: 4 (z_hi: 2, z_lo: 2; z = z_hi * 2 + z_lo), core: 2. Of those that a mesh axis runs over, the one named last changes fastest.
Arguments:
- tokens: bfloat16 [4, 4096, 1024], P('fsdp', 'ctx'), may hold values from -6 to 6
- cotangent: bfloat16 [4, 4096, 1024], P('fsdp', 'ctx'), may hold values from -6 to 6
- positions: int32 [4, 4096], P('fsdp'), may hold values from 0 to 3071, as said below
- seq_ids: int32 [4, 4096], P('fsdp'), may hold values from 0 to 1, as said below
- query_weight: float32 [1024, 2048], P(('ctx', 'fsdp')), may hold values from -0.1875 to 0.1875
- keyval_weight: float32 [1024, 2048], P(('ctx', 'fsdp')), may hold values from -0.1875 to 0.1875
- output_weight: float32 [2048, 1024], P(('ctx', 'fsdp')), may hold values from -0.125 to 0.125
- gateup_weight: float32 [1024, 6144], P(('ctx', 'fsdp')), may hold values from -0.1875 to 0.1875
- down_weight: float32 [3072, 1024], P(('ctx', 'fsdp')), may hold values from -0.109375 to 0.109375
- norm_gains: float32 [2304], P(('ctx', 'fsdp')), may hold values from 0.6 to 1.8
- query_mean: float32 [1024, 2048], P(('ctx', 'fsdp')), may hold values from -80 to 80
- keyval_mean: float32 [1024, 2048], P(('ctx', 'fsdp')), may hold values from -80 to 80
- output_mean: float32 [2048, 1024], P(('ctx', 'fsdp')), may hold values from -80 to 80
- gateup_mean: float32 [1024, 6144], P(('ctx', 'fsdp')), may hold values from -80 to 80
- down_mean: float32 [3072, 1024], P(('ctx', 'fsdp')), may hold values from -80 to 80
- gains_mean: float32 [2304], P(('ctx', 'fsdp')), may hold values from -80 to 80
- query_square: float32 [1024, 2048], P(('ctx', 'fsdp')), may hold values from 862 to 3449
- keyval_square: float32 [1024, 2048], P(('ctx', 'fsdp')), may hold values from 862 to 3449
- output_square: float32 [2048, 1024], P(('ctx', 'fsdp')), may hold values from 862 to 3449
- gateup_square: float32 [1024, 6144], P(('ctx', 'fsdp')), may hold values from 862 to 3449
- down_square: float32 [3072, 1024], P(('ctx', 'fsdp')), may hold values from 862 to 3449
- gains_square: float32 [2304], P(('ctx', 'fsdp')), may hold values from 862 to 3449
Outputs:
- block_output: bfloat16 [4, 4096, 1024], P('fsdp', 'ctx')
- token_gradient: float32 [4, 4096, 1024], P('fsdp', 'ctx')
- query_gradient: float32 [1024, 2048], P(('ctx', 'fsdp'))
- keyval_gradient: float32 [1024, 2048], P(('ctx', 'fsdp'))
- output_gradient: float32 [2048, 1024], P(('ctx', 'fsdp'))
- gateup_gradient: float32 [1024, 6144], P(('ctx', 'fsdp'))
- down_gradient: float32 [3072, 1024], P(('ctx', 'fsdp'))
- gains_gradient: float32 [2304], P(('ctx', 'fsdp'))
- query_new: float32 [1024, 2048], P(('ctx', 'fsdp'))
- keyval_new: float32 [1024, 2048], P(('ctx', 'fsdp'))
- output_new: float32 [2048, 1024], P(('ctx', 'fsdp'))
- gateup_new: float32 [1024, 6144], P(('ctx', 'fsdp'))
- down_new: float32 [3072, 1024], P(('ctx', 'fsdp'))
- gains_new: float32 [2304], P(('ctx', 'fsdp'))
- query_mean_new: float32 [1024, 2048], P(('ctx', 'fsdp'))
- keyval_mean_new: float32 [1024, 2048], P(('ctx', 'fsdp'))
- output_mean_new: float32 [2048, 1024], P(('ctx', 'fsdp'))
- gateup_mean_new: float32 [1024, 6144], P(('ctx', 'fsdp'))
- down_mean_new: float32 [3072, 1024], P(('ctx', 'fsdp'))
- gains_mean_new: float32 [2304], P(('ctx', 'fsdp'))
- query_square_new: float32 [1024, 2048], P(('ctx', 'fsdp'))
- keyval_square_new: float32 [1024, 2048], P(('ctx', 'fsdp'))
- output_square_new: float32 [2048, 1024], P(('ctx', 'fsdp'))
- gateup_square_new: float32 [1024, 6144], P(('ctx', 'fsdp'))
- down_square_new: float32 [3072, 1024], P(('ctx', 'fsdp'))
- gains_square_new: float32 [2304], P(('ctx', 'fsdp'))
Inputs may be any that keep to these rules, and one draw needn't show every extreme that they name: Each pack holds a sequence of 3072 tokens, then one of 1024, cut in order into 64 blocks of 64 tokens; the 128 rows of the i-th device of ctx hold a block b and then the block 63 - b, with b drawn per device and pack, each b once. positions gives a token's place in its sequence. `seq_ids`: 0 for the first sequence of the pack, 1 for the second, in the layout stated for positions.
All inputs are finite; a program needn't handle non-finite values.
Results may differ from a plain program's by a relative error of at most 0.02.
The roundings to bfloat16 on the way count: a program that leaves them out, or rounds other values in their place, can miss the bound.
Values may be sent and summed in bfloat16 or wider, within the bound.
A program may use at most 320 MiB of HBM per device.

v0:
```python
from functools import partial

import jax
import jax.numpy as jnp
from jax import lax
from jax.sharding import PartitionSpec as P

D = 1024
H = 16
KVH = 8
HD = 128
FF = 3072
KV = 1024
STEP = 10


NORM_EPS = 1e-06
ROPE_BASE = 1000000.0
BETA_ONE = 0.9
BETA_TWO = 0.95
ADAM_EPS = 1e-08
DECAY = 0.1
RATE_MATRIX = 0.1
RATE_GAIN = 0.3


def side_by_side(arrays, axis, dim, along):
    ends, at = ([], 0)
    for a in arrays[:-1]:
        at += a.shape[along]
        ends.append(at)
    both = jnp.concatenate(arrays, axis=along)
    return tuple(jnp.split(lax.all_gather(both, axis, axis=dim, tiled=True), ends, axis=along))


def joined_along(pieces, dim):
    pieces = jnp.moveaxis(pieces, 0, dim)
    dims = pieces.shape
    return pieces.reshape(*dims[:dim], dims[dim] * dims[dim + 1], *dims[dim + 2 :])


def gather_together(arrays, axis, dims):
    vector = jnp.concatenate([a.reshape(-1) for a in arrays])
    lines, at, finished = (lax.all_gather(vector, axis), 0, [])
    for a, dim in zip(arrays, dims):
        pieces = lines[:, at : at + a.size].reshape(-1, *a.shape)
        finished.append(joined_along(pieces, dim))
        at += a.size
    return tuple(finished)


def in_blocks(x, dim, peers):
    before, after = (x.shape[:dim], x.shape[dim + 1 :])
    return jnp.moveaxis(x.reshape(*before, peers, -1, *after), dim, 0)


def sum_together(arrays, axis, dims):
    peers = lax.axis_size(axis)
    pieces = [in_blocks(a, dim, peers) for a, dim in zip(arrays, dims)]
    lines = jnp.concatenate([b.reshape(peers, -1) for b in pieces], axis=1)
    extent = max(16, -(-lines.shape[1] // 1024) * 8)
    lines = jnp.pad(lines, ((0, 0), (0, extent * 128 - lines.shape[1]))).reshape(-1, 128)
    vector, at, finished = (lax.psum_scatter(lines, axis, tiled=True).reshape(-1), 0, [])
    for b in pieces:
        part = b[0]
        finished.append(vector[at : at + part.size].reshape(part.shape))
        at += part.size
    return tuple(finished)


def in_one_piece(arrays, axis, dim, along):
    ends, at = ([], 0)
    for a in arrays[:-1]:
        at += a.shape[along]
        ends.append(at)
    both = jnp.concatenate(arrays, axis=along)
    return tuple(
        jnp.split(lax.psum_scatter(both, axis, scatter_dimension=dim, tiled=True), ends, axis=along)
    )


def rms_norm(values, norm_gain):
    factor = lax.rsqrt(jnp.mean(values * values, axis=-1, keepdims=True) + NORM_EPS)
    return values * factor * norm_gain


def rotate(values, places):
    halfway = values.shape[-1] // 2
    frequency = ROPE_BASE ** (-jnp.arange(halfway, dtype=jnp.float32) * 2.0 / values.shape[-1])
    angles = places.astype(jnp.float32)[:, None] * frequency[None, :]
    cosine = jnp.cos(angles)[:, None, :]
    sine_part = jnp.sin(angles)[:, None, :]
    leading = values[..., :halfway]
    trailing = values[..., halfway:]
    return jnp.concatenate(
        [leading * cosine - trailing * sine_part, trailing * cosine + leading * sine_part], axis=-1
    )


def head_prepare(projected, norm_gain, places):
    row_count = projected.shape[0]
    heads = projected.shape[1] // HD
    shaped = projected.reshape(row_count, heads, HD)
    return rotate(rms_norm(shaped, norm_gain), places).reshape(row_count, heads * HD)


def swiglu(gate_up):
    return jax.nn.silu(gate_up[:, :FF]) * gate_up[:, FF:]


def inner_rows(left, right):
    return lax.dot_general(
        left, right, (((0,), (0,)), ((), ())), preferred_element_type=jnp.float32
    )


def times_transpose(left, right):
    return lax.dot_general(
        left, right, (((1,), (1,)), ((), ())), preferred_element_type=jnp.float32
    )


def head_scores(query_rows, key_rows, allowed):
    scores = jnp.einsum(
        "tgd,kd->gtk", query_rows, key_rows, preferred_element_type=jnp.float32
    ) * HD ** (-0.5)
    return jnp.where(allowed[None], scores, -1e30)


def head_slices(query_use, key_all, value_all, head_index):
    row_count = query_use.shape[0]
    per_group = H // KVH
    head_width = per_group * HD
    query_rows = lax.dynamic_slice_in_dim(
        query_use, head_index * head_width, head_width, 1
    ).reshape(row_count, per_group, HD)
    key_rows = lax.dynamic_slice_in_dim(key_all, head_index * HD, HD, 1)
    value_rows = lax.dynamic_slice_in_dim(value_all, head_index * HD, HD, 1)
    return (query_rows, key_rows, value_rows)


def attend_forward(query_use, key_all, value_all, allowed):
    row_count = query_use.shape[0]
    per_group = H // KVH
    head_width = per_group * HD

    def per_head(head_index, state_pair):
        attended, totals = state_pair
        query_rows, key_rows, value_rows = head_slices(query_use, key_all, value_all, head_index)
        scores = head_scores(query_rows, key_rows, allowed)
        summed = jax.nn.logsumexp(scores, axis=-1)
        weights = jnp.exp(scores - summed[..., None]).astype(jnp.bfloat16)
        result = jnp.einsum(
            "gtk,kd->tgd", weights, value_rows, preferred_element_type=jnp.float32
        ).reshape(row_count, head_width)
        attended = lax.dynamic_update_slice_in_dim(attended, result, head_index * head_width, 1)
        totals = lax.dynamic_update_index_in_dim(totals, summed, head_index, 0)
        return (attended, totals)

    initial = (
        jnp.zeros((row_count, H * HD), jnp.float32),
        jnp.zeros((KVH, per_group, row_count), jnp.float32),
    )
    return lax.fori_loop(0, KVH, per_head, initial)


def attend_backward(query_use, key_all, value_all, allowed, totals, grad_attended):
    row_count = query_use.shape[0]
    key_count = key_all.shape[0]
    per_group = H // KVH
    head_width = per_group * HD

    def per_head(head_index, state_triple):
        grad_query, grad_key, grad_value = state_triple
        query_rows, key_rows, value_rows = head_slices(query_use, key_all, value_all, head_index)
        grad_rows = lax.dynamic_slice_in_dim(
            grad_attended, head_index * head_width, head_width, 1
        ).reshape(row_count, per_group, HD)
        scores = head_scores(query_rows, key_rows, allowed)
        summed = lax.dynamic_index_in_dim(totals, head_index, 0, keepdims=False)
        probs = jnp.exp(scores - summed[..., None])
        grad_probs = jnp.einsum(
            "tgd,kd->gtk", grad_rows, value_rows, preferred_element_type=jnp.float32
        )
        inner = jnp.sum(probs * grad_probs, axis=-1, keepdims=True)
        grad_scores = (probs * (grad_probs - inner)).astype(jnp.bfloat16)
        query_part = jnp.einsum(
            "gtk,kd->tgd", grad_scores, key_rows, preferred_element_type=jnp.float32
        ) * HD ** (-0.5)
        key_part = jnp.einsum(
            "gtk,tgd->kd", grad_scores, query_rows, preferred_element_type=jnp.float32
        ) * HD ** (-0.5)
        value_part = jnp.einsum(
            "gtk,tgd->kd", probs.astype(jnp.bfloat16), grad_rows, preferred_element_type=jnp.float32
        )
        grad_query = lax.dynamic_update_slice_in_dim(
            grad_query, query_part.reshape(row_count, head_width), head_index * head_width, 1
        )
        grad_key = lax.dynamic_update_slice_in_dim(grad_key, key_part, head_index * HD, 1)
        grad_value = lax.dynamic_update_slice_in_dim(grad_value, value_part, head_index * HD, 1)
        return (grad_query, grad_key, grad_value)

    initial = (
        jnp.zeros((row_count, H * HD), jnp.float32),
        jnp.zeros((key_count, KVH * HD), jnp.float32),
        jnp.zeros((key_count, KVH * HD), jnp.float32),
    )
    return lax.fori_loop(0, KVH, per_head, initial)


def adam_update(weight, gradient, mean_old, square_old, rate, decay):
    mean_new = BETA_ONE * mean_old + (1.0 - BETA_ONE) * gradient
    square_new = BETA_TWO * square_old + (1.0 - BETA_TWO) * gradient * gradient
    mean_hat = mean_new / (1.0 - BETA_ONE**STEP)
    square_hat = square_new / (1.0 - BETA_TWO**STEP)
    weight_new = weight - rate * (mean_hat / (jnp.sqrt(square_hat) + ADAM_EPS) + decay * weight)
    return (weight_new, mean_new, square_new)


def body(
    tokens,
    cotangent,
    positions,
    seq_ids,
    query_weight,
    keyval_weight,
    output_weight,
    gateup_weight,
    down_weight,
    norm_gains,
    query_mean,
    keyval_mean,
    output_mean,
    gateup_mean,
    down_mean,
    gains_mean,
    query_square,
    keyval_square,
    output_square,
    gateup_square,
    down_square,
    gains_square,
):
    inputs = tokens[0]
    upstream = cotangent[0].astype(jnp.float32)
    row_count = inputs.shape[0]
    offset = lax.axis_index("ctx") * row_count
    key_places = positions[0]
    key_labels = seq_ids[0]
    places = lax.dynamic_slice_in_dim(key_places, offset, row_count)
    labels = lax.dynamic_slice_in_dim(key_labels, offset, row_count)
    allowed = (labels[:, None] == key_labels[None, :]) & (key_places[None, :] <= places[:, None])
    attn_low = (
        query_weight.astype(jnp.bfloat16),
        keyval_weight.astype(jnp.bfloat16),
        output_weight.astype(jnp.bfloat16),
        norm_gains.astype(jnp.bfloat16),
    )
    ffn_low = (gateup_weight.astype(jnp.bfloat16), down_weight.astype(jnp.bfloat16))
    query_full, keyval_full, output_full, gains_full = (
        *side_by_side((attn_low[0], attn_low[1]), ("ctx", "fsdp"), 0, 1),
        lax.all_gather(attn_low[2], ("ctx", "fsdp"), axis=0, tiled=True),
        lax.all_gather(attn_low[3], ("ctx", "fsdp"), axis=0, tiled=True),
    )
    gains_all = gains_full.astype(jnp.float32)
    attn_gain = gains_all[:D]
    ffn_gain = gains_all[D : 2 * D]
    query_gain = gains_all[2 * D : 2 * D + HD]
    key_gain = gains_all[2 * D + HD :]
    query_proj = jnp.dot(inputs, query_full, preferred_element_type=jnp.float32)
    keyval_proj = jnp.dot(inputs, keyval_full, preferred_element_type=jnp.float32)
    query_use = head_prepare(query_proj, query_gain, places).astype(jnp.bfloat16)
    key_use = head_prepare(keyval_proj[:, :KV], key_gain, places).astype(jnp.bfloat16)
    value_use = keyval_proj[:, KV:].astype(jnp.bfloat16)
    key_all, value_all = side_by_side((key_use, value_use), "ctx", 0, 1)
    attended, totals = attend_forward(query_use, key_all, value_all, allowed)
    attended_low = attended.astype(jnp.bfloat16)
    branch = jnp.dot(attended_low, output_full, preferred_element_type=jnp.float32)
    hidden = inputs.astype(jnp.float32) + rms_norm(branch, attn_gain)
    hidden_low = hidden.astype(jnp.bfloat16)
    gateup_full, down_full = gather_together((ffn_low[0], ffn_low[1]), ("ctx", "fsdp"), (0, 0))
    gate_up = jnp.dot(hidden_low, gateup_full, preferred_element_type=jnp.float32)
    activated = swiglu(gate_up).astype(jnp.bfloat16)
    ffn_out = jnp.dot(activated, down_full, preferred_element_type=jnp.float32)
    result = hidden + rms_norm(ffn_out, ffn_gain)
    ffn_norm_out, ffn_pull = jax.vjp(rms_norm, ffn_out, ffn_gain)
    grad_ffn_out, grad_ffn_gain = ffn_pull(upstream)
    grad_ffn_low = grad_ffn_out.astype(jnp.bfloat16)
    down_grad = inner_rows(activated, grad_ffn_low)
    grad_act = times_transpose(grad_ffn_low, down_full)
    act_out, act_pull = jax.vjp(swiglu, gate_up)
    grad_gate_up = act_pull(grad_act)[0]
    grad_gate_low = grad_gate_up.astype(jnp.bfloat16)
    gateup_grad = inner_rows(hidden_low, grad_gate_low)
    grad_hidden = upstream + times_transpose(grad_gate_low, gateup_full)
    gateup_sum, down_sum = sum_together((gateup_grad, down_grad), ("ctx", "fsdp"), (0, 0))
    attn_norm_out, attn_pull = jax.vjp(rms_norm, branch, attn_gain)
    grad_branch, grad_attn_gain = attn_pull(grad_hidden)
    grad_branch_low = grad_branch.astype(jnp.bfloat16)
    output_grad = inner_rows(attended_low, grad_branch_low)
    grad_attended = times_transpose(grad_branch_low, output_full).astype(jnp.bfloat16)
    grad_query_use, grad_key_all, grad_value_all = attend_backward(
        query_use, key_all, value_all, allowed, totals, grad_attended
    )
    grad_key_use, grad_value = in_one_piece((grad_key_all, grad_value_all), "ctx", 0, 1)
    query_out, query_pull = jax.vjp(partial(head_prepare, places=places), query_proj, query_gain)
    grad_query_proj, grad_query_gain = query_pull(grad_query_use)
    key_out, key_pull = jax.vjp(partial(head_prepare, places=places), keyval_proj[:, :KV], key_gain)
    grad_key_proj, grad_key_gain = key_pull(grad_key_use)
    grad_query_low = grad_query_proj.astype(jnp.bfloat16)
    grad_keyval_low = jnp.concatenate([grad_key_proj, grad_value], axis=1).astype(jnp.bfloat16)
    query_grad = inner_rows(inputs, grad_query_low)
    keyval_grad = inner_rows(inputs, grad_keyval_low)
    token_grad = (
        grad_hidden
        + times_transpose(grad_query_low, query_full)
        + times_transpose(grad_keyval_low, keyval_full)
    )
    gains_grad = jnp.concatenate([grad_attn_gain, grad_ffn_gain, grad_query_gain, grad_key_gain])
    query_sum, keyval_sum, output_sum, gains_sum = sum_together(
        (query_grad, keyval_grad, output_grad, gains_grad), ("ctx", "fsdp"), (0, 0, 0, 0)
    )
    query_new, query_mean_new, query_square_new = adam_update(
        query_weight, query_sum, query_mean, query_square, RATE_MATRIX, DECAY
    )
    keyval_new, keyval_mean_new, keyval_square_new = adam_update(
        keyval_weight, keyval_sum, keyval_mean, keyval_square, RATE_MATRIX, DECAY
    )
    output_new, output_mean_new, output_square_new = adam_update(
        output_weight, output_sum, output_mean, output_square, RATE_MATRIX, DECAY
    )
    gateup_new, gateup_mean_new, gateup_square_new = adam_update(
        gateup_weight, gateup_sum, gateup_mean, gateup_square, RATE_MATRIX, DECAY
    )
    down_new, down_mean_new, down_square_new = adam_update(
        down_weight, down_sum, down_mean, down_square, RATE_MATRIX, DECAY
    )
    gains_new, gains_mean_new, gains_square_new = adam_update(
        norm_gains, gains_sum, gains_mean, gains_square, RATE_GAIN, 0.0
    )
    return (
        result.astype(jnp.bfloat16)[None],
        token_grad[None],
        query_sum,
        keyval_sum,
        output_sum,
        gateup_sum,
        down_sum,
        gains_sum,
        query_new,
        keyval_new,
        output_new,
        gateup_new,
        down_new,
        gains_new,
        query_mean_new,
        keyval_mean_new,
        output_mean_new,
        gateup_mean_new,
        down_mean_new,
        gains_mean_new,
        query_square_new,
        keyval_square_new,
        output_square_new,
        gateup_square_new,
        down_square_new,
        gains_square_new,
    )


def solution(mesh):
    in_specs = (
        P("fsdp", "ctx", None),
        P("fsdp", "ctx", None),
        P("fsdp", None),
        P("fsdp", None),
        P(("ctx", "fsdp"), None),
        P(("ctx", "fsdp"), None),
        P(("ctx", "fsdp"), None),
        P(("ctx", "fsdp"), None),
        P(("ctx", "fsdp"), None),
        P(("ctx", "fsdp")),
        P(("ctx", "fsdp"), None),
        P(("ctx", "fsdp"), None),
        P(("ctx", "fsdp"), None),
        P(("ctx", "fsdp"), None),
        P(("ctx", "fsdp"), None),
        P(("ctx", "fsdp")),
        P(("ctx", "fsdp"), None),
        P(("ctx", "fsdp"), None),
        P(("ctx", "fsdp"), None),
        P(("ctx", "fsdp"), None),
        P(("ctx", "fsdp"), None),
        P(("ctx", "fsdp")),
    )
    out_specs = (
        P("fsdp", "ctx", None),
        P("fsdp", "ctx", None),
        P(("ctx", "fsdp"), None),
        P(("ctx", "fsdp"), None),
        P(("ctx", "fsdp"), None),
        P(("ctx", "fsdp"), None),
        P(("ctx", "fsdp"), None),
        P(("ctx", "fsdp")),
        P(("ctx", "fsdp"), None),
        P(("ctx", "fsdp"), None),
        P(("ctx", "fsdp"), None),
        P(("ctx", "fsdp"), None),
        P(("ctx", "fsdp"), None),
        P(("ctx", "fsdp")),
        P(("ctx", "fsdp"), None),
        P(("ctx", "fsdp"), None),
        P(("ctx", "fsdp"), None),
        P(("ctx", "fsdp"), None),
        P(("ctx", "fsdp"), None),
        P(("ctx", "fsdp")),
        P(("ctx", "fsdp"), None),
        P(("ctx", "fsdp"), None),
        P(("ctx", "fsdp"), None),
        P(("ctx", "fsdp"), None),
        P(("ctx", "fsdp"), None),
        P(("ctx", "fsdp")),
    )
    return jax.shard_map(body, mesh=mesh, in_specs=in_specs, out_specs=out_specs, check_vma=False)
```

profile of v0, /device:TPU:1, one launch (start us, length us, event | category | flops | bytes accessed | tf_op | source)
XLA Modules:
  0.0 2361.8 jit_solution(11439635839446447)
XLA Ops:
  13.1 68.9 %all-reduce.7 = bf16[2304]{0:T(1024)(128)(2,1)S(1)} all-reduce(bf16[2304]{0:T(1024)(128)(2,1)S(1)} %dynamic-update-slice), channel_id=1, replica_groups=mesh['ctx'=32,'fsdp'=4] {'ctx','fsdp'}, use_global_device_ids=true, to_apply=%add.7 | all-reduce | flops 2304 | bytes 9216
  82.9 133.8 %all-gather.6.cloned.1.call-done = bf16[1024,4096]{1,0:T(8,128)(2,1)} async-done(((bf16[8,4096]{1,0:T(8,128)(2,1)}), bf16[1024,4096]{1,0:T(8,128)(2,1)}) %all-gather.6.cloned.1.call-update) | async-done | bytes 8388624 | tf_op jit(solution)/shard_map/all_gather | solution.py:33
  228.2 207.6 %all-gather.12.cloned.1.call-done = bf16[9437184]{0:T(1024)(128)(2,1)} async-done(((bf16[73728]{0:T(1024)(128)(2,1)}), bf16[9437184]{0:T(1024)(128)(2,1)}) %all-gather.12.cloned.1.call-update) | async-done | bytes 18874384 | tf_op jit(solution)/shard_map/all_gather | solution.py:44
  435.8 21.7 reshape.370
  457.5 10.5 slice.98
  473.9 17.3 reshape_reshape.21
  500.2 167.2 %all-gather.8.cloned.1.call-done = bf16[4096,2048]{0,1:T(8,128)(2,1)} async-done(((bf16[128,2048]{0,1:T(8,128)(2,1)}), bf16[4096,2048]{0,1:T(8,128)(2,1)}) %all-gather.8.cloned.1.call-update) | async-done | bytes 16777232 | tf_op jit(solution)/shard_map/all_gather | solution.py:33
  667.4 11.8 fusion.99
  679.2 12.0 copy.83
  691.1 54.9 %while.34 = (s32[]{:T(128)}, bf16[128,2048]{0,1:T(8,128)(2,1)S(1)}, f32[8,2,128]{2,1,0:T(2,128)}, bf16[4096,1024]{0,1:T(8,128)(2,1)}, bf16[4096,1024]{1,0:T(8,12...) while((s32[]{:T(128)}, bf16[128,2048]{0,1:T(8,128)(2,1)S(1)}, ...), condition=%wide.region_5.6_spmd.clone, body=%wide.region_2.5_spmd.clone.sunk | while | flops 545785856 | bytes 16168205 | solution.py:164
  746.1 120.7 %all-gather.10.cloned.1.call-done = bf16[2048,1024]{1,0:T(8,128)(2,1)} async-done(((bf16[16,1024]{1,0:T(8,128)(2,1)}), bf16[2048,1024]{1,0:T(8,128)(2,1)}) %all-gather.10.cloned.1.call-update) | async-done | bytes 4194320 | tf_op jit(solution)/shard_map/all_gather | solution.py:262
  882.7 10.2 multiply_reduce_fusion.5
  912.4 119.9 %while.35 = (s32[]{:T(128)}, f32[128,2048]{0,1:T(8,128)S(1)}, f32[4096,1024]{1,0:T(8,128)}, f32[4096,1024]{1,0:T(8,128)}, bf16[4096,1024]{1,0:T(8,128)(2,1)}, /*...) while((s32[]{:T(128)}, f32[128,2048]{0,1:T(8,128)S(1)}, ...), condition=%wide.region_12.13_spmd.clone, body=%wide.region_10.12_spmd.clone.sunk | while | flops 1353744128 | bytes 41003400 | solution.py:208
  1032.3 23.2 pad_maximum_fusion.1
  1062.9 12.4 reshape_reshape.27
  1075.4 11.8 fusion.75
  1087.1 23.5 reshape_reshape.26
  1110.6 25.0 %pad_maximum_fusion = f32[128,73728]{1,0:T(8,128)} fusion(f32[128,24576]{1,0:T(8,128)} %reshape_reshape.27, f32[128,49152]{1,0:T(8,128)} %reshape_reshape.26), kind=kLoop, calls=%fused_computation.54 | loop fusion | flops 9437184 | bytes 75497472 | tf_op jit(solution)/shard_map/concatenate | solution.py:60
  1135.6 31.0 %reshape.365 = f32[73728,128]{1,0:T(8,128)} reshape(f32[128,73728]{1,0:T(8,128)} %pad_maximum_fusion) | data formatting | bytes 75497472 | tf_op jit(solution)/shard_map/reshape | solution.py:62
  1206.3 214.3 %reduce-scatter.3.cloned.1.call-done = f32[128,2048]{1,0:T(8,128)} async-done(((f32[4096,2048]{1,0:T(8,128)}), f32[128,2048]{1,0:T(8,128)}) %reduce-scatter.3.cloned.1.call-update) | async-done | bytes 1048592 | tf_op jit(solution)/shard_map/reduce_scatter | solution.py:78
  1447.0 18.5 select_maximum_fusion
  1465.5 23.6 reshape.361
  1499.0 612.5 %reduce-scatter.5.cloned.1.call-done = f32[576,128]{1,0:T(8,128)} async-done(((f32[73728,128]{1,0:T(8,128)}), f32[576,128]{1,0:T(8,128)}) %reduce-scatter.5.cloned.1.call-update) | async-done | bytes 294928 | tf_op jit(solution)/shard_map/reduce_scatter | solution.py:63
  2115.2 235.1 %all-reduce.11.cloned.1.call-done = f32[50176,128]{1,0:T(8,128)} async-done(((f32[50176,128]{1,0:T(8,128)}), f32[50176,128]{1,0:T(8,128)}) %all-reduce.11.cloned.1.call-update) | async-done | bytes 25690128
  (462 shorter events, 332.4 us)
Async XLA Ops:
  7.2 209.5 %all-gather.6.cloned.1.call-start = ((), (), s32[]{:S(2)}) async-start(), calls=%async_computation.2 | async-start | bytes 8454144 | tf_op jit(solution)/shard_map/all_gather | solution.py:33
  9.6 426.2 %all-gather.12.cloned.1.call-start = ((), (), s32[]{:S(2)}) async-start(), calls=%async_computation.7 | async-start | bytes 19021824 | tf_op jit(solution)/shard_map/all_gather | solution.py:44
  12.2 655.2 %all-gather.8.cloned.1.call-start = ((), (), s32[]{:S(2)}) async-start(), calls=%async_computation.3 | async-start | bytes 17301504 | tf_op jit(solution)/shard_map/all_gather | solution.py:33
  222.4 644.5 %all-gather.10.cloned.1.call-start = ((), (), s32[]{:S(2)}) async-start(), calls=%async_computation.4 | async-start | bytes 4227072 | tf_op jit(solution)/shard_map/all_gather | solution.py:262
  223.1 1197.5 %reduce-scatter.3.cloned.1.call-start = ((), (), s32[]{:S(2)}) async-start(), calls=%async_computation.5 | async-start | bytes 34603008 | tf_op jit(solution)/shard_map/reduce_scatter | solution.py:78
  1055.5 1056.0 %reduce-scatter.5.cloned.1.call-start = ((), (), s32[]{:S(2)}) async-start(), calls=%async_computation.6 | async-start | bytes 38043648 | tf_op jit(solution)/shard_map/reduce_scatter | solution.py:63
  1166.6 1183.7 %all-reduce.11.cloned.1.call-start = ((), (), s32[]{:S(2)}) async-start(), calls=%async_computation.8 | async-start | bytes 51380224
  1493.9 619.6 %copy-start.30 = (f32[24,1024]{1,0:T(8,128)S(1)}, f32[24,1024]{1,0:T(8,128)}, u32[]{:S(2)}) copy-start(f32[24,1024]{1,0:T(8,128)} %param.34) | copy-start | bytes 294916
  1493.9 619.6 %copy-start.43 = (f32[24,1024]{1,0:T(8,128)S(1)}, f32[24,1024]{1,0:T(8,128)}, u32[]{:S(2)}) copy-start(f32[24,1024]{1,0:T(8,128)} %param.40) | copy-start | bytes 294916
  1494.0 620.4 %copy-start.28 = (f32[8,6144]{1,0:T(8,128)S(1)}, f32[8,6144]{1,0:T(8,128)}, u32[]{:S(2)}) copy-start(f32[8,6144]{1,0:T(8,128)} %param.33) | copy-start | bytes 589828
  1494.0 620.4 %copy-start.39 = (f32[8,6144]{1,0:T(8,128)S(1)}, f32[8,6144]{1,0:T(8,128)}, u32[]{:S(2)}) copy-start(f32[8,6144]{1,0:T(8,128)} %param.39) | copy-start | bytes 589828
  1494.0 620.3 %copy-start.40 = (f32[8,6144]{1,0:T(8,128)S(1)}, f32[8,6144]{1,0:T(8,128)}, u32[]{:S(2)}) copy-start(f32[8,6144]{1,0:T(8,128)} %param.45) | copy-start | bytes 589828
  1494.0 858.4 %copy-start.67 = (f32[18]{0:T(128)S(1)}, f32[18]{0:T(128)}, u32[]{:S(2)}) copy-start(f32[18]{0:T(128)} %param.35) | copy-start | bytes 220
  1494.0 858.4 %copy-start.68 = (f32[18]{0:T(128)S(1)}, f32[18]{0:T(128)}, u32[]{:S(2)}) copy-start(f32[18]{0:T(128)} %param.41) | copy-start | bytes 220
  1494.0 858.4 %copy-start.69 = (f32[18]{0:T(128)S(1)}, f32[18]{0:T(128)}, u32[]{:S(2)}) copy-start(f32[18]{0:T(128)} %param.47) | copy-start | bytes 220
  1494.0 858.9 %copy-start.37 = (f32[16,1024]{1,0:T(8,128)S(1)}, f32[16,1024]{1,0:T(8,128)}, u32[]{:S(2)}) copy-start(f32[16,1024]{1,0:T(8,128)} %param.32) | copy-start | bytes 196612
  1494.0 858.9 %copy-start.51 = (f32[16,1024]{1,0:T(8,128)S(1)}, f32[16,1024]{1,0:T(8,128)}, u32[]{:S(2)}) copy-start(f32[16,1024]{1,0:T(8,128)} %param.38) | copy-start | bytes 196612
  1494.1 858.9 %copy-start.52 = (f32[16,1024]{1,0:T(8,128)S(1)}, f32[16,1024]{1,0:T(8,128)}, u32[]{:S(2)}) copy-start(f32[16,1024]{1,0:T(8,128)} %param.44) | copy-start | bytes 196612
  1494.1 859.6 %copy-start.32 = (f32[8,2048]{1,0:T(8,128)S(1)}, f32[8,2048]{1,0:T(8,128)}, u32[]{:S(2)}) copy-start(f32[8,2048]{1,0:T(8,128)} %param.31) | copy-start | bytes 196612
  1494.1 859.6 %copy-start.33 = (f32[8,2048]{1,0:T(8,128)S(1)}, f32[8,2048]{1,0:T(8,128)}, u32[]{:S(2)}) copy-start(f32[8,2048]{1,0:T(8,128)} %param.30) | copy-start | bytes 196612
  1494.1 859.6 %copy-start.47 = (f32[8,2048]{1,0:T(8,128)S(1)}, f32[8,2048]{1,0:T(8,128)}, u32[]{:S(2)}) copy-start(f32[8,2048]{1,0:T(8,128)} %param.37) | copy-start | bytes 196612
  1494.1 859.6 %copy-start.48 = (f32[8,2048]{1,0:T(8,128)S(1)}, f32[8,2048]{1,0:T(8,128)}, u32[]{:S(2)}) copy-start(f32[8,2048]{1,0:T(8,128)} %param.43) | copy-start | bytes 196612
  1494.1 859.6 %copy-start.49 = (f32[8,2048]{1,0:T(8,128)S(1)}, f32[8,2048]{1,0:T(8,128)}, u32[]{:S(2)}) copy-start(f32[8,2048]{1,0:T(8,128)} %param.42) | copy-start | bytes 196612
  1494.1 859.6 %copy-start.50 = (f32[8,2048]{1,0:T(8,128)S(1)}, f32[8,2048]{1,0:T(8,128)}, u32[]{:S(2)}) copy-start(f32[8,2048]{1,0:T(8,128)} %param.36) | copy-start | bytes 196612
  (77 other events, 4894.8 us)
Sparse Core Ops, SparseCore 0:
  10.3 206.3 all-gather.5
  219.0 216.7 all-gather.11
  439.2 228.2 all-gather.7
  669.6 197.2 all-gather.9
  1055.6 364.9 reduce-scatter.2
  1422.9 688.5 reduce-scatter.4
  2117.0 233.2 all-reduce.10
where the time goes:
time: 2380 us; the launch traced here: 2360 us
  waiting for transfers between devices  1690 us (71%)
  local copies, waits for them, and re-layouts  274 us (12%)
  matrix products  192 us (8%)
  other arithmetic  118 us (5%)
  blocking collectives  68.9 us (3%)
    reduce_scatter x1, waiting for transfers between devices, sum_together(): lax.psum_scatter(lines, axis, tiled=True).reshape(-1)  612 us
    all_gather x2, waiting for transfers between devices, side_by_side(): lax.all_gather(both, axis, axis=dim, tiled=True)  301 us
    unnamed x8, waiting for transfers between devices  235 us
    reduce_scatter x1, waiting for transfers between devices, in_one_piece(): lax.psum_scatter(both, axis, scatter_dimension=dim, tiled=True)  214 us
    all_gather x1, waiting for transfers between devices, gather_together(): lines, at, finished = (lax.all_gather(vector, axis), 0, [])  208 us
    all_gather x1, waiting for transfers between devices, body(): lax.all_gather(attn_low[2], ('ctx', 'fsdp'), axis=0, tiled=True)  121 us
    unnamed x1, blocking collectives  68.9 us
    another operation x5, local copies, waits for them, and re-layouts, sum_together(): lines = jnp.concatenate([b.reshape(peers, -1) for b in pieces], axis=1)  64.7 us
  transfers between devices with their start and end apart: 7, of which 7 were waited for; matrix products, arithmetic and copies ran while one was open for 16% of the time, Pallas kernels for 0%

commit v1 on v0

v1 whole, which is shorter than its diff:
```python
import functools
import math

import jax
import jax.numpy as jnp
from jax import lax
from jax.experimental import pallas as pl
from jax.experimental.pallas import tpu as pltpu
from jax.sharding import Mesh
from jax.sharding import PartitionSpec as P

D = 1024
H = 16
KVH = 8
HD = 128
FF = 3072
KV = 1024
STEP = 10
LONG = 3072
ROWS = 128
BLOCK = 64
CHUNK = 512
PACK_TOK = 4096
RANKS = 8
PLANE = 16


NORM_EPS = 1e-06
ROPE_BASE = 1000000.0
BETA_ONE = 0.9
BETA_TWO = 0.95
ADAM_EPS = 1e-08
DECAY = 0.1
RATE_MATRIX = 0.1
RATE_GAIN = 0.3

SCALE = HD**-0.5
LOG2E = math.log2(math.e)

AXES = ("zh", "x", "y", "zl", "co")
SIZE = {"zh": 2, "x": 4, "y": 4, "zl": 2, "co": 2}
COLUMN = ("zh", "zl", "co")
SURFACE = ("x", "y")
MESH = pl.DeviceIdType.MESH
F32 = jnp.float32
BF16 = jnp.bfloat16
VMEM_LIMIT = 50 * 1024 * 1024


def where_am_i():
    return {a: lax.axis_index(a) for a in AXES}


def address(place):
    return tuple(place[a] for a in AXES)


def flat_index(place, axes):
    at = 0
    for a in axes:
        at = at * SIZE[a] + place[a]
    return at


def shifted(place, axes, k, sign):
    to = dict(place)
    for a in reversed(axes):
        step = lax.rem(k, SIZE[a])
        k = lax.div(k, SIZE[a])
        to[a] = lax.rem(place[a] + sign * step + SIZE[a], SIZE[a])
    return to


def push_kernel(channels, n_in, n_out, *refs):
    ins, outs = refs[:n_in], refs[n_in : n_in + n_out]
    sems = refs[n_in + n_out :]
    me = where_am_i()
    barrier = pltpu.get_barrier_semaphore()
    greeted = max((c[2] for c in channels), key=len)
    peers = math.prod(SIZE[a] for a in greeted)

    def greet(k, carry):
        pl.semaphore_signal(
            barrier, inc=1, device_id=address(shifted(me, greeted, k, 1)), device_id_type=MESH
        )
        return carry

    lax.fori_loop(1, peers, greet, 0)
    own = []
    for i, (src, dst, axes, take, put) in enumerate(channels):
        copy = pltpu.make_async_copy(take(ins[src], me), put(outs[dst], me), sems[3 * i + 2])
        copy.start()
        own.append(copy)
    pl.semaphore_wait(barrier, peers - 1)
    for i, (src, dst, axes, take, put) in enumerate(channels):
        n = math.prod(SIZE[a] for a in axes)
        mix = {4: 1, 8: 3, 16: 7}[n]

        def begin(j, carry):
            k = lax.rem(j * mix, n)
            to = shifted(me, axes, k, 1)
            pltpu.make_async_remote_copy(
                src_ref=take(ins[src], to),
                dst_ref=put(outs[dst], me),
                send_sem=sems[3 * i].at[k],
                recv_sem=sems[3 * i + 1].at[k],
                device_id=address(to),
                device_id_type=MESH,
            ).start()
            return carry

        lax.fori_loop(1, n, begin, 0)
    for copy in own:
        copy.wait()
    for i, (src, dst, axes, take, put) in enumerate(channels):
        n = math.prod(SIZE[a] for a in axes)
        mix = {4: 1, 8: 3, 16: 7}[n]

        def finish(j, carry):
            k = lax.rem(j * mix, n)
            to, back = shifted(me, axes, k, 1), shifted(me, axes, k, -1)
            copy = pltpu.make_async_remote_copy(
                src_ref=take(ins[src], to),
                dst_ref=put(outs[dst], back),
                send_sem=sems[3 * i].at[k],
                recv_sem=sems[3 * i + 1].at[k],
                device_id=address(to),
                device_id_type=MESH,
            )
            copy.wait_send()
            copy.wait_recv()
            return carry

        lax.fori_loop(1, n, finish, 0)


def push(name, number, arrays, out_shapes, channels):
    scratch = []
    for _, _, axes, _, _ in channels:
        n = math.prod(SIZE[a] for a in axes)
        scratch += [
            pltpu.SemaphoreType.DMA((n,)),
            pltpu.SemaphoreType.DMA((n,)),
            pltpu.SemaphoreType.DMA,
        ]
    return pl.pallas_call(
        functools.partial(push_kernel, channels, len(arrays), len(out_shapes)),
        out_shape=tuple(jax.ShapeDtypeStruct(s, t) for s, t in out_shapes),
        in_specs=[pl.BlockSpec(memory_space=pl.ANY)] * len(arrays),
        out_specs=tuple([pl.BlockSpec(memory_space=pl.ANY)] * len(out_shapes)),
        scratch_shapes=scratch,
        compiler_params=pltpu.CompilerParams(collective_id=number, has_side_effects=True),
        name=name,
    )(*arrays)


def column_place(me, z, core):
    return dict(me, zh=lax.div(z, 2), zl=lax.rem(z, 2), co=core)


def greet_column(me, z, core):
    barrier = pltpu.get_barrier_semaphore()
    for off in (1, 2, 3):
        to = column_place(me, lax.rem(z + off, 4), core)
        pl.semaphore_signal(barrier, inc=1, device_id=address(to), device_id_type=MESH)
    sibling = column_place(me, z, 1 - core)
    pl.semaphore_signal(barrier, inc=1, device_id=address(sibling), device_id_type=MESH)
    pl.semaphore_wait(barrier, 4)


def gather_kernel(x_ref, out_ref, far_send, far_recv, near_send, near_recv, own_sem):
    me = where_am_i()
    z, core = me["zh"] * 2 + me["zl"], me["co"]
    sibling = address(column_place(me, z, 1 - core))
    own = pltpu.make_async_copy(x_ref, out_ref.at[z * 2 + core], own_sem)
    own.start()
    greet_column(me, z, core)

    def far(off):
        return pltpu.make_async_remote_copy(
            src_ref=x_ref,
            dst_ref=out_ref.at[z * 2 + core],
            send_sem=far_send.at[off],
            recv_sem=far_recv.at[off],
            device_id=address(column_place(me, lax.rem(z + off, 4), core)),
            device_id_type=MESH,
        )

    def near(off, core_of):
        slot = lax.rem(z + 4 - off, 4) * 2 + core_of
        return pltpu.make_async_remote_copy(
            src_ref=x_ref if off == 0 else out_ref.at[slot],
            dst_ref=out_ref.at[slot],
            send_sem=near_send.at[off],
            recv_sem=near_recv.at[off],
            device_id=sibling,
            device_id_type=MESH,
        )

    for off in (1, 3, 2):
        far(off).start()
    near(0, core).start()
    for off in (1, 3, 2):
        slot = lax.rem(z + 4 - off, 4) * 2 + core
        pltpu.make_async_remote_copy(
            src_ref=x_ref,
            dst_ref=out_ref.at[slot],
            send_sem=far_send.at[off],
            recv_sem=far_recv.at[off],
            device_id=address(column_place(me, lax.rem(z + off, 4), core)),
            device_id_type=MESH,
        ).wait_recv()
        near(off, core).start()
    own.wait()
    for off in (1, 3, 2):
        far(off).wait_send()
    for off in (0, 1, 3, 2):
        near(off, core).wait_send()
        near(off, 1 - core).wait_recv()


def gather_column(name, number, x):
    return pl.pallas_call(
        gather_kernel,
        out_shape=jax.ShapeDtypeStruct((RANKS,) + x.shape, x.dtype),
        in_specs=[pl.BlockSpec(memory_space=pl.ANY)],
        out_specs=pl.BlockSpec(memory_space=pl.ANY),
        scratch_shapes=[pltpu.SemaphoreType.DMA((4,))] * 4 + [pltpu.SemaphoreType.DMA],
        compiler_params=pltpu.CompilerParams(collective_id=number, has_side_effects=True),
        name=name,
    )(x)


def sum_kernel(
    part_ref, out_ref, paired, sending, landed, near_send, near_recv, far_send, far_recv
):
    me = where_am_i()
    z, core = me["zh"] * 2 + me["zl"], me["co"]
    sibling = address(column_place(me, z, 1 - core))
    greet_column(me, z, core)

    def near(off):
        to_z = lax.rem(z + off, 4)
        return pltpu.make_async_remote_copy(
            src_ref=part_ref.at[to_z * 2 + (1 - core)],
            dst_ref=paired.at[off],
            send_sem=near_send.at[off],
            recv_sem=near_recv.at[off],
            device_id=sibling,
            device_id_type=MESH,
        )

    def far(off):
        return pltpu.make_async_remote_copy(
            src_ref=sending.at[off],
            dst_ref=landed.at[off],
            send_sem=far_send.at[off],
            recv_sem=far_recv.at[off],
            device_id=address(column_place(me, lax.rem(z + off, 4), core)),
            device_id_type=MESH,
        )

    for off in (2, 1, 3, 0):
        near(off).start()
    for off in (2, 1, 3):
        near(off).wait_recv()
        mine = part_ref[lax.rem(z + off, 4) * 2 + core].astype(F32)
        sending[off] = (mine + paired[off].astype(F32)).astype(BF16)
        far(off).start()
    near(0).wait_recv()
    out_ref[...] = part_ref[z * 2 + core].astype(F32) + paired[0].astype(F32)
    for off in (1, 3, 2):
        far(off).wait_recv()
        out_ref[...] += landed[off].astype(F32)
    for off in (2, 1, 3):
        near(off).wait_send()
        far(off).wait_send()
    near(0).wait_send()


def sum_column(name, number, parts):
    block = parts.shape[1:]
    return pl.pallas_call(
        sum_kernel,
        out_shape=jax.ShapeDtypeStruct(block, F32),
        in_specs=[pl.BlockSpec(memory_space=pltpu.VMEM)],
        out_specs=pl.BlockSpec(memory_space=pltpu.VMEM),
        scratch_shapes=[pltpu.VMEM((4,) + block, BF16)] * 3
        + [pltpu.SemaphoreType.DMA((4,))] * 4,
        compiler_params=pltpu.CompilerParams(
            collective_id=number, has_side_effects=True, vmem_limit_bytes=VMEM_LIMIT
        ),
        name=name,
    )(parts)


def dot_nn(a, b):
    return lax.dot_general(a, b, (((1,), (0,)), ((), ())), preferred_element_type=F32)


def dot_nt(a, b):
    return lax.dot_general(a, b, (((1,), (1,)), ((), ())), preferred_element_type=F32)


def dot_tn(a, b):
    return lax.dot_general(a, b, (((0,), (0,)), ((), ())), preferred_element_type=F32)


def stacked_heads(ref, tile):
    rows = ref[pl.ds(tile * BLOCK, BLOCK), :]
    return jnp.concatenate([rows[:, :HD], rows[:, HD:]], axis=0)


def allowed_keys(block, chunk):
    keys = chunk * CHUNK + lax.broadcasted_iota(jnp.int32, (CHUNK, 2 * BLOCK), 0)
    lanes = lax.broadcasted_iota(jnp.int32, (CHUNK, 2 * BLOCK), 1)
    return keys <= block * BLOCK + lax.rem(lanes, BLOCK)


def first_chunk(block):
    return jnp.where(block >= LONG // BLOCK, LONG // CHUNK, 0)


def attend_kernel(q_blocks, k_blocks, q_ref, kv_ref, out_ref, lse_ref, keys, values, values_t):
    def sort(i, carry):
        to = pl.multiple_of(k_blocks[i] * BLOCK, BLOCK)
        here = pl.multiple_of(i * BLOCK, BLOCK)
        keys[pl.ds(to, BLOCK), :] = kv_ref[pl.ds(here, BLOCK), :HD]
        values[pl.ds(to, BLOCK), :] = kv_ref[pl.ds(here, BLOCK), HD:]
        return carry

    lax.fori_loop(0, PACK_TOK // BLOCK, sort, 0)
    for c in range(PACK_TOK // CHUNK):
        part = values[c * CHUNK : (c + 1) * CHUNK, :].astype(F32)
        values_t[c] = part.T.astype(BF16)

    def one_tile(tile, carry):
        block = q_blocks[tile]
        query = stacked_heads(q_ref, tile)
        last = lax.div(block, CHUNK // BLOCK)

        def one_chunk(c, state, masked):
            total, mixed = state
            chunk_keys = keys[pl.ds(pl.multiple_of(c * CHUNK, CHUNK), CHUNK), :]
            weights = jnp.exp2(dot_nt(chunk_keys, query) * (SCALE * LOG2E))
            if masked:
                weights = jnp.where(allowed_keys(block, c), weights, 0.0)
            total = total + jnp.sum(weights, axis=0, keepdims=True)
            mixed = mixed + dot_nn(values_t[c], weights.astype(BF16))
            return total, mixed

        state = (jnp.zeros((1, 2 * BLOCK), F32), jnp.zeros((HD, 2 * BLOCK), F32))
        state = lax.fori_loop(
            first_chunk(block), last, lambda c, s: one_chunk(c, s, False), state
        )
        total, mixed = one_chunk(last, state, True)
        result = (mixed / total).T.astype(BF16)
        rows = pl.ds(pl.multiple_of(tile * BLOCK, BLOCK), BLOCK)
        out_ref[rows, :HD] = result[:BLOCK]
        out_ref[rows, HD:] = result[BLOCK:]
        lse_ref[pl.ds(tile, 1), :] = jnp.log2(total)
        return carry

    lax.fori_loop(0, q_ref.shape[0] // BLOCK, one_tile, 0)


def attend(q_blocks, k_blocks, q, kv):
    smem = pl.BlockSpec(memory_space=pltpu.SMEM)
    vmem = pl.BlockSpec(memory_space=pltpu.VMEM)
    tiles = q.shape[0] // BLOCK
    return pl.pallas_call(
        attend_kernel,
        out_shape=(
            jax.ShapeDtypeStruct(q.shape, BF16),
            jax.ShapeDtypeStruct((tiles, 2 * BLOCK), F32),
        ),
        in_specs=[smem, smem, vmem, vmem],
        out_specs=(vmem, vmem),
        scratch_shapes=[
            pltpu.VMEM((PACK_TOK, HD), BF16),
            pltpu.VMEM((PACK_TOK, HD), BF16),
            pltpu.VMEM((PACK_TOK // CHUNK, HD, CHUNK), BF16),
        ],
        compiler_params=pltpu.CompilerParams(vmem_limit_bytes=VMEM_LIMIT),
        cost_estimate=pl.CostEstimate(
            flops=4 * 10**9, bytes_accessed=4 * 10**6, transcendentals=8 * 10**6
        ),
        name="attend",
    )(q_blocks, k_blocks, q, kv)


def attend_back_kernel(
    q_blocks,
    k_blocks,
    q_ref,
    kv_ref,
    grad_ref,
    out_ref,
    lse_ref,
    dq_ref,
    dkv_ref,
    keys,
    values,
    keys_t,
    dk,
    dv,
):
    def sort(i, carry):
        to = pl.multiple_of(k_blocks[i] * BLOCK, BLOCK)
        here = pl.multiple_of(i * BLOCK, BLOCK)
        keys[pl.ds(to, BLOCK), :] = kv_ref[pl.ds(here, BLOCK), :HD]
        values[pl.ds(to, BLOCK), :] = kv_ref[pl.ds(here, BLOCK), HD:]
        return carry

    lax.fori_loop(0, PACK_TOK // BLOCK, sort, 0)
    for c in range(PACK_TOK // CHUNK):
        part = keys[c * CHUNK : (c + 1) * CHUNK, :].astype(F32)
        keys_t[c] = part.T.astype(BF16)
    dk[...] = jnp.zeros_like(dk)
    dv[...] = jnp.zeros_like(dv)

    def one_tile(tile, carry):
        block = q_blocks[tile]
        query = stacked_heads(q_ref, tile)
        grad = stacked_heads(grad_ref, tile)
        out = stacked_heads(out_ref, tile)
        inner = jnp.sum((grad.astype(F32) * out.astype(F32)).T, axis=0, keepdims=True)
        lse = lse_ref[pl.ds(tile, 1), :]
        last = lax.div(block, CHUNK // BLOCK)

        def one_chunk(c, dq, masked):
            rows = pl.ds(pl.multiple_of(c * CHUNK, CHUNK), CHUNK)
            probs = jnp.exp2(dot_nt(keys[rows, :], query) * (SCALE * LOG2E) - lse)
            if masked:
                probs = jnp.where(allowed_keys(block, c), probs, 0.0)
            grad_probs = dot_nt(values[rows, :], grad)
            grad_scores = (probs * (grad_probs - inner)).astype(BF16)
            dv[rows, :] += dot_nn(probs.astype(BF16), grad)
            dk[rows, :] += dot_nn(grad_scores, query)
            return dq + dot_nn(keys_t[c], grad_scores)

        dq = lax.fori_loop(
            first_chunk(block),
            last,
            lambda c, s: one_chunk(c, s, False),
            jnp.zeros((HD, 2 * BLOCK), F32),
        )
        dq = (one_chunk(last, dq, True) * SCALE).T.astype(BF16)
        rows = pl.ds(pl.multiple_of(tile * BLOCK, BLOCK), BLOCK)
        dq_ref[rows, :HD] = dq[:BLOCK]
        dq_ref[rows, HD:] = dq[BLOCK:]
        return carry

    lax.fori_loop(0, q_ref.shape[0] // BLOCK, one_tile, 0)

    def unsort(i, carry):
        at = pl.multiple_of(k_blocks[i] * BLOCK, BLOCK)
        here = pl.multiple_of(i * BLOCK, BLOCK)
        dkv_ref[pl.ds(here, BLOCK), :HD] = (dk[pl.ds(at, BLOCK), :] * SCALE).astype(BF16)
        dkv_ref[pl.ds(here, BLOCK), HD:] = dv[pl.ds(at, BLOCK), :].astype(BF16)
        return carry

    lax.fori_loop(0, PACK_TOK // BLOCK, unsort, 0)


def attend_back(q_blocks, k_blocks, q, kv, grad, out, lse):
    smem = pl.BlockSpec(memory_space=pltpu.SMEM)
    vmem = pl.BlockSpec(memory_space=pltpu.VMEM)
    return pl.pallas_call(
        attend_back_kernel,
        out_shape=(
            jax.ShapeDtypeStruct(q.shape, BF16),
            jax.ShapeDtypeStruct(kv.shape, BF16),
        ),
        in_specs=[smem, smem] + [vmem] * 5,
        out_specs=(vmem, vmem),
        scratch_shapes=[
            pltpu.VMEM((PACK_TOK, HD), BF16),
            pltpu.VMEM((PACK_TOK, HD), BF16),
            pltpu.VMEM((PACK_TOK // CHUNK, HD, CHUNK), BF16),
            pltpu.VMEM((PACK_TOK, HD), F32),
            pltpu.VMEM((PACK_TOK, HD), F32),
        ],
        compiler_params=pltpu.CompilerParams(vmem_limit_bytes=VMEM_LIMIT),
        cost_estimate=pl.CostEstimate(
            flops=10**10, bytes_accessed=8 * 10**6, transcendentals=8 * 10**6
        ),
        name="attend_back",
    )(q_blocks, k_blocks, q, kv, grad, out, lse)


def rms_norm(values, norm_gain):
    factor = lax.rsqrt(jnp.mean(values * values, axis=-1, keepdims=True) + NORM_EPS)
    return values * factor * norm_gain


def head_prepare(projected, norm_gain, cosine, sine_part):
    normed = rms_norm(projected, norm_gain)
    halfway = HD // 2
    leading, trailing = normed[..., :halfway], normed[..., halfway:]
    return jnp.concatenate(
        [leading * cosine - trailing * sine_part, trailing * cosine + leading * sine_part], axis=-1
    )


def swiglu(gate_up):
    half = gate_up.shape[-1] // 2
    return jax.nn.silu(gate_up[:, :half]) * gate_up[:, half:]


def adam_update(weight, gradient, mean_old, square_old, rate, decay):
    mean_new = BETA_ONE * mean_old + (1.0 - BETA_ONE) * gradient
    square_new = BETA_TWO * square_old + (1.0 - BETA_TWO) * gradient * gradient
    mean_hat = mean_new / (1.0 - BETA_ONE**STEP)
    square_hat = square_new / (1.0 - BETA_TWO**STEP)
    weight_new = weight - rate * (mean_hat / (jnp.sqrt(square_hat) + ADAM_EPS) + decay * weight)
    return (weight_new, mean_new, square_new)


def by_rank(array, width):
    return array.reshape(array.shape[0], RANKS, width)


def swap_owner(array):
    pairs = [(a * 4 + b, b * 4 + a) for a in range(4) for b in range(4)]
    return lax.ppermute(array, ("x", "zl", "co"), pairs)


def body(
    tokens,
    cotangent,
    positions,
    seq_ids,
    query_weight,
    keyval_weight,
    output_weight,
    gateup_weight,
    down_weight,
    norm_gains,
    query_mean,
    keyval_mean,
    output_mean,
    gateup_mean,
    down_mean,
    gains_mean,
    query_square,
    keyval_square,
    output_square,
    gateup_square,
    down_square,
    gains_square,
):
    inputs = tokens[0]
    upstream = cotangent[0].astype(F32)
    at_x, at_y = lax.axis_index("x"), lax.axis_index("y")

    own_blocks = (positions[0] + LONG * seq_ids[0]).reshape(-1, BLOCK)[:, 0] // BLOCK
    extra = jnp.zeros((8, HD), F32)
    extra = extra.at[0, : norm_gains.shape[0]].set(norm_gains)
    extra = extra.at[1, :BLOCK].set(own_blocks.astype(F32))
    sent = jnp.concatenate(
        [
            by_rank(query_weight, 256),
            by_rank(keyval_weight[:, :KV], 128),
            by_rank(keyval_weight[:, KV:], 128),
            jnp.broadcast_to(extra[:, None, :], (8, RANKS, HD)),
            by_rank(gateup_weight[:, :FF], 384),
            by_rank(gateup_weight[:, FF:], 384),
        ],
        axis=2,
    ).transpose(1, 0, 2)
    (shares,) = push(
        "weights_column",
        1,
        [sent],
        [(sent.shape, F32)],
        [
            (
                0,
                0,
                COLUMN,
                lambda ref, to: ref.at[flat_index(to, COLUMN)],
                lambda ref, frm: ref.at[flat_index(frm, COLUMN)],
            )
        ],
    )
    shares_low = shares.astype(BF16).reshape(2, 32, 1408)
    all_tokens = gather_column("tokens_column", 2, inputs).reshape(RANKS * ROWS, D)
    (qkv_wide,) = push(
        "weights_plane",
        3,
        [shares_low[..., :640]],
        [((2, PLANE, 32, 640), BF16)],
        [
            (
                0,
                0,
                SURFACE,
                lambda ref, to: ref,
                lambda ref, frm: ref.at[:, flat_index(frm, SURFACE)],
            )
        ],
    )
    row_shares = swap_owner(
        jnp.concatenate(
            [output_weight.astype(BF16), down_weight.astype(BF16).reshape(16, 1536)], axis=1
        )
    )
    row_wide = lax.all_gather(row_shares, ("y", "x"))
    output_part = row_wide[:, :, :D].reshape(256, D)
    down_part = row_wide[:, :, D:].reshape(384, D)
    gateup_part = lax.all_gather(shares_low[..., 640:], SURFACE, axis=1).reshape(D, 768)

    qkv_part = qkv_wide[..., :512].reshape(D, 512)
    gains_all = (
        qkv_wide[..., 512:].reshape(2, PLANE, 4, 8, HD)[:, :, :, 0, :18].reshape(-1).astype(F32)
    )
    attn_gain = gains_all[:D]
    ffn_gain = gains_all[D : 2 * D]
    query_gain = gains_all[2 * D : 2 * D + HD]
    key_gain = gains_all[2 * D + HD :]

    blocks = shares[:4, 1, 512 : 512 + BLOCK].astype(jnp.int32).reshape(4, 2, 4, 4, 2)
    pack_blocks = lax.dynamic_index_in_dim(blocks, at_x, 0, keepdims=False)
    key_blocks = pack_blocks.transpose(1, 2, 0, 3).reshape(-1)
    query_blocks = (
        lax.dynamic_index_in_dim(pack_blocks, at_y, 2, keepdims=False).transpose(1, 0, 2).reshape(-1)
    )
    row_blocks = lax.dynamic_index_in_dim(
        lax.dynamic_index_in_dim(blocks, at_x, 2, keepdims=False), at_y, 2, keepdims=False
    ).transpose(1, 0, 2)
    slots = row_blocks[..., None] * BLOCK + jnp.arange(BLOCK, dtype=jnp.int32)
    places = jnp.where(slots >= LONG, slots - LONG, slots).reshape(-1)
    halfway = HD // 2
    frequency = ROPE_BASE ** (-jnp.arange(halfway, dtype=F32) * 2.0 / HD)
    angles = places.astype(F32)[:, None] * frequency[None, :]
    cosine = jnp.cos(angles)[:, None, :]
    sine_part = jnp.sin(angles)[:, None, :]

    qkv_proj = dot_nn(all_tokens, qkv_part)
    head_gains = jnp.stack([query_gain, query_gain, key_gain])
    heads_in = qkv_proj[:, :384].reshape(-1, 3, HD)
    prepare = functools.partial(head_prepare, cosine=cosine, sine_part=sine_part)
    heads_use, heads_pull = jax.vjp(prepare, heads_in, head_gains)
    qkv = jnp.concatenate(
        [heads_use.reshape(-1, 384).astype(BF16), qkv_proj[:, 384:].astype(BF16)], axis=1
    ).reshape(2, 4, ROWS, 512)

    def to_pack_x(ref, to):
        return ref.at[:, to["x"]]

    def from_x(ref, frm):
        return ref.at[frm["x"]]

    q_mine, kv_mine = push(
        "attention_in",
        4,
        [qkv[..., :256], qkv[..., 256:]],
        [((4, 2, ROWS, 256), BF16), ((PLANE, 2, ROWS, 256), BF16)],
        [
            (1, 1, SURFACE, to_pack_x, lambda ref, frm: ref.at[flat_index(frm, SURFACE)]),
            (0, 0, ("x",), to_pack_x, from_x),
        ],
    )
    q_mine = q_mine.reshape(1024, 256)
    kv_mine = kv_mine.reshape(PACK_TOK, 256)
    out_mine, lse = attend(query_blocks, key_blocks, q_mine, kv_mine)

    def to_x(ref, to):
        return ref.at[to["x"]]

    def from_pack_x(ref, frm):
        return ref.at[:, frm["x"]]

    (attended,) = push(
        "attention_out",
        5,
        [out_mine.reshape(4, 2, ROWS, 256)],
        [((2, 4, ROWS, 256), BF16)],
        [(0, 0, ("x",), to_x, from_pack_x)],
    )
    attended = attended.reshape(RANKS * ROWS, 256)

    branch = sum_column(
        "branch_column", 6, dot_nn(attended, output_part).astype(BF16).reshape(RANKS, ROWS, D)
    )
    hidden = inputs.astype(F32) + rms_norm(branch, attn_gain)

    all_hidden = gather_column("hidden_column", 7, hidden.astype(BF16)).reshape(RANKS * ROWS, D)
    gate_up = dot_nn(all_hidden, gateup_part)
    activated = swiglu(gate_up).astype(BF16)
    ffn_out = sum_column(
        "ffn_column", 8, dot_nn(activated, down_part).astype(BF16).reshape(RANKS, ROWS, D)
    )
    ffn_norm_out, ffn_pull = jax.vjp(rms_norm, ffn_out, ffn_gain)
    result = hidden + ffn_norm_out
    grad_ffn_out, grad_ffn_gain = ffn_pull(upstream)

    grad_ffn = gather_column("grad_ffn_column", 9, grad_ffn_out.astype(BF16)).reshape(
        RANKS * ROWS, D
    )
    down_grad = dot_tn(activated, grad_ffn)
    grad_act = dot_nt(grad_ffn, down_part)
    act_out, act_pull = jax.vjp(swiglu, gate_up)
    grad_gate_low = act_pull(grad_act)[0].astype(BF16)
    gateup_grad = dot_tn(all_hidden, grad_gate_low)
    grad_hidden = upstream + sum_column(
        "grad_hidden_column",
        10,
        dot_nt(grad_gate_low, gateup_part).astype(BF16).reshape(RANKS, ROWS, D),
    )
    attn_norm_out, attn_pull = jax.vjp(rms_norm, branch, attn_gain)
    grad_branch_own, grad_attn_gain = attn_pull(grad_hidden)
    grad_branch = gather_column("grad_branch_column", 11, grad_branch_own.astype(BF16)).reshape(
        RANKS * ROWS, D
    )
    output_grad = dot_tn(attended, grad_branch)
    grad_attended = dot_nt(grad_branch, output_part).astype(BF16)

    (grad_mine,) = push(
        "attention_grad_in",
        12,
        [grad_attended.reshape(2, 4, ROWS, 256)],
        [((4, 2, ROWS, 256), BF16)],
        [(0, 0, ("x",), to_pack_x, from_x)],
    )
    dq_mine, dkv_mine = attend_back(
        query_blocks, key_blocks, q_mine, kv_mine, grad_mine.reshape(1024, 256), out_mine, lse
    )
    dq, dkv_parts = push(
        "attention_grad_out",
        13,
        [dq_mine.reshape(4, 2, ROWS, 256), dkv_mine.reshape(PLANE, 2, ROWS, 256)],
        [((2, 4, ROWS, 256), BF16), ((4, 2, 4, ROWS, 256), BF16)],
        [
            (
                1,
                1,
                SURFACE,
                lambda ref, to: ref.at[flat_index(to, SURFACE)],
                lambda ref, frm: ref.at[frm["y"], :, frm["x"]],
            ),
            (0, 0, ("x",), to_x, from_pack_x),
        ],
    )
    dkv = jnp.sum(dkv_parts.astype(F32), axis=0).reshape(RANKS * ROWS, 256)
    grad_heads = jnp.concatenate([dq.reshape(RANKS * ROWS, 256).astype(F32), dkv[:, :HD]], axis=1)
    grad_heads_in, grad_head_gains = heads_pull(grad_heads.reshape(-1, 3, HD))
    grad_qkv = jnp.concatenate(
        [grad_heads_in.reshape(-1, 384).astype(BF16), dkv[:, HD:].astype(BF16)], axis=1
    )
    qkv_grad = dot_tn(all_tokens, grad_qkv)
    token_grad = grad_hidden + sum_column(
        "grad_token_column",
        14,
        dot_nt(grad_qkv, qkv_part).astype(BF16).reshape(RANKS, ROWS, D),
    )

    gains_grad = jnp.concatenate(
        [
            grad_attn_gain,
            grad_ffn_gain,
            grad_head_gains[0] + grad_head_gains[1],
            grad_head_gains[2],
        ]
    )
    gains_lines = jnp.pad(
        gains_grad.reshape(2, PLANE, 4, 18).transpose(1, 0, 2, 3).reshape(PLANE, RANKS, 18),
        ((0, 0), (0, 0), (0, HD - 18)),
    )

    def to_surface_inner(ref, to):
        return ref.at[:, flat_index(to, SURFACE)]

    def to_surface(ref, to):
        return ref.at[flat_index(to, SURFACE)]

    def to_surface_swapped(ref, to):
        return ref.at[flat_index(to, ("y", "x"))]

    gateup_lines = gateup_grad.astype(BF16).reshape(2, PLANE, 32, 768)
    qkv_lines = qkv_grad.astype(BF16).reshape(2, PLANE, 32, 512)
    row_lines = jnp.concatenate(
        [
            output_grad.astype(BF16).reshape(PLANE, 16, D),
            down_grad.astype(BF16).reshape(PLANE, 16, 1536),
        ],
        axis=2,
    )
    gateup_parts, row_parts, qkv_parts, gains_parts = push(
        "grads_plane",
        15,
        [gateup_lines, row_lines, qkv_lines, gains_lines],
        [
            ((PLANE, 2, 32, 768), BF16),
            ((PLANE, 16, D + 1536), BF16),
            ((PLANE, 2, 32, 512), BF16),
            ((PLANE, RANKS, HD), F32),
        ],
        [
            (0, 0, SURFACE, to_surface_inner, to_surface),
            (1, 1, SURFACE, to_surface_swapped, to_surface),
            (2, 2, SURFACE, to_surface_inner, to_surface),
            (3, 3, SURFACE, to_surface, to_surface),
        ],
    )
    row_sum = swap_owner(jnp.sum(row_parts.astype(F32), axis=0))
    output_sum = row_sum[:, :D]
    down_sum = row_sum[:, D:].reshape(24, D)
    gains_sums = jnp.sum(gains_parts, axis=0).reshape(RANKS, 1, HD)
    column_sums = jnp.concatenate(
        [
            jnp.sum(qkv_parts.astype(F32), axis=0).reshape(RANKS, 8, 512),
            jnp.pad(gains_sums, ((0, 0), (0, 7), (0, 0))),
            jnp.sum(gateup_parts.astype(F32), axis=0).reshape(RANKS, 8, 768),
        ],
        axis=2,
    )
    (summed,) = push(
        "grads_column",
        16,
        [column_sums],
        [((RANKS, 8, 1408), F32)],
        [
            (
                0,
                0,
                COLUMN,
                lambda ref, to: ref.at[flat_index(to, COLUMN)],
                lambda ref, frm: ref.at[flat_index(frm, COLUMN)],
            )
        ],
    )
    gains_sum = jnp.sum(summed[:, 0, 512 : 512 + 18], axis=0)
    wide = summed.transpose(1, 0, 2)
    query_sum = wide[:, :, :256].reshape(8, 2048)
    keyval_sum = jnp.concatenate(
        [wide[:, :, 256:384].reshape(8, KV), wide[:, :, 384:512].reshape(8, KV)], axis=1
    )
    gateup_sum = jnp.concatenate(
        [wide[:, :, 640:1024].reshape(8, FF), wide[:, :, 1024:].reshape(8, FF)], axis=1
    )

    query_new, query_mean_new, query_square_new = adam_update(
        query_weight, query_sum, query_mean, query_square, RATE_MATRIX, DECAY
    )
    keyval_new, keyval_mean_new, keyval_square_new = adam_update(
        keyval_weight, keyval_sum, keyval_mean, keyval_square, RATE_MATRIX, DECAY
    )
    output_new, output_mean_new, output_square_new = adam_update(
        output_weight, output_sum, output_mean, output_square, RATE_MATRIX, DECAY
    )
    gateup_new, gateup_mean_new, gateup_square_new = adam_update(
        gateup_weight, gateup_sum, gateup_mean, gateup_square, RATE_MATRIX, DECAY
    )
    down_new, down_mean_new, down_square_new = adam_update(
        down_weight, down_sum, down_mean, down_square, RATE_MATRIX, DECAY
    )
    gains_new, gains_mean_new, gains_square_new = adam_update(
        norm_gains, gains_sum, gains_mean, gains_square, RATE_GAIN, 0.0
    )
    return (
        result.astype(BF16)[None],
        token_grad[None],
        query_sum,
        keyval_sum,
        output_sum,
        gateup_sum,
        down_sum,
        gains_sum,
        query_new,
        keyval_new,
        output_new,
        gateup_new,
        down_new,
        gains_new,
        query_mean_new,
        keyval_mean_new,
        output_mean_new,
        gateup_mean_new,
        down_mean_new,
        gains_mean_new,
        query_square_new,
        keyval_square_new,
        output_square_new,
        gateup_square_new,
        down_square_new,
        gains_square_new,
    )


def solution(mesh):
    fine = Mesh(mesh.devices.reshape([SIZE[a] for a in AXES]), AXES)
    rows = P(("zl", "co"), ("zh", "x", "y"), None)
    packs = P(("zl", "co"), None)
    matrix = P(AXES, None)
    vector = P(AXES)
    params = [matrix] * 5 + [vector]
    return jax.shard_map(
        body,
        mesh=fine,
        in_specs=(rows, rows, packs, packs, *params, *params, *params),
        out_specs=(rows, rows, *params, *params, *params, *params),
        check_vma=False,
    )
```

time: 2380 us -> 516 us (0.22)
  waiting for transfers between devices: 1690 us -> 3.82 us
  Pallas kernels: 0 us -> 385 us
  local copies, waits for them, and re-layouts: 274 us -> 40.6 us
  matrix products: 192 us -> 29.9 us
  other arithmetic: 118 us -> 28.1 us
  blocking collectives: 68.9 us -> 0 us
    reduce_scatter x2 -> x0, waiting for transfers between devices: 827 us -> none  [the longest x1 612 us: sum_together(): lax.psum_scatter(lines, axis, tiled=True).reshape(-1)]
    all_gather x4 -> x2, waiting for transfers between devices: 629 us -> 0.04 us  [the longest x1 0.02 us: body(): row_wide = lax.all_gather(row_shares, ('y', 'x'))]
    pallas_call x0 -> x18, Pallas kernels: none -> 385 us  [the longest x8 189 us: push(): pl.pallas_call(functools.partial(push_kernel, channels, len(arrays), len(...]
    unnamed x8 -> x2, waiting for transfers between devices: 235 us -> 0.03 us
    dot_general x71 -> x12, matrix products: 192 us -> 29.9 us  [the longest x4 10.6 us: dot_nt(): lax.dot_general(a, b, (((1,), (1,)), ((), ())), preferred_element_type=F32)]
    another operation x10 -> x1, local copies, waits for them, and re-layouts: 107 us -> 0.01 us  [body(): head_gains = jnp.stack([query_gain, query_gain, key_gain])]
    unnamed x1 -> x0, blocking collectives: 68.9 us -> none
    concatenate x9 -> x7, other arithmetic: 68.9 us -> 4.26 us  [the longest x1 1.2 us: body(): jnp.concatenate([dq.reshape(RANKS * ROWS, 256).astype(F32), dkv[:, :HD]],...]
  transfers between devices with their start and end apart: 7 -> 4, of which waited for: 7 -> 2; matrix products, arithmetic and copies ran while one was open for 16% -> 6% of each run, Pallas kernels for 0% -> 32%
where the time goes in v1:
time: 516 us; the launch traced here: 510 us
  Pallas kernels  385 us (75%)
  local copies, waits for them, and re-layouts  40.6 us (8%)
  matrix products  29.9 us (6%)
  other arithmetic  28.1 us (5%)
  between operations  15.1 us (3%)
  starting transfers between devices  7.34 us (1%)
    pallas_call x8, Pallas kernels, push(): pl.pallas_call(functools.partial(push_kernel, channels, len(arrays), len(...  189 us
    pallas_call x4, Pallas kernels, gather_column(): pl.pallas_call(gather_kernel, out_shape=jax.ShapeDtypeStruct((RANKS,) + x...  71.5 us
    pallas_call x4, Pallas kernels, sum_column(): pl.pallas_call(sum_kernel, out_shape=jax.ShapeDtypeStruct(block, F32), in...  71 us
    pallas_call x1, Pallas kernels, attend_back(): pl.pallas_call(attend_back_kernel, out_shape=(jax.ShapeDtypeStruct(q.shap...  30.1 us
    pallas_call x1, Pallas kernels, attend(): pl.pallas_call(attend_kernel, out_shape=(jax.ShapeDtypeStruct(q.shape, BF...  23.2 us
    unnamed x121, local copies, waits for them, and re-layouts  16.4 us
    dot_general x4, matrix products, dot_nt(): lax.dot_general(a, b, (((1,), (1,)), ((), ())), preferred_element_type=F32)  10.6 us
  transfers between devices with their start and end apart: 4, of which 2 were waited for; matrix products, arithmetic and copies ran while one was open for 6% of the time, Pallas kernels for 32%

profile of v1, /device:TPU:1, one launch (start us, length us, event | category | flops | bytes accessed | tf_op | source)
XLA Modules:
  0.0 509.7 jit_solution(11712673362681826973)
XLA Ops:
  9.1 4.5 collective-permute-start
  22.3 13.8 %weights_column.1 = f32[8,8,1408]{2,1,0:T(8,128)} custom-call(f32[8,8,1408]{2,1,0:T(8,128)} %bitcast.186), custom_call_target="tpu_custom_call" | custom-call | tf_op jit(solution)/shard_map/weights_column/pallas_call | solution.py:146
  39.5 23.7 %weights_plane.1 = bf16[2,16,32,640]{3,2,1,0:T(8,128)(2,1)} custom-call(bf16[2,32,640]{2,1,0:T(8,128)(2,1)} %slice.194.refs_0_), custom_call_target="tpu_custom_call" | custom-call | tf_op jit(solution)/shard_map/weights_plane/pallas_call | solution.py:146
  65.5 18.5 %tokens_column.1 = bf16[8,128,1024]{2,1,0:T(8,128)(2,1)} custom-call(bf16[128,1024]{1,0:T(8,128)(2,1)} %bitcast.162), custom_call_target="tpu_custom_call" | custom-call | tf_op jit(solution)/shard_map/tokens_column/pallas_call | solution.py:223
  84.0 2.9 convolution_bitcast_fusion
  94.3 40.6 %attention_in.1 = (bf16[4,2,128,256]{3,2,1,0:T(8,128)(2,1)}, bf16[16,2,128,256]{3,2,1,0:T(8,128)(2,1)}) custom-call(bf16[2,4,128,256]{3,2,1,0:T(8,128)(2,1)} %get-tuple-element.108.refs_0_, bf16[2,4,128,256]{3,2,1,0:T(8,128)(2,1)} %get-tuple-element.107.refs_1_), custom_call_target="tpu_custom_call" | custom-call | tf_op jit(solution)/shard_map/attention_in/pallas_call | solution.py:146
  137.5 23.2 %attend.1 = (bf16[1024,256]{1,0:T(8,128)(2,1)S(1)}, f32[16,128]{1,0:T(8,128)S(1)}) custom-call(s32[16]{0:T(128)S(1)} %reshape.481.q_blocks, s32[64]{0:T(128)S(1)} %reshape.482.k_blocks, bf16[1024,256]{1,0:T(8,128)(2,1)S(1)} %bitcast.144, bf16[4096,256]{1,0:T(8,128)(2,1)S(1)} %bitcast.143), custom_call_target="tpu_custom_call" | custom-call | flops 4000000000 | bytes 4000000 | tf_op jit(solution)/shard_map/attend/pallas_call | solution.py:371
  161.5 8.5 %attention_out.1 = bf16[2,4,128,256]{3,2,1,0:T(8,128)(2,1)} custom-call(bf16[4,2,128,256]{3,2,1,0:T(8,128)(2,1)} %bitcast.140), custom_call_target="tpu_custom_call" | custom-call | tf_op jit(solution)/shard_map/attention_out/pallas_call | solution.py:146
  176.3 19.0 %branch_column.1 = f32[128,1024]{1,0:T(8,128)S(1)} custom-call(bf16[8,128,1024]{2,1,0:T(8,128)(2,1)S(1)} %bitcast.135), custom_call_target="tpu_custom_call" | custom-call | tf_op jit(solution)/shard_map/branch_column/pallas_call | solution.py:283
  196.3 17.7 %hidden_column.1 = bf16[8,128,1024]{2,1,0:T(8,128)(2,1)} custom-call(bf16[128,1024]{1,0:T(8,128)(2,1)} %fusion.13.x_ref), custom_call_target="tpu_custom_call" | custom-call | tf_op jit(solution)/shard_map/hidden_column/pallas_call | solution.py:223
  214.0 3.8 fusion.42
  220.8 17.3 %ffn_column.1 = f32[128,1024]{1,0:T(8,128)S(1)} custom-call(bf16[8,128,1024]{2,1,0:T(8,128)(2,1)S(1)} %bitcast.138), custom_call_target="tpu_custom_call" | custom-call | tf_op jit(solution)/shard_map/ffn_column/pallas_call | solution.py:283
  239.4 17.7 %grad_ffn_column.1 = bf16[8,128,1024]{2,1,0:T(8,128)(2,1)} custom-call(bf16[128,1024]{1,0:T(8,128)(2,1)} %fusion.8.x_ref), custom_call_target="tpu_custom_call" | custom-call | tf_op jit(solution)/shard_map/grad_ffn_column/pallas_call | solution.py:223
  257.1 4.6 fusion.16
  263.6 3.2 convolution_convert_fusion.4
  268.6 17.4 %grad_hidden_column.1 = f32[128,1024]{1,0:T(8,128)S(1)} custom-call(bf16[8,128,1024]{2,1,0:T(8,128)(2,1)S(1)} %bitcast.137), custom_call_target="tpu_custom_call" | custom-call | tf_op jit(solution)/shard_map/grad_hidden_column/pallas_call | solution.py:283
  287.3 17.7 %grad_branch_column.1 = bf16[8,128,1024]{2,1,0:T(8,128)(2,1)} custom-call(bf16[128,1024]{1,0:T(8,128)(2,1)} %get-tuple-element.109.x_ref), custom_call_target="tpu_custom_call" | custom-call | tf_op jit(solution)/shard_map/grad_branch_column/pallas_call | solution.py:223
  305.0 3.3 convolution_convert_fusion.7
  309.8 9.7 %attention_grad_in.1 = bf16[4,2,128,256]{3,2,1,0:T(8,128)(2,1)} custom-call(bf16[2,4,128,256]{3,2,1,0:T(8,128)(2,1)} %bitcast.184), custom_call_target="tpu_custom_call" | custom-call | tf_op jit(solution)/shard_map/attention_grad_in/pallas_call | solution.py:146
  320.6 30.1 %attend_back.1 = (bf16[1024,256]{1,0:T(8,128)(2,1)S(1)}, bf16[4096,256]{1,0:T(8,128)(2,1)}) custom-call(s32[16]{0:T(128)S(1)} %reshape.481.q_blocks, s32[64]{0:T(128)S(1)} %reshape.482.k_blocks, bf16[1024,256]{1,0:T(8,128)(2,1)S(1)} %bitcast.145, bf16[4096,256]{1,0:T(8,128)(2,1)} %bitcast.142, bf16[1024,256]{1,0:T(8,128)(2,1)S(1)} %bitcast.141, ...), custom_call_target="tpu_custom_call" | custom-call | flops 10000000000 | bytes 8000000 | tf_op jit(solution)/shard_map/attend_back/pallas_call | solution.py:469
  351.4 32.7 %attention_grad_out.1 = (bf16[2,4,128,256]{3,2,1,0:T(8,128)(2,1)}, bf16[4,2,4,128,256]{4,3,2,1,0:T(8,128)(2,1)}) custom-call(bf16[4,2,128,256]{3,2,1,0:T(8,128)(2,1)} %bitcast.139, bf16[16,2,128,256]{3,2,1,0:T(8,128)(2,1)} %bitcast.163), custom_call_target="tpu_custom_call" | custom-call | tf_op jit(solution)/shard_map/attention_grad_out/pallas_call | solution.py:146
  405.6 49.1 %grads_plane.1 = (bf16[16,2,32,768]{3,2,1,0:T(8,128)(2,1)}, bf16[16,16,2560]{2,1,0:T(8,128)(2,1)}, bf16[16,2,32,512]{3,2,1,0:T(8,128)(2,1)}, f32[16,8,128]{2,1,0:T(8,128)}) custom-call(bf16[2,16,32,768]{3,2,1,0:T(8,128)(2,1)} %bitcast.171, bf16[16,16,2560]{2,1,0:T(8,128)(2,1)} %pad_maximum_fusion.1.refs_1_, bf16[2,16,32,512]{3,2,1,0:T(8,128)(2,1)} %bitcast.158, ...), custom_call_target="tpu_custom_call" | custom-call | tf_op jit(solution)/shard_map/grads_plane/pallas_call | solution.py:146
  459.4 11.1 %grads_column.1 = f32[8,8,1408]{2,1,0:T(8,128)} custom-call(f32[8,8,1408]{2,1,0:T(8,128)} %fusion.11.refs_0_), custom_call_target="tpu_custom_call" | custom-call | tf_op jit(solution)/shard_map/grads_column/pallas_call | solution.py:146
  475.5 17.3 %grad_token_column.1 = f32[128,1024]{1,0:T(8,128)S(1)} custom-call(bf16[8,128,1024]{2,1,0:T(8,128)(2,1)S(1)} %bitcast.136), custom_call_target="tpu_custom_call" | custom-call | tf_op jit(solution)/shard_map/grad_token_column/pallas_call | solution.py:283
  (236 shorter events, 87.6 us)
Async XLA Ops:
  7.2 162.9 %all-gather.5.cloned.1.call-start = ((), (), s32[]{:S(2)}) async-start(), calls=%async_computation | async-start | bytes 1392640 | tf_op jit(solution)/shard_map/all_gather | solution.py:609
  9.1 6.6 %collective-permute-start = (bf16[16,2560]{1,0:T(8,128)(2,1)S(1)}, bf16[16,2560]{1,0:T(8,128)(2,1)S(1)}, u32[]{:S(2)}, u32[]{:S(2)}) collective-permute-start(bf16[16,2560]{1,0:T(8,128)(2,1)S(1)} %pad_maximum_fusion.8), channel_id=1, source_target_pairs={{0,0},{1,16},{2,32},{3,48},{16,1},{17,17},{18,33},{19,49},{32,2},{... | collective-permute-start | bytes 245768 | tf_op jit(solution)/shard_map/ppermute | solution.py:526
  16.3 197.7 %all-gather.7.cloned.1.call-start = ((), (), s32[]{:S(2)}) async-start(), calls=%async_computation.1 | async-start | bytes 1671168 | tf_op jit(solution)/shard_map/all_gather | solution.py:612
  65.5 21.4 %copy-start.28 = (bf16[2,16,32,512]{3,2,1,0:T(8,128)(2,1)}, bf16[2,16,32,512]{3,2,1,0:T(8,128)(2,1)S(1)}, u32[]{:S(2)}) copy-start(bf16[2,16,32,512]{3,2,1,0:T(8,128)(2,1)S(1)} %slice.162) | copy-start | bytes 3145732
  176.3 19.1 %copy-start.21 = (bf16[1,128,1024]{2,1,0:T(8,128)(2,1)S(1)}, bf16[1,128,1024]{2,1,0:T(8,128)(2,1)}, u32[]{:S(2)}) copy-start(bf16[1,128,1024]{2,1,0:T(8,128)(2,1)} %param.26) | copy-start | bytes 786436
  220.8 17.5 %copy-start.10 = (bf16[1,128,1024]{2,1,0:T(8,128)(2,1)S(1)}, bf16[1,128,1024]{2,1,0:T(8,128)(2,1)}, u32[]{:S(2)}) copy-start(bf16[1,128,1024]{2,1,0:T(8,128)(2,1)} %param.27) | copy-start | bytes 786436
  257.1 4.6 copy-start.8
  257.1 4.6 copy-start.16
  268.6 17.6 %copy-start.22 = (bf16[1,128,1024]{2,1,0:T(8,128)(2,1)S(1)}, bf16[1,128,1024]{2,1,0:T(8,128)(2,1)}, u32[]{:S(2)}) copy-start(bf16[1,128,1024]{2,1,0:T(8,128)(2,1)} %param.26) | copy-start | bytes 786436
  287.3 17.7 %copy-start.12 = (bf16[2,4,128,256]{3,2,1,0:T(8,128)(2,1)S(1)}, bf16[2,4,128,256]{3,2,1,0:T(8,128)(2,1)}, u32[]{:S(2)}) copy-start(bf16[2,4,128,256]{3,2,1,0:T(8,128)(2,1)} %attention_out.1) | copy-start | bytes 1572868
  308.2 11.2 %copy-start.3 = (bf16[1024,256]{1,0:T(8,128)(2,1)S(1)}, bf16[1024,256]{1,0:T(8,128)(2,1)}, u32[]{:S(2)}) copy-start(bf16[1024,256]{1,0:T(8,128)(2,1)} %copy-done.2) | copy-start | bytes 1572868
  308.2 11.3 %copy-start.7 = (bf16[4,2,128,256]{3,2,1,0:T(8,128)(2,1)S(1)}, bf16[4,2,128,256]{3,2,1,0:T(8,128)(2,1)}, u32[]{:S(2)}) copy-start(bf16[4,2,128,256]{3,2,1,0:T(8,128)(2,1)} %get-tuple-element.62) | copy-start | bytes 1572868
  471.3 27.8 %copy-start.53 = (f32[18]{0:T(128)}, f32[18]{0:T(128)S(1)}, u32[]{:S(2)}) copy-start(f32[18]{0:T(128)S(1)} %slice_reduce_fusion) | copy-start | bytes 220
  472.2 26.2 %copy-start.40 = (f32[8,8,256]{2,0,1:T(8,128)}, f32[8,8,256]{2,0,1:T(8,128)S(1)}, u32[]{:S(2)}) copy-start(f32[8,8,256]{2,0,1:T(8,128)S(1)} %slice.213) | copy-start | bytes 196612
  494.5 4.6 copy-start.52
  494.5 4.6 copy-start.54
  494.5 4.6 copy-start.55
  494.5 6.9 %copy-start.34 = (f32[24,1024]{1,0:T(8,128)S(1)}, f32[24,1024]{1,0:T(8,128)}, u32[]{:S(2)}) copy-start(f32[24,1024]{1,0:T(8,128)} %param.34) | copy-start | bytes 294916
  494.5 6.9 %copy-start.43 = (f32[24,1024]{1,0:T(8,128)S(1)}, f32[24,1024]{1,0:T(8,128)}, u32[]{:S(2)}) copy-start(f32[24,1024]{1,0:T(8,128)} %param.40) | copy-start | bytes 294916
  494.6 6.9 %copy-start.44 = (f32[24,1024]{1,0:T(8,128)S(1)}, f32[24,1024]{1,0:T(8,128)}, u32[]{:S(2)}) copy-start(f32[24,1024]{1,0:T(8,128)} %param.46) | copy-start | bytes 294916
  494.6 6.8 %collective-permute-start.1 = (f32[16,2560]{1,0:T(8,128)S(1)}, f32[16,2560]{1,0:T(8,128)S(1)}, u32[]{:S(2)}, u32[]{:S(2)}) collective-permute-start(f32[16,2560]{1,0:T(8,128)S(1)} %convert_reduce_fusion.2), channel_id=1, source_target_pairs={{0,0},{1,16},{2,32},{3,48},{16,1},{17,17},{18,33},{19,49},{32,2},{... | collective-permute-start | bytes 491528 | tf_op jit(solution)/shard_map/ppermute | solution.py:526
  497.4 4.8 copy-start.37
  497.4 4.8 copy-start.46
  497.4 4.8 copy-start.47
  (37 other events, 85.8 us)
Sparse Core Ops, SparseCore 0:
  16.5 51.0 all-gather.4
  70.3 61.6 all-gather.6

commit v2 on v1

--- a/solution.py
+++ b/solution.py
@@ -487,6 +487,942 @@
         ),
         name="attend_back",
     )(q_blocks, k_blocks, q, kv, grad, out, lse)
+
+
+class ColumnSums:
+    def __init__(self, me, part, paired, sending, landed, near_send, near_recv, far_send, far_recv):
+        self.me, self.z, self.core = me, me["zh"] * 2 + me["zl"], me["co"]
+        self.part, self.paired, self.sending, self.landed = part, paired, sending, landed
+        self.near_sems, self.far_sems = (near_send, near_recv), (far_send, far_recv)
+
+    def near(self, phase, off):
+        return pltpu.make_async_remote_copy(
+            src_ref=self.part.at[phase, off, 1 - self.core],
+            dst_ref=self.paired.at[phase, off],
+            send_sem=self.near_sems[0].at[phase, off],
+            recv_sem=self.near_sems[1].at[phase, off],
+            device_id=address(column_place(self.me, self.z, 1 - self.core)),
+            device_id_type=MESH,
+        )
+
+    def far(self, phase, off):
+        return pltpu.make_async_remote_copy(
+            src_ref=self.sending.at[phase, off],
+            dst_ref=self.landed.at[phase, off],
+            send_sem=self.far_sems[0].at[phase, off],
+            recv_sem=self.far_sems[1].at[phase, off],
+            device_id=address(column_place(self.me, lax.rem(self.z + off, 4), self.core)),
+            device_id_type=MESH,
+        )
+
+    def put(self, phase, off, terms):
+        self.part[phase, off] = terms.astype(BF16).reshape(2, ROWS, D)
+        self.near(phase, off).start()
+
+    def pass_on(self, phase, off):
+        self.near(phase, off).wait_recv()
+        both = self.part[phase, off, self.core].astype(F32) + self.paired[phase, off].astype(F32)
+        self.sending[phase, off] = both.astype(BF16)
+        self.far(phase, off).start()
+
+    def total(self, phase):
+        self.near(phase, 0).wait_recv()
+        total = self.part[phase, 0, self.core].astype(F32) + self.paired[phase, 0].astype(F32)
+        for off in (1, 3, 2):
+            self.far(phase, off).wait_recv()
+            total = total + self.landed[phase, off].astype(F32)
+        return total
+
+    def drain(self, phase):
+        for off in range(4):
+            self.near(phase, off).wait_send()
+            if off:
+                self.far(phase, off).wait_send()
+
+
+class ColumnGathers:
+    def __init__(self, me, blocks, near_send, near_recv, far_send, far_recv):
+        self.me, self.z, self.core = me, me["zh"] * 2 + me["zl"], me["co"]
+        self.blocks = blocks
+        self.near_sems, self.far_sems = (near_send, near_recv), (far_send, far_recv)
+
+    def far(self, phase, off, arriving):
+        z = lax.rem(self.z + 4 - off, 4) if arriving else self.z
+        block = self.blocks.at[phase, z * 2 + self.core]
+        return pltpu.make_async_remote_copy(
+            src_ref=block,
+            dst_ref=block,
+            send_sem=self.far_sems[0].at[phase, off],
+            recv_sem=self.far_sems[1].at[phase, off],
+            device_id=address(column_place(self.me, lax.rem(self.z + off, 4), self.core)),
+            device_id_type=MESH,
+        )
+
+    def near(self, phase, off, arriving):
+        core = 1 - self.core if arriving else self.core
+        block = self.blocks.at[phase, lax.rem(self.z + 4 - off, 4) * 2 + core]
+        return pltpu.make_async_remote_copy(
+            src_ref=block,
+            dst_ref=block,
+            send_sem=self.near_sems[0].at[phase, off],
+            recv_sem=self.near_sems[1].at[phase, off],
+            device_id=address(column_place(self.me, self.z, 1 - self.core)),
+            device_id_type=MESH,
+        )
+
+    def begin(self, phase, rows):
+        self.blocks[phase, self.z * 2 + self.core] = rows
+        for off in (1, 3, 2):
+            self.far(phase, off, False).start()
+        self.near(phase, 0, False).start()
+
+    def await_chip(self, phase, i):
+        off = i + lax.div(i, 2) * (5 - 2 * i)
+
+        @pl.when(i == 1)
+        def _():
+            for near_by in (1, 3):
+                self.far(phase, near_by, True).wait_recv()
+                self.near(phase, near_by, False).start()
+
+        @pl.when(i == 3)
+        def _():
+            self.far(phase, 2, True).wait_recv()
+            self.near(phase, 2, False).start()
+
+        self.near(phase, off, True).wait_recv()
+        return off, lax.rem(self.z + 4 - off, 4)
+
+    def drain(self, phase):
+        for off in range(4):
+            self.near(phase, off, False).wait_send()
+            if off:
+                self.far(phase, off, False).wait_send()
+
+
+def norm_factor(values):
+    return lax.rsqrt(jnp.mean(values * values, axis=-1, keepdims=True) + NORM_EPS)
+
+
+def norm_back(values, norm_gain, grad):
+    factor = norm_factor(values)
+    scaled = grad * norm_gain
+    inner = jnp.mean(values * scaled, axis=-1, keepdims=True)
+    grad_gain = jnp.sum(grad * values * factor, axis=0, keepdims=True)
+    return factor * scaled - values * (factor * factor * factor * inner), grad_gain
+
+
+def quarter(place):
+    return place["zl"] * 2 + place["co"]
+
+
+def at_quarter(place, t):
+    return dict(place, zl=lax.div(t, 2), co=lax.rem(t, 2))
+
+
+def row_user(me, k):
+    return at_quarter(shifted(me, SURFACE, k, 1), me["x"])
+
+
+def row_owner(me, k):
+    y, t = lax.div(k, 4), lax.rem(k, 4)
+    to = dict(me, x=quarter(me), y=lax.rem(me["y"] + y, 4))
+    return at_quarter(to, lax.rem(quarter(me) + t, 4))
+
+
+def row_slot(owner):
+    return owner["y"] * 4 + quarter(owner)
+
+
+def greet(barrier, place):
+    pl.semaphore_signal(barrier, inc=1, device_id=address(place), device_id_type=MESH)
+
+
+def greet_all(me, column, rows):
+    barrier = pltpu.get_barrier_semaphore()
+
+    def greet_surface(k, carry):
+        greet(barrier, shifted(me, SURFACE, k, 1))
+        return carry
+
+    def greet_column_all(k, carry):
+        greet(barrier, shifted(me, COLUMN, k, 1))
+        return carry
+
+    lax.fori_loop(1, PLANE, greet_surface, 0)
+    expected = PLANE - 1
+    if column == "all":
+        lax.fori_loop(1, RANKS, greet_column_all, 0)
+        expected = expected + RANKS - 1
+    else:
+        z = me["zh"] * 2 + me["zl"]
+        for off in (1, 2, 3):
+            greet(barrier, column_place(me, lax.rem(z + off, 4), me["co"]))
+        greet(barrier, column_place(me, z, 1 - me["co"]))
+        expected = expected + 4
+    if rows is not None:
+        at_home = me["x"] == quarter(me)
+
+        def greet_rows(k, carry):
+            @pl.when(jnp.logical_not(jnp.logical_and(k == 0, at_home)))
+            def _():
+                if rows != "own":
+                    greet(barrier, row_owner(me, k))
+                if rows != "use":
+                    greet(barrier, row_user(me, k))
+
+            return carry
+
+        lax.fori_loop(0, PLANE, greet_rows, 0)
+        count = PLANE - jnp.where(at_home, 1, 0)
+        expected = expected + (2 * count if rows == "both" else count)
+    pl.semaphore_wait(barrier, expected)
+
+
+class RowCopies:
+    def __init__(self, me, src, dst, send, recv, back):
+        self.me, self.src, self.dst, self.send, self.recv, self.back = me, src, dst, send, recv, back
+        self.at_home = me["x"] == quarter(me)
+
+    def copy(self, k, arriving):
+        me = self.me
+        if self.back:
+            to = row_owner(me, k)
+            frm = row_user(me, k) if arriving else me
+            src, slot = self.src.at[row_slot(to)], flat_index(frm, SURFACE)
+        else:
+            to = row_user(me, k)
+            frm = row_owner(me, k) if arriving else me
+            src, slot = self.src, row_slot(frm)
+        return pltpu.make_async_remote_copy(
+            src_ref=src,
+            dst_ref=self.dst.at[slot],
+            send_sem=self.send.at[k],
+            recv_sem=self.recv.at[slot],
+            device_id=address(to),
+            device_id_type=MESH,
+        )
+
+    def own(self):
+        me = self.me
+        if self.back:
+            src, slot = self.src.at[row_slot(me)], flat_index(me, SURFACE)
+        else:
+            src, slot = self.src, row_slot(me)
+        return pltpu.make_async_copy(src, self.dst.at[slot], self.recv.at[slot])
+
+    def each(self, remote, own):
+        def one(j, carry):
+            k = lax.rem(j * 7, PLANE)
+            itself = jnp.logical_and(k == 0, self.at_home)
+
+            @pl.when(itself)
+            def _():
+                own()
+
+            @pl.when(jnp.logical_not(itself))
+            def _():
+                remote(k)
+
+            return carry
+
+        lax.fori_loop(0, PLANE, one, 0)
+
+    def begin(self):
+        self.each(lambda k: self.copy(k, False).start(), lambda: self.own().start())
+
+    def arrive(self):
+        self.each(lambda k: self.copy(k, True).wait_recv(), lambda: self.own().wait())
+
+    def drain(self):
+        self.each(lambda k: self.copy(k, False).wait_send(), lambda: None)
+
+
+class Exchange:
+    def __init__(self, me, axes, take, put, send, recv):
+        self.me, self.axes, self.take, self.put, self.send, self.recv = me, axes, take, put, send, recv
+        self.n = math.prod(SIZE[a] for a in axes)
+        self.mix = {4: 1, 8: 3, 16: 7}[self.n]
+
+    def copy(self, k, arriving):
+        to = shifted(self.me, self.axes, k, 1)
+        frm = shifted(self.me, self.axes, k, -1) if arriving else self.me
+        return pltpu.make_async_remote_copy(
+            src_ref=self.take(to),
+            dst_ref=self.put(frm),
+            send_sem=self.send.at[k],
+            recv_sem=self.recv.at[k],
+            device_id=address(to),
+            device_id_type=MESH,
+        )
+
+    def each(self, act):
+        def one(j, carry):
+            act(lax.rem(j * self.mix, self.n))
+            return carry
+
+        lax.fori_loop(1, self.n, one, 0)
+
+    def begin(self):
+        self.each(lambda k: self.copy(k, False).start())
+
+    def arrive(self):
+        self.each(lambda k: self.copy(k, True).wait_recv())
+
+    def drain(self):
+        self.each(lambda k: self.copy(k, False).wait_send())
+
+
+def start_kernel(
+    sent_a,
+    sent_b,
+    tokens,
+    output_rows,
+    frequency,
+    q_mine,
+    kv_mine,
+    all_tokens,
+    output_wide,
+    gateup_low,
+    extra_out,
+    gains_out,
+    qkv_part,
+    projected,
+    cosine,
+    sine,
+    head_gains,
+    shares_a,
+    shares_b,
+    wide,
+    blocks,
+    queries,
+    keyvals,
+    a_send,
+    a_recv,
+    b_send,
+    b_recv,
+    w_send,
+    w_recv,
+    row_send,
+    row_recv,
+    near_send,
+    near_recv,
+    far_send,
+    far_recv,
+    q_send,
+    q_recv,
+    kv_send,
+    kv_recv,
+    relay_send,
+    relay_recv,
+    own_sems,
+):
+    me = where_am_i()
+    x, y = me["x"], me["y"]
+    rank, here = flat_index(me, COLUMN), flat_index(me, SURFACE)
+    gathers = ColumnGathers(me, blocks, near_send, near_recv, far_send, far_recv)
+    to_a = Exchange(
+        me,
+        COLUMN,
+        lambda to: sent_a.at[flat_index(to, COLUMN)],
+        lambda frm: shares_a.at[flat_index(frm, COLUMN)],
+        a_send,
+        a_recv,
+    )
+    to_b = Exchange(
+        me,
+        COLUMN,
+        lambda to: sent_b.at[flat_index(to, COLUMN)],
+        lambda frm: shares_b.at[flat_index(frm, COLUMN)],
+        b_send,
+        b_recv,
+    )
+    spread = Exchange(
+        me,
+        SURFACE,
+        lambda to: wide.at[:, here],
+        lambda frm: wide.at[:, flat_index(frm, SURFACE)],
+        w_send,
+        w_recv,
+    )
+    rows = RowCopies(me, output_rows, output_wide, row_send, row_recv, False)
+    own_a = pltpu.make_async_copy(sent_a.at[rank], shares_a.at[rank], own_sems.at[0])
+    own_b = pltpu.make_async_copy(sent_b.at[rank], shares_b.at[rank], own_sems.at[1])
+    own_a.start()
+    own_b.start()
+    greet_all(me, "all", "both")
+    to_a.begin()
+    gathers.begin(0, tokens[...])
+    rows.begin()
+    to_b.begin()
+
+    own_a.wait()
+    to_a.arrive()
+    wide[:, here] = shares_a[...].astype(BF16).reshape(2, 32, 640)
+    spread.begin()
+    extra_out[...] = shares_a[:, :, 512:]
+
+    lanes = lax.broadcasted_iota(jnp.int32, (BLOCK, HD), 1)
+    place = lax.broadcasted_iota(jnp.int32, (BLOCK, HD), 0).astype(F32)
+
+    def tables(j, carry):
+        for half in range(2):
+            first = shares_a[j, 2 + half : 3 + half, 512:]
+            angles = (first * float(BLOCK) + place) * frequency[...]
+            at = pl.ds(pl.multiple_of(j * ROWS + half * BLOCK, BLOCK), BLOCK)
+            cosine[at, :] = jnp.cos(angles)
+            sines = jnp.sin(angles)
+            sine[at, :] = jnp.where(lanes < HD // 2, -sines, sines)
+        return carry
+
+    lax.fori_loop(0, RANKS, tables, 0)
+    own_b.wait()
+    to_b.arrive()
+    gateup_low[...] = shares_b[...].astype(BF16).reshape(2, 32, 768)
+
+    spread.arrive()
+    qkv_part[...] = wide[..., :512].reshape(D, 512)
+    extra = wide[..., 512:].reshape(D, HD)
+    gains_out[...] = extra
+    entry = 2 * D + lax.broadcasted_iota(jnp.int32, (HD, 2 * HD), 1)
+    pick = (lax.broadcasted_iota(jnp.int32, (HD, 2 * HD), 0) == lax.rem(entry, 18)).astype(BF16)
+    entries = 2 * D + lax.broadcasted_iota(jnp.int32, (D, 2 * HD), 1)
+    owned = lax.broadcasted_iota(jnp.int32, (D, 2 * HD), 0) == 8 * lax.div(entries, 18)
+    gains = jnp.sum(jnp.where(owned, dot_nn(extra, pick), 0.0), axis=0, keepdims=True)
+    head_gains[0:1, :] = gains[:, :HD]
+    head_gains[1:2, :] = gains[:, HD:]
+
+    def q_copy(row_zh, pack):
+        return pltpu.make_async_remote_copy(
+            src_ref=queries.at[row_zh, pack],
+            dst_ref=q_mine.at[x, row_zh],
+            send_sem=q_send.at[row_zh, pack],
+            recv_sem=q_recv.at[row_zh, x],
+            device_id=address(dict(me, x=pack)),
+            device_id_type=MESH,
+        )
+
+    def kv_copy(row_zh, pack):
+        return pltpu.make_async_remote_copy(
+            src_ref=keyvals.at[row_zh, pack],
+            dst_ref=kv_mine.at[here, row_zh],
+            send_sem=kv_send.at[row_zh, pack],
+            recv_sem=kv_recv.at[row_zh, x],
+            device_id=address(dict(me, x=pack)),
+            device_id_type=MESH,
+        )
+
+    def q_own(row_zh):
+        return pltpu.make_async_copy(
+            queries.at[row_zh, x], q_mine.at[x, row_zh], own_sems.at[2 + row_zh]
+        )
+
+    def kv_own(row_zh):
+        return pltpu.make_async_copy(
+            keyvals.at[row_zh, x], kv_mine.at[here, row_zh], own_sems.at[4 + row_zh]
+        )
+
+    def relay(row_zh, from_x, k, arriving):
+        to_y = lax.rem(y + k, 4)
+        from_y = lax.rem(y + 4 - k, 4) if arriving else y
+        block = kv_mine.at[from_x * 4 + from_y, row_zh]
+        return pltpu.make_async_remote_copy(
+            src_ref=block,
+            dst_ref=block,
+            send_sem=relay_send.at[row_zh, from_x, k],
+            recv_sem=relay_recv.at[row_zh, from_x, k],
+            device_id=address(dict(me, y=to_y)),
+            device_id_type=MESH,
+        )
+
+    def project(i, carry):
+        off, at_z = gathers.await_chip(0, i)
+        at = pl.ds(pl.multiple_of(at_z * 2 * ROWS, 2 * ROWS), 2 * ROWS)
+        both = dot_nn(blocks[0, pl.ds(at_z * 2, 2)].reshape(2 * ROWS, D), qkv_part[...])
+        projected[at, :] = both[:, :384]
+        row_zh, first = lax.div(at_z, 2), lax.rem(at_z, 2) * 2
+        for head in range(3):
+            values = both[:, head * HD : (head + 1) * HD]
+            gain = head_gains[1:2, :] if head == 2 else head_gains[0:1, :]
+            normed = values * norm_factor(values) * gain
+            turned = (
+                normed * cosine[at, :] + pltpu.roll(normed, HD // 2, 1) * sine[at, :]
+            ).astype(BF16)
+            turned = turned.reshape(2, ROWS, HD)
+            for at_core in range(2):
+                if head == 2:
+                    keyvals[row_zh, first + at_core, :, :HD] = turned[at_core]
+                else:
+                    queries[row_zh, first + at_core, :, head * HD : (head + 1) * HD] = turned[
+                        at_core
+                    ]
+        values = both[:, 384:].astype(BF16).reshape(2, ROWS, HD)
+        for at_core in range(2):
+            pack = first + at_core
+            keyvals[row_zh, pack, :, HD:] = values[at_core]
+
+            @pl.when(pack != x)
+            def _():
+                kv_copy(row_zh, pack).start()
+                q_copy(row_zh, pack).start()
+
+            @pl.when(pack == x)
+            def _():
+                kv_own(row_zh).start()
+                q_own(row_zh).start()
+
+        return carry
+
+    lax.fori_loop(0, 4, project, 0)
+    for i in range(RANKS):
+        slot = pltpu.make_async_copy(blocks.at[0, i], all_tokens.at[i], own_sems.at[6 + i])
+        slot.start()
+    for row_zh in range(2):
+        kv_own(row_zh).wait()
+        for k in (2, 1, 3):
+            relay(row_zh, x, k, False).start()
+    for off in (1, 3, 2):
+        from_x = lax.rem(x + 4 - off, 4)
+        to_x = lax.rem(x + off, 4)
+        for row_zh in range(2):
+            pltpu.make_async_remote_copy(
+                src_ref=keyvals.at[row_zh, to_x],
+                dst_ref=kv_mine.at[from_x * 4 + y, row_zh],
+                send_sem=kv_send.at[row_zh, to_x],
+                recv_sem=kv_recv.at[row_zh, from_x],
+                device_id=address(dict(me, x=to_x)),
+                device_id_type=MESH,
+            ).wait_recv()
+            for k in (2, 1, 3):
+                relay(row_zh, from_x, k, False).start()
+    for off in (1, 3, 2):
+        from_x = lax.rem(x + 4 - off, 4)
+        to_x = lax.rem(x + off, 4)
+        for row_zh in range(2):
+            pltpu.make_async_remote_copy(
+                src_ref=queries.at[row_zh, to_x],
+                dst_ref=q_mine.at[from_x, row_zh],
+                send_sem=q_send.at[row_zh, to_x],
+                recv_sem=q_recv.at[row_zh, from_x],
+                device_id=address(dict(me, x=to_x)),
+                device_id_type=MESH,
+            ).wait()
+            kv_copy(row_zh, to_x).wait_send()
+    for row_zh in range(2):
+        q_own(row_zh).wait()
+
+    def finish(j, carry):
+        row_zh, from_x = lax.div(j, 4), lax.rem(j, 4)
+        for k in (1, 3, 2):
+            relay(row_zh, from_x, k, False).wait_send()
+            relay(row_zh, from_x, k, True).wait_recv()
+        return carry
+
+    lax.fori_loop(0, 8, finish, 0)
+    rows.arrive()
+    for i in range(RANKS):
+        pltpu.make_async_copy(blocks.at[0, i], all_tokens.at[i], own_sems.at[6 + i]).wait()
+    for exchange in (to_a, to_b, spread, rows):
+        exchange.drain()
+    gathers.drain(0)
+
+
+def start(number, sent_a, sent_b, tokens, output_rows, frequency):
+    anywhere = pl.BlockSpec(memory_space=pl.ANY)
+    vmem = pl.BlockSpec(memory_space=pltpu.VMEM)
+    dma = pltpu.SemaphoreType.DMA
+    struct = jax.ShapeDtypeStruct
+    return pl.pallas_call(
+        start_kernel,
+        out_shape=(
+            struct((4, 2, ROWS, 256), BF16),
+            struct((PLANE, 2, ROWS, 256), BF16),
+            struct((RANKS, ROWS, D), BF16),
+            struct((PLANE, 16, D), BF16),
+            struct((2, 32, 768), BF16),
+            struct((RANKS, 8, HD), F32),
+            struct((D, HD), BF16),
+            struct((D, 512), BF16),
+            struct((RANKS * ROWS, 384), F32),
+            struct((RANKS * ROWS, HD), F32),
+            struct((RANKS * ROWS, HD), F32),
+            struct((2, HD), F32),
+        ),
+        in_specs=[anywhere, anywhere, vmem, anywhere, vmem],
+        out_specs=(anywhere, anywhere, anywhere, anywhere) + (vmem,) * 8,
+        scratch_shapes=[
+            pltpu.VMEM((RANKS, 8, 640), F32),
+            pltpu.VMEM((RANKS, 8, 768), F32),
+            pltpu.VMEM((2, PLANE, 32, 640), BF16),
+            pltpu.VMEM((1, RANKS, ROWS, D), BF16),
+            pltpu.VMEM((2, 4, ROWS, 256), BF16),
+            pltpu.VMEM((2, 4, ROWS, 256), BF16),
+        ]
+        + [dma((RANKS,))] * 4
+        + [dma((PLANE,))] * 4
+        + [dma((1, 4))] * 4
+        + [dma((2, 4))] * 4
+        + [dma((2, 4, 4)), dma((2, 4, 4)), dma((6 + RANKS,))],
+        compiler_params=pltpu.CompilerParams(
+            collective_id=number, has_side_effects=True, vmem_limit_bytes=VMEM_LIMIT
+        ),
+        name="start",
+    )(sent_a, sent_b, tokens, output_rows, frequency)
+
+
+def middle_kernel(
+    out_mine,
+    wo,
+    gateup_low,
+    down_rows_low,
+    inputs,
+    upstream,
+    gains,
+    result,
+    grad_hidden,
+    gains_grad,
+    grad_mine,
+    gateup_parts,
+    down_parts,
+    output_lines,
+    attended,
+    blocks,
+    part,
+    paired,
+    sending,
+    landed,
+    gate_up,
+    activated,
+    grad_gate,
+    grad_attended,
+    gateup_lines,
+    down_grad,
+    down_lines,
+    branch,
+    hidden,
+    wgu,
+    down_wide,
+    wd,
+    near_send,
+    near_recv,
+    far_send,
+    far_recv,
+    gnear_send,
+    gnear_recv,
+    gfar_send,
+    gfar_recv,
+    att_send,
+    att_recv,
+    back_send,
+    back_recv,
+    plane_send,
+    plane_recv,
+    w_send,
+    w_recv,
+    row_send,
+    row_recv,
+    down_send,
+    down_recv,
+    own_sems,
+):
+    me = where_am_i()
+    x, here = me["x"], flat_index(me, SURFACE)
+    z = me["zh"] * 2 + me["zl"]
+    sums = ColumnSums(
+        me, part, paired, sending, landed, near_send, near_recv, far_send, far_recv
+    )
+    gathers = ColumnGathers(me, blocks, gnear_send, gnear_recv, gfar_send, gfar_recv)
+    own = pltpu.make_async_copy(out_mine.at[x], attended.at[:, x], own_sems.at[0])
+    own.start()
+    own_wgu = pltpu.make_async_copy(gateup_low, wgu.at[:, here], own_sems.at[2])
+    own_wgu.start()
+    spread = Exchange(
+        me,
+        SURFACE,
+        lambda to: gateup_low,
+        lambda frm: wgu.at[:, flat_index(frm, SURFACE)],
+        w_send,
+        w_recv,
+    )
+    rows_in = RowCopies(me, down_rows_low, down_wide, row_send, row_recv, False)
+    rows_back = RowCopies(me, down_lines, down_parts, down_send, down_recv, True)
+    gateup_back = Exchange(
+        me,
+        SURFACE,
+        lambda to: gateup_lines.at[:, flat_index(to, SURFACE)],
+        lambda frm: gateup_parts.at[flat_index(frm, SURFACE)],
+        plane_send,
+        plane_recv,
+    )
+    own_gateup = pltpu.make_async_copy(
+        gateup_lines.at[:, here], gateup_parts.at[here], own_sems.at[1]
+    )
+    greet_all(me, "some", "both")
+
+    def attention_out(k, arriving):
+        frm = shifted(me, ("x",), k, -1) if arriving else me
+        to = shifted(me, ("x",), k, 1)
+        return pltpu.make_async_remote_copy(
+            src_ref=out_mine.at[to["x"]],
+            dst_ref=attended.at[:, frm["x"]],
+            send_sem=att_send.at[k],
+            recv_sem=att_recv.at[k],
+            device_id=address(to),
+            device_id_type=MESH,
+        )
+
+    for k in (2, 1, 3):
+        attention_out(k, False).start()
+    spread.begin()
+    rows_in.begin()
+    own.wait()
+    for k in (1, 3, 2):
+        attention_out(k, True).wait_recv()
+
+    def project_out(i, carry):
+        back = 3 - i
+        off = back + lax.div(back, 2) * (5 - 2 * back)
+        to_z = lax.rem(z + off, 4)
+        rows = attended[lax.div(to_z, 2), pl.ds(lax.rem(to_z, 2) * 2, 2)].reshape(2 * ROWS, 256)
+        sums.put(0, off, dot_nn(rows, wo[...]))
+
+        @pl.when(i >= 1)
+        def _():
+            last = back + 1
+            sums.pass_on(0, last + lax.div(last, 2) * (5 - 2 * last))
+
+        return carry
+
+    lax.fori_loop(0, 4, project_out, 0)
+    branch[...] = sums.total(0)
+    normed = branch[...] * norm_factor(branch[...]) * gains[0:1, :]
+    hidden[...] = inputs[...].astype(F32) + normed
+    gathers.begin(0, hidden[...].astype(BF16))
+
+    def chip_rows(phase, at_z):
+        return blocks[phase, pl.ds(at_z * 2, 2)].reshape(2 * ROWS, D)
+
+    def pass_on_last(phase, i):
+        @pl.when(i >= 2)
+        def _():
+            last = i - 1
+            sums.pass_on(phase, last + lax.div(last, 2) * (5 - 2 * last))
+
+    def at_rows(at_z):
+        return pl.ds(pl.multiple_of(at_z * 2 * ROWS, 2 * ROWS), 2 * ROWS)
+
+    own_wgu.wait()
+    spread.arrive()
+    rows_in.arrive()
+
+    def down_line_in(j, carry):
+        at = pl.ds(pl.multiple_of(j * 48, 16), 48)
+        pair = down_wide[pl.ds(2 * j, 2)].astype(F32)
+        for half in range(2):
+            part = pair[:, half * 24 : half * 24 + 24].reshape(48, 512)
+            wd[at, half * 512 : half * 512 + 512] = part.astype(BF16)
+        return carry
+
+    lax.fori_loop(0, PLANE // 2, down_line_in, 0)
+
+    def feed_forward(i, carry):
+        off, at_z = gathers.await_chip(0, i)
+        both = dot_nn(chip_rows(0, at_z), wgu[...].reshape(D, 768))
+        gate_up[at_rows(at_z), :] = both
+        gate, up = both[:, :384], both[:, 384:]
+        acts = (gate * (1.0 / (1.0 + jnp.exp(-gate))) * up).astype(BF16)
+        activated[at_rows(at_z), :] = acts
+        sums.put(1, lax.rem(4 - off, 4), dot_nn(acts, wd[...]))
+
+        @pl.when(i >= 2)
+        def _():
+            last = i - 1
+            sums.pass_on(1, 4 - (last + lax.div(last, 2) * (5 - 2 * last)))
+
+        return carry
+
+    lax.fori_loop(0, 4, feed_forward, 0)
+    sums.pass_on(1, 2)
+    ffn_out = sums.total(1)
+    grad = upstream[...].astype(F32)
+    result[...] = (hidden[...] + ffn_out * norm_factor(ffn_out) * gains[1:2, :]).astype(BF16)
+    grad_ffn, grad_ffn_gain = norm_back(ffn_out, gains[1:2, :], grad)
+    gathers.begin(1, grad_ffn.astype(BF16))
+    gains_grad[1:2, :] = grad_ffn_gain
+
+    def feed_forward_back(i, carry):
+        off, at_z = gathers.await_chip(1, i)
+        grad_act = dot_nt(chip_rows(1, at_z), wd[...])
+        gate, up = gate_up[at_rows(at_z), :384], gate_up[at_rows(at_z), 384:]
+        sig = 1.0 / (1.0 + jnp.exp(-gate))
+        grad_gate[at_rows(at_z), :384] = (
+            grad_act * up * (sig * (1.0 + gate * (1.0 - sig)))
+        ).astype(BF16)
+        grad_gate[at_rows(at_z), 384:] = (grad_act * (gate * sig)).astype(BF16)
+        sums.put(2, lax.rem(4 - off, 4), dot_nt(grad_gate[at_rows(at_z), :], wgu[...].reshape(D, 768)))
+
+        @pl.when(i >= 2)
+        def _():
+            last = i - 1
+            sums.pass_on(2, 4 - (last + lax.div(last, 2) * (5 - 2 * last)))
+
+        return carry
+
+    lax.fori_loop(0, 4, feed_forward_back, 0)
+    sums.pass_on(2, 2)
+
+    def gateup_rows(j, carry):
+        cols = pl.ds(pl.multiple_of(j * 256, 256), 256)
+        grads = dot_tn(blocks[0, :, :, cols].reshape(RANKS * ROWS, 256), grad_gate[...])
+        gateup_lines[lax.div(j, 2), pl.ds(lax.rem(j, 2) * 8, 8)] = grads.astype(BF16).reshape(
+            8, 32, 768
+        )
+        return carry
+
+    lax.fori_loop(0, 4, gateup_rows, 0)
+    own_gateup.start()
+    gateup_back.begin()
+
+    def down_rows(j, carry):
+        cols = pl.ds(pl.multiple_of(j * 128, 128), 128)
+        down_grad[cols, :] = dot_tn(activated[:, cols], blocks[1].reshape(RANKS * ROWS, D))
+        return carry
+
+    lax.fori_loop(0, 3, down_rows, 0)
+
+    def down_line(s, carry):
+        rows = down_grad[pl.ds(pl.multiple_of(s * 24, 8), 24), :].astype(BF16)
+        down_lines[s, 0:24, :] = rows[:, :512]
+        down_lines[s, 24:48, :] = rows[:, 512:]
+        return carry
+
+    lax.fori_loop(0, PLANE, down_line, 0)
+    rows_back.begin()
+
+    total = grad + sums.total(2)
+    grad_hidden[...] = total
+    grad_branch, grad_attn_gain = norm_back(branch[...], gains[0:1, :], total)
+    gathers.begin(2, grad_branch.astype(BF16))
+    gains_grad[0:1, :] = grad_attn_gain
+
+    def to_attention(row_zh, pack):
+        return pltpu.make_async_remote_copy(
+            src_ref=grad_attended.at[row_zh, pack],
+            dst_ref=grad_mine.at[x, row_zh],
+            send_sem=back_send.at[row_zh, pack],
+            recv_sem=back_recv.at[row_zh, x],
+            device_id=address(dict(me, x=pack)),
+            device_id_type=MESH,
+        )
+
+    def own_attention(row_zh):
+        return pltpu.make_async_copy(
+            grad_attended.at[row_zh, x], grad_mine.at[x, row_zh], own_sems.at[3 + row_zh]
+        )
+
+    def project_out_back(i, carry):
+        off, at_z = gathers.await_chip(2, i)
+        grads = dot_nt(chip_rows(2, at_z), wo[...]).astype(BF16).reshape(2, ROWS, 256)
+        row_zh = lax.div(at_z, 2)
+        for at_core in range(2):
+            pack = lax.rem(at_z, 2) * 2 + at_core
+            grad_attended[row_zh, pack] = grads[at_core]
+
+            @pl.when(pack != x)
+            def _():
+                to_attention(row_zh, pack).start()
+
+            @pl.when(pack == x)
+            def _():
+                own_attention(row_zh).start()
+
+        return carry
+
+    lax.fori_loop(0, 4, project_out_back, 0)
+
+    def output_rows(j, carry):
+        cols = pl.ds(pl.multiple_of(j * 128, 128), 128)
+        grads = dot_tn(
+            attended[:, :, :, cols].reshape(RANKS * ROWS, 128), blocks[2].reshape(RANKS * ROWS, D)
+        )
+        output_lines[pl.ds(j * 8, 8)] = grads.astype(BF16).reshape(8, 16, D)
+        return carry
+
+    lax.fori_loop(0, 2, output_rows, 0)
+
+    for k in (1, 3, 2):
+        attention_out(k, False).wait_send()
+        frm_x = lax.rem(x + 4 - k, 4)
+        to_x = lax.rem(x + k, 4)
+        for row_zh in range(2):
+            to_attention(row_zh, to_x).wait_send()
+            pltpu.make_async_remote_copy(
+                src_ref=grad_attended.at[row_zh, to_x],
+                dst_ref=grad_mine.at[frm_x, row_zh],
+                send_sem=back_send.at[row_zh, to_x],
+                recv_sem=back_recv.at[row_zh, frm_x],
+                device_id=address(dict(me, x=to_x)),
+                device_id_type=MESH,
+            ).wait_recv()
+    for row_zh in range(2):
+        own_attention(row_zh).wait()
+    for phase in range(3):
+        sums.drain(phase)
+        gathers.drain(phase)
+    own_gateup.wait()
+    gateup_back.arrive()
+    rows_back.arrive()
+    for exchange in (spread, rows_in, gateup_back, rows_back):
+        exchange.drain()
+
+
+def middle(number, out_mine, wo, gateup_low, down_rows, inputs, upstream, gains):
+    anywhere = pl.BlockSpec(memory_space=pl.ANY)
+    vmem = pl.BlockSpec(memory_space=pltpu.VMEM)
+    block = (ROWS, D)
+    dma = pltpu.SemaphoreType.DMA
+    return pl.pallas_call(
+        middle_kernel,
+        out_shape=(
+            jax.ShapeDtypeStruct(block, BF16),
+            jax.ShapeDtypeStruct(block, F32),
+            jax.ShapeDtypeStruct((2, D), F32),
+            jax.ShapeDtypeStruct((4, 2, ROWS, 256), BF16),
+            jax.ShapeDtypeStruct((PLANE, 2, 32, 768), BF16),
+            jax.ShapeDtypeStruct((PLANE, 48, 512), BF16),
+            jax.ShapeDtypeStruct((PLANE, 16, D), BF16),
+        ),
+        in_specs=[anywhere, vmem, anywhere, anywhere, vmem, vmem, vmem],
+        out_specs=(vmem, vmem, vmem, anywhere, anywhere, anywhere, vmem),
+        scratch_shapes=[
+            pltpu.VMEM((2, 4, ROWS, 256), BF16),
+            pltpu.VMEM((3, RANKS) + block, BF16),
+            pltpu.VMEM((3, 4, 2) + block, BF16),
+            pltpu.VMEM((3, 4) + block, BF16),
+            pltpu.VMEM((3, 4) + block, BF16),
+            pltpu.VMEM((3, 4) + block, BF16),
+            pltpu.VMEM((RANKS * ROWS, 768), F32),
+            pltpu.VMEM((RANKS * ROWS, 384), BF16),
+            pltpu.VMEM((RANKS * ROWS, 768), BF16),
+            pltpu.VMEM((2, 4, ROWS, 256), BF16),
+            pltpu.VMEM((2, PLANE, 32, 768), BF16),
+            pltpu.VMEM((384, D), F32),
+            pltpu.VMEM((PLANE, 48, 512), BF16),
+            pltpu.VMEM(block, F32),
+            pltpu.VMEM(block, F32),
+            pltpu.VMEM((2, PLANE, 32, 768), BF16),
+            pltpu.VMEM((PLANE, 48, 512), BF16),
+            pltpu.VMEM((384, D), BF16),
+        ]
+        + [dma((3, 4))] * 8
+        + [dma((4,)), dma((4,)), dma((2, 4)), dma((2, 4))]
+        + [dma((PLANE,))] * 8
+        + [dma((5,))],
+        compiler_params=pltpu.CompilerParams(
+            collective_id=number, has_side_effects=True, vmem_limit_bytes=VMEM_LIMIT
+        ),
+        name="middle",
+    )(out_mine, wo, gateup_low, down_rows, inputs, upstream, gains)
 
 
 def rms_norm(values, norm_gain):
@@ -551,117 +1487,64 @@
     gains_square,
 ):
     inputs = tokens[0]
-    upstream = cotangent[0].astype(F32)
     at_x, at_y = lax.axis_index("x"), lax.axis_index("y")
 
     own_blocks = (positions[0] + LONG * seq_ids[0]).reshape(-1, BLOCK)[:, 0] // BLOCK
-    extra = jnp.zeros((8, HD), F32)
-    extra = extra.at[0, : norm_gains.shape[0]].set(norm_gains)
-    extra = extra.at[1, :BLOCK].set(own_blocks.astype(F32))
-    sent = jnp.concatenate(
+    own_pair = lax.dynamic_slice_in_dim(own_blocks, 2 * lax.axis_index(("zh", "x", "y")), 2)
+    own_pair = jnp.where(own_pair >= LONG // BLOCK, own_pair - LONG // BLOCK, own_pair)
+    extra = jnp.concatenate(
+        [
+            jnp.pad(norm_gains, (0, HD - norm_gains.shape[0]))[None],
+            jnp.pad(own_blocks.astype(F32), (0, HD - BLOCK))[None],
+            jnp.broadcast_to(own_pair.astype(F32)[:, None], (2, HD)),
+            jnp.zeros((4, HD), F32),
+        ]
+    )
+    sent_a = jnp.concatenate(
         [
             by_rank(query_weight, 256),
             by_rank(keyval_weight[:, :KV], 128),
             by_rank(keyval_weight[:, KV:], 128),
             jnp.broadcast_to(extra[:, None, :], (8, RANKS, HD)),
-            by_rank(gateup_weight[:, :FF], 384),
-            by_rank(gateup_weight[:, FF:], 384),
         ],
         axis=2,
     ).transpose(1, 0, 2)
-    (shares,) = push(
-        "weights_column",
+    sent_b = jnp.concatenate(
+        [by_rank(gateup_weight[:, :FF], 384), by_rank(gateup_weight[:, FF:], 384)], axis=2
+    ).transpose(1, 0, 2)
+    frequency = ROPE_BASE ** (-jnp.arange(HD // 2, dtype=F32) * 2.0 / HD)
+    (
+        q_mine,
+        kv_mine,
+        all_tokens,
+        output_wide,
+        gateup_low,
+        extras,
+        gains_low,
+        qkv_part,
+        projected,
+        cosine,
+        sine,
+        head_gains,
+    ) = start(
         1,
-        [sent],
-        [(sent.shape, F32)],
-        [
-            (
-                0,
-                0,
-                COLUMN,
-                lambda ref, to: ref.at[flat_index(to, COLUMN)],
-                lambda ref, frm: ref.at[flat_index(frm, COLUMN)],
-            )
-        ],
-    )
-    shares_low = shares.astype(BF16).reshape(2, 32, 1408)
-    all_tokens = gather_column("tokens_column", 2, inputs).reshape(RANKS * ROWS, D)
-    (qkv_wide,) = push(
-        "weights_plane",
-        3,
-        [shares_low[..., :640]],
-        [((2, PLANE, 32, 640), BF16)],
-        [
-            (
-                0,
-                0,
-                SURFACE,
-                lambda ref, to: ref,
-                lambda ref, frm: ref.at[:, flat_index(frm, SURFACE)],
-            )
-        ],
-    )
-    row_shares = swap_owner(
-        jnp.concatenate(
-            [output_weight.astype(BF16), down_weight.astype(BF16).reshape(16, 1536)], axis=1
-        )
-    )
-    row_wide = lax.all_gather(row_shares, ("y", "x"))
-    output_part = row_wide[:, :, :D].reshape(256, D)
-    down_part = row_wide[:, :, D:].reshape(384, D)
-    gateup_part = lax.all_gather(shares_low[..., 640:], SURFACE, axis=1).reshape(D, 768)
-
-    qkv_part = qkv_wide[..., :512].reshape(D, 512)
-    gains_all = (
-        qkv_wide[..., 512:].reshape(2, PLANE, 4, 8, HD)[:, :, :, 0, :18].reshape(-1).astype(F32)
-    )
+        sent_a,
+        sent_b,
+        inputs,
+        output_weight.astype(BF16),
+        jnp.concatenate([frequency, frequency])[None],
+    )
+    all_tokens = all_tokens.reshape(RANKS * ROWS, D)
+    gains_all = gains_low.reshape(-1, 8, HD)[:, 0, :18].reshape(-1).astype(F32)
     attn_gain = gains_all[:D]
     ffn_gain = gains_all[D : 2 * D]
-    query_gain = gains_all[2 * D : 2 * D + HD]
-    key_gain = gains_all[2 * D + HD :]
-
-    blocks = shares[:4, 1, 512 : 512 + BLOCK].astype(jnp.int32).reshape(4, 2, 4, 4, 2)
+
+    blocks = extras[:4, 1, :BLOCK].astype(jnp.int32).reshape(4, 2, 4, 4, 2)
     pack_blocks = lax.dynamic_index_in_dim(blocks, at_x, 0, keepdims=False)
     key_blocks = pack_blocks.transpose(1, 2, 0, 3).reshape(-1)
     query_blocks = (
         lax.dynamic_index_in_dim(pack_blocks, at_y, 2, keepdims=False).transpose(1, 0, 2).reshape(-1)
     )
-    row_blocks = lax.dynamic_index_in_dim(
-        lax.dynamic_index_in_dim(blocks, at_x, 2, keepdims=False), at_y, 2, keepdims=False
-    ).transpose(1, 0, 2)
-    slots = row_blocks[..., None] * BLOCK + jnp.arange(BLOCK, dtype=jnp.int32)
-    places = jnp.where(slots >= LONG, slots - LONG, slots).reshape(-1)
-    halfway = HD // 2
-    frequency = ROPE_BASE ** (-jnp.arange(halfway, dtype=F32) * 2.0 / HD)
-    angles = places.astype(F32)[:, None] * frequency[None, :]
-    cosine = jnp.cos(angles)[:, None, :]
-    sine_part = jnp.sin(angles)[:, None, :]
-
-    qkv_proj = dot_nn(all_tokens, qkv_part)
-    head_gains = jnp.stack([query_gain, query_gain, key_gain])
-    heads_in = qkv_proj[:, :384].reshape(-1, 3, HD)
-    prepare = functools.partial(head_prepare, cosine=cosine, sine_part=sine_part)
-    heads_use, heads_pull = jax.vjp(prepare, heads_in, head_gains)
-    qkv = jnp.concatenate(
-        [heads_use.reshape(-1, 384).astype(BF16), qkv_proj[:, 384:].astype(BF16)], axis=1
-    ).reshape(2, 4, ROWS, 512)
-
-    def to_pack_x(ref, to):
-        return ref.at[:, to["x"]]
-
-    def from_x(ref, frm):
-        return ref.at[frm["x"]]
-
-    q_mine, kv_mine = push(
-        "attention_in",
-        4,
-        [qkv[..., :256], qkv[..., 256:]],
-        [((4, 2, ROWS, 256), BF16), ((PLANE, 2, ROWS, 256), BF16)],
-        [
-            (1, 1, SURFACE, to_pack_x, lambda ref, frm: ref.at[flat_index(frm, SURFACE)]),
-            (0, 0, ("x",), to_pack_x, from_x),
-        ],
-    )
     q_mine = q_mine.reshape(1024, 256)
     kv_mine = kv_mine.reshape(PACK_TOK, 256)
     out_mine, lse = attend(query_blocks, key_blocks, q_mine, kv_mine)
@@ -672,57 +1555,15 @@
     def from_pack_x(ref, frm):
         return ref.at[:, frm["x"]]
 
-    (attended,) = push(
-        "attention_out",
+    result, grad_hidden, gains_grad, grad_mine, gateup_parts, down_parts, output_lines = middle(
         5,
-        [out_mine.reshape(4, 2, ROWS, 256)],
-        [((2, 4, ROWS, 256), BF16)],
-        [(0, 0, ("x",), to_x, from_pack_x)],
-    )
-    attended = attended.reshape(RANKS * ROWS, 256)
-
-    branch = sum_column(
-        "branch_column", 6, dot_nn(attended, output_part).astype(BF16).reshape(RANKS, ROWS, D)
-    )
-    hidden = inputs.astype(F32) + rms_norm(branch, attn_gain)
-
-    all_hidden = gather_column("hidden_column", 7, hidden.astype(BF16)).reshape(RANKS * ROWS, D)
-    gate_up = dot_nn(all_hidden, gateup_part)
-    activated = swiglu(gate_up).astype(BF16)
-    ffn_out = sum_column(
-        "ffn_column", 8, dot_nn(activated, down_part).astype(BF16).reshape(RANKS, ROWS, D)
-    )
-    ffn_norm_out, ffn_pull = jax.vjp(rms_norm, ffn_out, ffn_gain)
-    result = hidden + ffn_norm_out
-    grad_ffn_out, grad_ffn_gain = ffn_pull(upstream)
-
-    grad_ffn = gather_column("grad_ffn_column", 9, grad_ffn_out.astype(BF16)).reshape(
-        RANKS * ROWS, D
-    )
-    down_grad = dot_tn(activated, grad_ffn)
-    grad_act = dot_nt(grad_ffn, down_part)
-    act_out, act_pull = jax.vjp(swiglu, gate_up)
-    grad_gate_low = act_pull(grad_act)[0].astype(BF16)
-    gateup_grad = dot_tn(all_hidden, grad_gate_low)
-    grad_hidden = upstream + sum_column(
-        "grad_hidden_column",
-        10,
-        dot_nt(grad_gate_low, gateup_part).astype(BF16).reshape(RANKS, ROWS, D),
-    )
-    attn_norm_out, attn_pull = jax.vjp(rms_norm, branch, attn_gain)
-    grad_branch_own, grad_attn_gain = attn_pull(grad_hidden)
-    grad_branch = gather_column("grad_branch_column", 11, grad_branch_own.astype(BF16)).reshape(
-        RANKS * ROWS, D
-    )
-    output_grad = dot_tn(attended, grad_branch)
-    grad_attended = dot_nt(grad_branch, output_part).astype(BF16)
-
-    (grad_mine,) = push(
-        "attention_grad_in",
-        12,
-        [grad_attended.reshape(2, 4, ROWS, 256)],
-        [((4, 2, ROWS, 256), BF16)],
-        [(0, 0, ("x",), to_pack_x, from_x)],
+        out_mine.reshape(4, 2, ROWS, 256),
+        output_wide.reshape(256, D),
+        gateup_low,
+        jnp.concatenate([down_weight[:, :512], down_weight[:, 512:]], axis=0).astype(BF16),
+        inputs,
+        cotangent[0],
+        jnp.stack([attn_gain, ffn_gain]),
     )
     dq_mine, dkv_mine = attend_back(
         query_blocks, key_blocks, q_mine, kv_mine, grad_mine.reshape(1024, 256), out_mine, lse
@@ -744,6 +1585,12 @@
         ],
     )
     dkv = jnp.sum(dkv_parts.astype(F32), axis=0).reshape(RANKS * ROWS, 256)
+    half = HD // 2
+    prepare = functools.partial(
+        head_prepare, cosine=cosine[:, None, :half], sine_part=sine[:, None, half:]
+    )
+    three = jnp.stack([head_gains[0], head_gains[0], head_gains[1]])
+    heads_use, heads_pull = jax.vjp(prepare, projected.reshape(-1, 3, HD), three)
     grad_heads = jnp.concatenate([dq.reshape(RANKS * ROWS, 256).astype(F32), dkv[:, :HD]], axis=1)
     grad_heads_in, grad_head_gains = heads_pull(grad_heads.reshape(-1, 3, HD))
     grad_qkv = jnp.concatenate(
@@ -758,8 +1605,8 @@
 
     gains_grad = jnp.concatenate(
         [
-            grad_attn_gain,
-            grad_ffn_gain,
+            gains_grad[0],
+            gains_grad[1],
             grad_head_gains[0] + grad_head_gains[1],
             grad_head_gains[2],
         ]
@@ -778,35 +1625,25 @@
     def to_surface_swapped(ref, to):
         return ref.at[flat_index(to, ("y", "x"))]
 
-    gateup_lines = gateup_grad.astype(BF16).reshape(2, PLANE, 32, 768)
     qkv_lines = qkv_grad.astype(BF16).reshape(2, PLANE, 32, 512)
-    row_lines = jnp.concatenate(
-        [
-            output_grad.astype(BF16).reshape(PLANE, 16, D),
-            down_grad.astype(BF16).reshape(PLANE, 16, 1536),
-        ],
-        axis=2,
-    )
-    gateup_parts, row_parts, qkv_parts, gains_parts = push(
+    output_parts, qkv_parts, gains_parts = push(
         "grads_plane",
         15,
-        [gateup_lines, row_lines, qkv_lines, gains_lines],
+        [output_lines, qkv_lines, gains_lines],
         [
-            ((PLANE, 2, 32, 768), BF16),
-            ((PLANE, 16, D + 1536), BF16),
+            ((PLANE, 16, D), BF16),
             ((PLANE, 2, 32, 512), BF16),
             ((PLANE, RANKS, HD), F32),
         ],
         [
-            (0, 0, SURFACE, to_surface_inner, to_surface),
-            (1, 1, SURFACE, to_surface_swapped, to_surface),
-            (2, 2, SURFACE, to_surface_inner, to_surface),
-            (3, 3, SURFACE, to_surface, to_surface),
+            (0, 0, SURFACE, to_surface_swapped, to_surface),
+            (1, 1, SURFACE, to_surface_inner, to_surface),
+            (2, 2, SURFACE, to_surface, to_surface),
         ],
     )
-    row_sum = swap_owner(jnp.sum(row_parts.astype(F32), axis=0))
-    output_sum = row_sum[:, :D]
-    down_sum = row_sum[:, D:].reshape(24, D)
+    down_wide = jnp.sum(down_parts.astype(F32), axis=0)
+    output_sum = swap_owner(jnp.sum(output_parts.astype(F32), axis=0))
+    down_sum = jnp.concatenate([down_wide[:24], down_wide[24:]], axis=1)
     gains_sums = jnp.sum(gains_parts, axis=0).reshape(RANKS, 1, HD)
     column_sums = jnp.concatenate(
         [
@@ -860,7 +1697,7 @@
         norm_gains, gains_sum, gains_mean, gains_square, RATE_GAIN, 0.0
     )
     return (
-        result.astype(BF16)[None],
+        result[None],
         token_grad[None],
         query_sum,
         keyval_sum,

time: 516 us -> 405 us (0.78)
  Pallas kernels: 385 us -> 350 us
  matrix products: 29.9 us -> 5.23 us
  local copies, waits for them, and re-layouts: 40.6 us -> 22.2 us
  between operations: 15.1 us -> 1.34 us
  other arithmetic: 28.1 us -> 18.1 us
    pallas_call x4 -> x2, Pallas kernels: 71.5 us -> 214 us  [the longest x1 141 us: middle(): pl.pallas_call(middle_kernel, out_shape=(jax.ShapeDtypeStruct(block, BF16...]
    pallas_call x8 -> x3, Pallas kernels: 189 us -> 75.2 us  [push(): pl.pallas_call(functools.partial(push_kernel, channels, len(arrays), len(...]
    pallas_call x4 -> x1, Pallas kernels: 71 us -> 17.4 us  [sum_column(): pl.pallas_call(sum_kernel, out_shape=jax.ShapeDtypeStruct(block, F32), in...]
    dot_general x4 -> x0, matrix products: 9.72 us -> none  [dot_nn(): lax.dot_general(a, b, (((1,), (0,)), ((), ())), preferred_element_type=F32)]
    dot_general x4 -> x1, matrix products: 10.6 us -> 1.3 us  [dot_nt(): lax.dot_general(a, b, (((1,), (1,)), ((), ())), preferred_element_type=F32)]
    unnamed x121 -> x73, local copies, waits for them, and re-layouts: 16.4 us -> 8.35 us
    slice x11 -> x10, local copies, waits for them, and re-layouts: 7.94 us -> 1.58 us  [the longest x1 0.95 us: body(): gateup_weight[:, :FF]]
    convert_element_type x10 -> x4, other arithmetic: 6.13 us -> 0.1 us  [the longest x1 0.08 us: body(): own_pair.astype(F32)[:, None]]
  transfers between devices with their start and end apart: 4 -> 1, of which waited for: 2 -> 0; matrix products, arithmetic and copies ran while one was open for 6% -> 3% of each run, Pallas kernels for 32% -> 7%
where the time goes in v2:
time: 405 us; the launch traced here: 402 us
  Pallas kernels  350 us (86%)
  local copies, waits for them, and re-layouts  22.2 us (5%)
  other arithmetic  18.1 us (4%)
  matrix products  5.23 us (1%)
  starting transfers between devices  4.72 us (1%)
    pallas_call x1, Pallas kernels, middle(): pl.pallas_call(middle_kernel, out_shape=(jax.ShapeDtypeStruct(block, BF16...  141 us
    pallas_call x3, Pallas kernels, push(): pl.pallas_call(functools.partial(push_kernel, channels, len(arrays), len(...  75.2 us
    pallas_call x1, Pallas kernels, start(): pl.pallas_call(start_kernel, out_shape=(struct((4, 2, ROWS, 256), BF16),...  72.9 us
    pallas_call x1, Pallas kernels, attend_back(): pl.pallas_call(attend_back_kernel, out_shape=(jax.ShapeDtypeStruct(q.shap...  25.1 us
    pallas_call x1, Pallas kernels, attend(): pl.pallas_call(attend_kernel, out_shape=(jax.ShapeDtypeStruct(q.shape, BF...  18.6 us
    pallas_call x1, Pallas kernels, sum_column(): pl.pallas_call(sum_kernel, out_shape=jax.ShapeDtypeStruct(block, F32), in...  17.4 us
    unnamed x73, local copies, waits for them, and re-layouts  8.35 us
  transfers between devices with their start and end apart: 1, of which 0 were waited for; matrix products, arithmetic and copies ran while one was open for 3% of the time, Pallas kernels for 7%

profile of v2, /device:TPU:1, one launch (start us, length us, event | category | flops | bytes accessed | tf_op | source)
XLA Modules:
  0.0 402.0 jit_solution(5954677271581511936)
XLA Ops:
  2.8 0.9 convert.11
  4.5 1.0 fusion.21
  7.1 72.9 %start.1 = (bf16[4,2,128,256]{3,2,1,0:T(8,128)(2,1)S(1)}, bf16[16,2,128,256]{3,2,1,0:T(8,128)(2,1)}, bf16[8,128,1024]{2,1,0:T(8,128)(2,1)}, bf16[16,16,1024]{2,1...) custom-call(f32[8,8,640]{2,1,0:T(8,128)S(1)} %maximum_bitcast_fusion, ...), custom_call_target="tpu_custom_call" | custom-call | tf_op jit(solution)/shard_map/start/pallas_call | solution.py:1035
  81.2 1.6 copy-done.4
  82.8 18.6 %attend.1 = (bf16[1024,256]{1,0:T(8,128)(2,1)S(1)}, f32[16,128]{1,0:T(8,128)S(1)}) custom-call(s32[16]{0:T(128)S(1)} %reshape.198.q_blocks, s32[64]{0:T(128)S(1)} %reshape.199.k_blocks, bf16[1024,256]{1,0:T(8,128)(2,1)S(1)} %bitcast.98, bf16[4096,256]{1,0:T(8,128)(2,1)S(1)} %bitcast.97), custom_call_target="tpu_custom_call" | custom-call | flops 4000000000 | bytes 4000000 | tf_op jit(solution)/shard_map/attend/pallas_call | solution.py:371
  101.5 141.1 %middle.1 = (bf16[128,1024]{1,0:T(8,128)(2,1)S(1)}, f32[128,1024]{1,0:T(8,128)S(1)}, f32[2,1024]{1,0:T(2,128)S(1)}, bf16[4,2,128,256]{3,2,1,0:T(8,128)(2,1)S(1)}...) custom-call(bf16[4,2,128,256]{3,2,1,0:T(8,128)(2,1)S(1)} %bitcast.92, ...), custom_call_target="tpu_custom_call" | custom-call | tf_op jit(solution)/shard_map/middle/pallas_call | solution.py:1384
  243.4 25.1 %attend_back.1 = (bf16[1024,256]{1,0:T(8,128)(2,1)S(1)}, bf16[4096,256]{1,0:T(8,128)(2,1)}) custom-call(s32[16]{0:T(128)S(1)} %reshape.198.q_blocks, s32[64]{0:T(128)S(1)} %reshape.199.k_blocks, bf16[1024,256]{1,0:T(8,128)(2,1)S(1)} %bitcast.99, bf16[4096,256]{1,0:T(8,128)(2,1)} %bitcast.96, bf16[1024,256]{1,0:T(8,128)(2,1)S(1)} %bitcast.100, ...), custom_call_target="tpu_custom_call" | custom-call | flops 10000000000 | bytes 8000000 | tf_op jit(solution)/shard_map/attend_back/pallas_call | solution.py:469
  269.3 41.2 %attention_grad_out.1 = (bf16[2,4,128,256]{3,2,1,0:T(8,128)(2,1)}, bf16[4,2,4,128,256]{4,3,2,1,0:T(8,128)(2,1)}) custom-call(bf16[4,2,128,256]{3,2,1,0:T(8,128)(2,1)} %bitcast.89, bf16[16,2,128,256]{3,2,1,0:T(8,128)(2,1)} %bitcast.107), custom_call_target="tpu_custom_call" | custom-call | tf_op jit(solution)/shard_map/attention_grad_out/pallas_call | solution.py:146
  310.5 2.0 convert_reduce_fusion
  314.7 1.9 copy.90
  317.6 1.1 bitcast_convert_fusion
  318.7 2.7 copy.87
  321.4 1.8 copy.97
  323.2 1.0 copy.96
  324.2 1.5 pad_maximum_fusion
  327.7 3.9 convolution_convert_fusion.1
  331.6 23.1 %grads_plane.1 = (bf16[16,16,1024]{2,1,0:T(8,128)(2,1)}, bf16[16,2,32,512]{3,2,1,0:T(8,128)(2,1)}, f32[16,8,128]{2,1,0:T(8,128)}) custom-call(bf16[16,16,1024]{2,1,0:T(8,128)(2,1)} %copy-done.1, bf16[2,16,32,512]{3,2,1,0:T(8,128)(2,1)} %bitcast.111, f32[16,8,128]{2,1,0:T(8,128)} %pad.26.refs_2_), custom_call_target="tpu_custom_call" | custom-call | tf_op jit(solution)/shard_map/grads_plane/pallas_call | solution.py:146
  354.7 1.2 convert_reduce_fusion.4
  355.9 4.7 %collective-permute-start = (f32[16,1024]{1,0:T(8,128)S(1)}, f32[16,1024]{1,0:T(8,128)S(1)}, u32[]{:S(2)}, u32[]{:S(2)}) collective-permute-start(f32[16,1024]{1,0:T(8,128)S(1)} %convert_reduce_fusion.4), channel_id=1, source_target_pairs={{0,0},{1,16},{2,32},{3,48},{16,1},{17,17},{18,33},{19,49},{32,2},{... | collective-permute-start | bytes 196616 | tf_op jit(solution)/shard_map/ppermute | solution.py:1462
  361.9 11.0 %grads_column.1 = f32[8,8,1408]{2,1,0:T(8,128)} custom-call(f32[8,8,1408]{2,1,0:T(8,128)} %fusion.1.refs_0_), custom_call_target="tpu_custom_call" | custom-call | tf_op jit(solution)/shard_map/grads_column/pallas_call | solution.py:146
  375.4 1.0 fusion.20
  376.5 1.3 convolution_convert_fusion
  377.8 17.4 %grad_token_column.1 = f32[128,1024]{1,0:T(8,128)S(1)} custom-call(bf16[8,128,1024]{2,1,0:T(8,128)(2,1)S(1)} %bitcast.86), custom_call_target="tpu_custom_call" | custom-call | tf_op jit(solution)/shard_map/grad_token_column/pallas_call | solution.py:283
  398.5 0.9 multiply_subtract_fusion
  (138 shorter events, 21.9 us)
Async XLA Ops:
  0.7 6.4 %copy-start = (bf16[1,128,1024]{2,1,0:T(8,128)(2,1)S(1)}, bf16[1,128,1024]{2,1,0:T(8,128)(2,1)}, u32[]{:S(2)}) copy-start(bf16[1,128,1024]{2,1,0:T(8,128)(2,1)} %param.22) | copy-start | bytes 786436
  82.8 18.6 %copy-start.3 = (bf16[1,128,1024]{2,1,0:T(8,128)(2,1)S(1)}, bf16[1,128,1024]{2,1,0:T(8,128)(2,1)}, u32[]{:S(2)}) copy-start(bf16[1,128,1024]{2,1,0:T(8,128)(2,1)} %param.23) | copy-start | bytes 786436
  318.7 4.5 %copy-start.5 = (f32[1024,128]{1,0:T(8,128)S(1)}, f32[1024,128]{1,0:T(8,128)}, u32[]{:S(2)}) copy-start(f32[1024,128]{1,0:T(8,128)} %slice.130) | copy-start | bytes 1572868
  331.6 29.0 %copy-start.6 = (bf16[16,2,32,768]{3,2,1,0:T(8,128)(2,1)S(1)}, bf16[16,2,32,768]{3,2,1,0:T(8,128)(2,1)}, u32[]{:S(2)}) copy-start(bf16[16,2,32,768]{3,2,1,0:T(8,128)(2,1)} %get-tuple-element.79) | copy-start | bytes 4718596
  354.7 6.2 %copy-start.7 = (bf16[16,2,32,512]{3,2,1,0:T(8,128)(2,1)S(1)}, bf16[16,2,32,512]{3,2,1,0:T(8,128)(2,1)}, u32[]{:S(2)}) copy-start(bf16[16,2,32,512]{3,2,1,0:T(8,128)(2,1)} %get-tuple-element.77) | copy-start | bytes 3145732
  355.9 5.1 %copy-start.26 = (f32[16,8,128]{2,1,0:T(8,128)S(1)}, f32[16,8,128]{2,1,0:T(8,128)}, u32[]{:S(2)}) copy-start(f32[16,8,128]{2,1,0:T(8,128)} %get-tuple-element.78) | copy-start | bytes 196612
  355.9 44.1 %collective-permute-start = (f32[16,1024]{1,0:T(8,128)S(1)}, f32[16,1024]{1,0:T(8,128)S(1)}, u32[]{:S(2)}, u32[]{:S(2)}) collective-permute-start(f32[16,1024]{1,0:T(8,128)S(1)} %convert_reduce_fusion.4), channel_id=1, source_target_pairs={{0,0},{1,16},{2,32},{3,48},{16,1},{17,17},{18,33},{19,49},{32,2},{... | collective-permute-start | bytes 196616 | tf_op jit(solution)/shard_map/ppermute | solution.py:1462
  360.9 15.4 %copy-start.9 = (bf16[16,48,512]{2,1,0:T(8,128)(2,1)S(1)}, bf16[16,48,512]{2,1,0:T(8,128)(2,1)}, u32[]{:S(2)}) copy-start(bf16[16,48,512]{2,1,0:T(8,128)(2,1)} %get-tuple-element.81) | copy-start | bytes 2359300
  361.1 15.4 %copy-start.16 = (bf16[1024,128]{0,1:T(8,128)(2,1)S(1)}, bf16[1024,128]{0,1:T(8,128)(2,1)}, u32[]{:S(2)}) copy-start(bf16[1024,128]{0,1:T(8,128)(2,1)} %copy.97) | copy-start | bytes 786436
  372.8 3.7 copy-start.33
  373.7 25.7 %copy-start.29 = (f32[18]{0:T(128)}, f32[18]{0:T(128)S(1)}, u32[]{:S(2)}) copy-start(f32[18]{0:T(128)S(1)} %slice_reduce_fusion) | copy-start | bytes 220
  374.6 21.7 %copy-start.14 = (f32[8,8,256]{2,0,1:T(8,128)}, f32[8,8,256]{2,0,1:T(8,128)S(1)}, u32[]{:S(2)}) copy-start(f32[8,8,256]{2,0,1:T(8,128)S(1)} %slice.132) | copy-start | bytes 196612
  377.8 18.4 %copy-start.12 = (f32[8,2048]{1,0:T(8,128)S(1)}, f32[8,2048]{1,0:T(8,128)}, u32[]{:S(2)}) copy-start(f32[8,2048]{1,0:T(8,128)} %param.26) | copy-start | bytes 196612
  377.8 18.4 %copy-start.22 = (f32[8,2048]{1,0:T(8,128)S(1)}, f32[8,2048]{1,0:T(8,128)}, u32[]{:S(2)}) copy-start(f32[8,2048]{1,0:T(8,128)} %param.32) | copy-start | bytes 196612
  377.8 18.4 %copy-start.23 = (f32[8,2048]{1,0:T(8,128)S(1)}, f32[8,2048]{1,0:T(8,128)}, u32[]{:S(2)}) copy-start(f32[8,2048]{1,0:T(8,128)} %param.38) | copy-start | bytes 196612
  395.3 3.2 copy-start.8
  395.4 3.2 copy-start.18
  395.4 3.1 copy-start.19
  396.3 3.2 copy-start.30
  396.3 3.2 copy-start.31
  396.3 3.2 copy-start.32
  396.3 3.7 copy-start.13
  396.3 3.7 copy-start.24
  396.3 3.7 copy-start.25
  (11 other events, 18.1 us)

commit v3 on v2

--- a/solution.py
+++ b/solution.py
@@ -71,227 +71,8 @@
     return to
 
 
-def push_kernel(channels, n_in, n_out, *refs):
-    ins, outs = refs[:n_in], refs[n_in : n_in + n_out]
-    sems = refs[n_in + n_out :]
-    me = where_am_i()
-    barrier = pltpu.get_barrier_semaphore()
-    greeted = max((c[2] for c in channels), key=len)
-    peers = math.prod(SIZE[a] for a in greeted)
-
-    def greet(k, carry):
-        pl.semaphore_signal(
-            barrier, inc=1, device_id=address(shifted(me, greeted, k, 1)), device_id_type=MESH
-        )
-        return carry
-
-    lax.fori_loop(1, peers, greet, 0)
-    own = []
-    for i, (src, dst, axes, take, put) in enumerate(channels):
-        copy = pltpu.make_async_copy(take(ins[src], me), put(outs[dst], me), sems[3 * i + 2])
-        copy.start()
-        own.append(copy)
-    pl.semaphore_wait(barrier, peers - 1)
-    for i, (src, dst, axes, take, put) in enumerate(channels):
-        n = math.prod(SIZE[a] for a in axes)
-        mix = {4: 1, 8: 3, 16: 7}[n]
-
-        def begin(j, carry):
-            k = lax.rem(j * mix, n)
-            to = shifted(me, axes, k, 1)
-            pltpu.make_async_remote_copy(
-                src_ref=take(ins[src], to),
-                dst_ref=put(outs[dst], me),
-                send_sem=sems[3 * i].at[k],
-                recv_sem=sems[3 * i + 1].at[k],
-                device_id=address(to),
-                device_id_type=MESH,
-            ).start()
-            return carry
-
-        lax.fori_loop(1, n, begin, 0)
-    for copy in own:
-        copy.wait()
-    for i, (src, dst, axes, take, put) in enumerate(channels):
-        n = math.prod(SIZE[a] for a in axes)
-        mix = {4: 1, 8: 3, 16: 7}[n]
-
-        def finish(j, carry):
-            k = lax.rem(j * mix, n)
-            to, back = shifted(me, axes, k, 1), shifted(me, axes, k, -1)
-            copy = pltpu.make_async_remote_copy(
-                src_ref=take(ins[src], to),
-                dst_ref=put(outs[dst], back),
-                send_sem=sems[3 * i].at[k],
-                recv_sem=sems[3 * i + 1].at[k],
-                device_id=address(to),
-                device_id_type=MESH,
-            )
-            copy.wait_send()
-            copy.wait_recv()
-            return carry
-
-        lax.fori_loop(1, n, finish, 0)
-
-
-def push(name, number, arrays, out_shapes, channels):
-    scratch = []
-    for _, _, axes, _, _ in channels:
-        n = math.prod(SIZE[a] for a in axes)
-        scratch += [
-            pltpu.SemaphoreType.DMA((n,)),
-            pltpu.SemaphoreType.DMA((n,)),
-            pltpu.SemaphoreType.DMA,
-        ]
-    return pl.pallas_call(
-        functools.partial(push_kernel, channels, len(arrays), len(out_shapes)),
-        out_shape=tuple(jax.ShapeDtypeStruct(s, t) for s, t in out_shapes),
-        in_specs=[pl.BlockSpec(memory_space=pl.ANY)] * len(arrays),
-        out_specs=tuple([pl.BlockSpec(memory_space=pl.ANY)] * len(out_shapes)),
-        scratch_shapes=scratch,
-        compiler_params=pltpu.CompilerParams(collective_id=number, has_side_effects=True),
-        name=name,
-    )(*arrays)
-
-
 def column_place(me, z, core):
     return dict(me, zh=lax.div(z, 2), zl=lax.rem(z, 2), co=core)
-
-
-def greet_column(me, z, core):
-    barrier = pltpu.get_barrier_semaphore()
-    for off in (1, 2, 3):
-        to = column_place(me, lax.rem(z + off, 4), core)
-        pl.semaphore_signal(barrier, inc=1, device_id=address(to), device_id_type=MESH)
-    sibling = column_place(me, z, 1 - core)
-    pl.semaphore_signal(barrier, inc=1, device_id=address(sibling), device_id_type=MESH)
-    pl.semaphore_wait(barrier, 4)
-
-
-def gather_kernel(x_ref, out_ref, far_send, far_recv, near_send, near_recv, own_sem):
-    me = where_am_i()
-    z, core = me["zh"] * 2 + me["zl"], me["co"]
-    sibling = address(column_place(me, z, 1 - core))
-    own = pltpu.make_async_copy(x_ref, out_ref.at[z * 2 + core], own_sem)
-    own.start()
-    greet_column(me, z, core)
-
-    def far(off):
-        return pltpu.make_async_remote_copy(
-            src_ref=x_ref,
-            dst_ref=out_ref.at[z * 2 + core],
-            send_sem=far_send.at[off],
-            recv_sem=far_recv.at[off],
-            device_id=address(column_place(me, lax.rem(z + off, 4), core)),
-            device_id_type=MESH,
-        )
-
-    def near(off, core_of):
-        slot = lax.rem(z + 4 - off, 4) * 2 + core_of
-        return pltpu.make_async_remote_copy(
-            src_ref=x_ref if off == 0 else out_ref.at[slot],
-            dst_ref=out_ref.at[slot],
-            send_sem=near_send.at[off],
-            recv_sem=near_recv.at[off],
-            device_id=sibling,
-            device_id_type=MESH,
-        )
-
-    for off in (1, 3, 2):
-        far(off).start()
-    near(0, core).start()
-    for off in (1, 3, 2):
-        slot = lax.rem(z + 4 - off, 4) * 2 + core
-        pltpu.make_async_remote_copy(
-            src_ref=x_ref,
-            dst_ref=out_ref.at[slot],
-            send_sem=far_send.at[off],
-            recv_sem=far_recv.at[off],
-            device_id=address(column_place(me, lax.rem(z + off, 4), core)),
-            device_id_type=MESH,
-        ).wait_recv()
-        near(off, core).start()
-    own.wait()
-    for off in (1, 3, 2):
-        far(off).wait_send()
-    for off in (0, 1, 3, 2):
-        near(off, core).wait_send()
-        near(off, 1 - core).wait_recv()
-
-
-def gather_column(name, number, x):
-    return pl.pallas_call(
-        gather_kernel,
-        out_shape=jax.ShapeDtypeStruct((RANKS,) + x.shape, x.dtype),
-        in_specs=[pl.BlockSpec(memory_space=pl.ANY)],
-        out_specs=pl.BlockSpec(memory_space=pl.ANY),
-        scratch_shapes=[pltpu.SemaphoreType.DMA((4,))] * 4 + [pltpu.SemaphoreType.DMA],
-        compiler_params=pltpu.CompilerParams(collective_id=number, has_side_effects=True),
-        name=name,
-    )(x)
-
-
-def sum_kernel(
-    part_ref, out_ref, paired, sending, landed, near_send, near_recv, far_send, far_recv
-):
-    me = where_am_i()
-    z, core = me["zh"] * 2 + me["zl"], me["co"]
-    sibling = address(column_place(me, z, 1 - core))
-    greet_column(me, z, core)
-
-    def near(off):
-        to_z = lax.rem(z + off, 4)
-        return pltpu.make_async_remote_copy(
-            src_ref=part_ref.at[to_z * 2 + (1 - core)],
-            dst_ref=paired.at[off],
-            send_sem=near_send.at[off],
-            recv_sem=near_recv.at[off],
-            device_id=sibling,
-            device_id_type=MESH,
-        )
-
-    def far(off):
-        return pltpu.make_async_remote_copy(
-            src_ref=sending.at[off],
-            dst_ref=landed.at[off],
-            send_sem=far_send.at[off],
-            recv_sem=far_recv.at[off],
-            device_id=address(column_place(me, lax.rem(z + off, 4), core)),
-            device_id_type=MESH,
-        )
-
-    for off in (2, 1, 3, 0):
-        near(off).start()
-    for off in (2, 1, 3):
-        near(off).wait_recv()
-        mine = part_ref[lax.rem(z + off, 4) * 2 + core].astype(F32)
-        sending[off] = (mine + paired[off].astype(F32)).astype(BF16)
-        far(off).start()
-    near(0).wait_recv()
-    out_ref[...] = part_ref[z * 2 + core].astype(F32) + paired[0].astype(F32)
-    for off in (1, 3, 2):
-        far(off).wait_recv()
-        out_ref[...] += landed[off].astype(F32)
-    for off in (2, 1, 3):
-        near(off).wait_send()
-        far(off).wait_send()
-    near(0).wait_send()
-
-
-def sum_column(name, number, parts):
-    block = parts.shape[1:]
-    return pl.pallas_call(
-        sum_kernel,
-        out_shape=jax.ShapeDtypeStruct(block, F32),
-        in_specs=[pl.BlockSpec(memory_space=pltpu.VMEM)],
-        out_specs=pl.BlockSpec(memory_space=pltpu.VMEM),
-        scratch_shapes=[pltpu.VMEM((4,) + block, BF16)] * 3
-        + [pltpu.SemaphoreType.DMA((4,))] * 4,
-        compiler_params=pltpu.CompilerParams(
-            collective_id=number, has_side_effects=True, vmem_limit_bytes=VMEM_LIMIT
-        ),
-        name=name,
-    )(parts)
 
 
 def dot_nn(a, b):
@@ -850,7 +631,7 @@
     own_b = pltpu.make_async_copy(sent_b.at[rank], shares_b.at[rank], own_sems.at[1])
     own_a.start()
     own_b.start()
-    greet_all(me, "all", "both")
+    greet_all(me, "all", "use")
     to_a.begin()
     gathers.begin(0, tokens[...])
     rows.begin()
@@ -1425,23 +1206,321 @@
     )(out_mine, wo, gateup_low, down_rows, inputs, upstream, gains)
 
 
-def rms_norm(values, norm_gain):
-    factor = lax.rsqrt(jnp.mean(values * values, axis=-1, keepdims=True) + NORM_EPS)
-    return values * factor * norm_gain
-
-
-def head_prepare(projected, norm_gain, cosine, sine_part):
-    normed = rms_norm(projected, norm_gain)
-    halfway = HD // 2
-    leading, trailing = normed[..., :halfway], normed[..., halfway:]
-    return jnp.concatenate(
-        [leading * cosine - trailing * sine_part, trailing * cosine + leading * sine_part], axis=-1
-    )
-
-
-def swiglu(gate_up):
-    half = gate_up.shape[-1] // 2
-    return jax.nn.silu(gate_up[:, :half]) * gate_up[:, half:]
+def end_kernel(
+    dq_mine,
+    dkv_mine,
+    projected,
+    cosine,
+    sine,
+    head_gains,
+    all_tokens,
+    qkv_part,
+    output_lines,
+    gateup_parts,
+    grad_hidden,
+    gains_grad,
+    token_grad,
+    summed_a,
+    summed_b,
+    output_parts,
+    gains_sum,
+    own_kv,
+    stage,
+    passing,
+    dq_all,
+    dkv_all,
+    grad_qkv,
+    part,
+    paired,
+    sending,
+    landed,
+    qkv_lines,
+    qkv_parts,
+    column_a,
+    column_b,
+    gains_column,
+    gains_plane,
+    stage_send,
+    stage_recv,
+    kv_send,
+    kv_recv,
+    dq_send,
+    dq_recv,
+    near_send,
+    near_recv,
+    far_send,
+    far_recv,
+    plane_send,
+    plane_recv,
+    gplane_send,
+    gplane_recv,
+    row_send,
+    row_recv,
+    a_send,
+    a_recv,
+    b_send,
+    b_recv,
+    gcolumn_send,
+    gcolumn_recv,
+    own_sems,
+):
+    me = where_am_i()
+    x, y, z = me["x"], me["y"], me["zh"] * 2 + me["zl"]
+    rank, here = flat_index(me, COLUMN), flat_index(me, SURFACE)
+    sums = ColumnSums(
+        me, part, paired, sending, landed, near_send, near_recv, far_send, far_recv
+    )
+
+    def by_column(ref, out, send, recv):
+        return Exchange(
+            me,
+            COLUMN,
+            lambda to: ref.at[flat_index(to, COLUMN)],
+            lambda frm: out.at[flat_index(frm, COLUMN)],
+            send,
+            recv,
+        )
+
+    to_a = by_column(column_a, summed_a, a_send, a_recv)
+    to_b = by_column(column_b, summed_b, b_send, b_recv)
+    gains_in = Exchange(
+        me,
+        COLUMN,
+        lambda to: gains_column.at[rank],
+        lambda frm: gains_column.at[flat_index(frm, COLUMN)],
+        gcolumn_send,
+        gcolumn_recv,
+    )
+    gains_over = Exchange(
+        me,
+        SURFACE,
+        lambda to: gains_plane.at[here],
+        lambda frm: gains_plane.at[flat_index(frm, SURFACE)],
+        gplane_send,
+        gplane_recv,
+    )
+    plane = Exchange(
+        me,
+        SURFACE,
+        lambda to: qkv_lines.at[:, flat_index(to, SURFACE)],
+        lambda frm: qkv_parts.at[flat_index(frm, SURFACE)],
+        plane_send,
+        plane_recv,
+    )
+    queries = Exchange(
+        me,
+        ("x",),
+        lambda to: dq_mine.at[to["x"]],
+        lambda frm: dq_all.at[:, frm["x"]],
+        dq_send,
+        dq_recv,
+    )
+    rows = RowCopies(me, output_lines, output_parts, row_send, row_recv, True)
+    own_dq = pltpu.make_async_copy(dq_mine.at[x], dq_all.at[:, x], own_sems.at[4])
+    own_plane = pltpu.make_async_copy(qkv_lines.at[:, here], qkv_parts.at[here], own_sems.at[5])
+    own_a = pltpu.make_async_copy(column_a.at[rank], summed_a.at[rank], own_sems.at[6])
+    own_b = pltpu.make_async_copy(column_b.at[rank], summed_b.at[rank], own_sems.at[7])
+
+    def own_copy(j):
+        to_x = lax.rem(x + j, 4)
+        return pltpu.make_async_copy(dkv_mine.at[to_x * 4 + y], own_kv.at[j], own_sems.at[j])
+
+    def stage_copy(j, k):
+        to_x, to_y = lax.rem(x + j, 4), lax.rem(y + k, 4)
+        return pltpu.make_async_remote_copy(
+            src_ref=dkv_mine.at[to_x * 4 + to_y],
+            dst_ref=stage.at[k, j],
+            send_sem=stage_send.at[k, j],
+            recv_sem=stage_recv.at[k, j],
+            device_id=address(dict(me, y=to_y)),
+            device_id_type=MESH,
+        )
+
+    def kv_copy(j, arriving):
+        frm_x = lax.rem(x + 4 - j, 4) if arriving else x
+        return pltpu.make_async_remote_copy(
+            src_ref=passing.at[j],
+            dst_ref=dkv_all.at[:, frm_x],
+            send_sem=kv_send.at[j],
+            recv_sem=kv_recv.at[j],
+            device_id=address(dict(me, x=lax.rem(x + j, 4))),
+            device_id_type=MESH,
+        )
+
+    own_dq.start()
+    for j in (2, 1, 3, 0):
+        own_copy(j).start()
+    greet_all(me, "all", "own")
+    for j in (2, 1, 3, 0):
+        for k in (1, 3, 2):
+            stage_copy(j, k).start()
+    queries.begin()
+    rows.begin()
+
+    for row_zh in range(2):
+
+        def add_part(s, total):
+            return total + gateup_parts[s, row_zh].astype(F32)
+
+        total = lax.fori_loop(0, PLANE, add_part, jnp.zeros((32, 768), F32))
+        column_b[pl.ds(row_zh * 4, 4)] = total.reshape(4, 8, 768)
+    own_b.start()
+    to_b.begin()
+
+    for j in (2, 1, 3, 0):
+        own_copy(j).wait()
+        total = own_kv[j].astype(F32)
+        for k in (1, 3, 2):
+            stage_copy(j, k).wait_recv()
+            total = total + stage[k, j].astype(F32)
+        if j:
+            passing[j] = total.astype(BF16)
+            kv_copy(j, False).start()
+        else:
+            dkv_all[:, x] = total.astype(BF16)
+    own_dq.wait()
+    queries.arrive()
+    for j in (2, 1, 3):
+        kv_copy(j, True).wait_recv()
+
+    def project_back(i, carry):
+        gain_q, gain_k = carry
+        back = 3 - i
+        off = back + lax.div(back, 2) * (5 - 2 * back)
+        to_z = lax.rem(z + off, 4)
+        at = pl.ds(pl.multiple_of(to_z * 2 * ROWS, 2 * ROWS), 2 * ROWS)
+        row_zh, first = lax.div(to_z, 2), lax.rem(to_z, 2) * 2
+        grad_q = dq_all[row_zh, pl.ds(first, 2)].reshape(2 * ROWS, 256).astype(F32)
+        grad_kv = dkv_all[row_zh, pl.ds(first, 2)].reshape(2 * ROWS, 256)
+        for head in range(3):
+            if head == 2:
+                grad, gain = grad_kv[:, :HD].astype(F32), head_gains[1:2, :]
+            else:
+                grad, gain = grad_q[:, head * HD : (head + 1) * HD], head_gains[0:1, :]
+            turned = grad * cosine[at, :] - pltpu.roll(grad, HD // 2, 1) * sine[at, :]
+            grad_in, grad_gain = norm_back(
+                projected[at, head * HD : (head + 1) * HD], gain, turned
+            )
+            grad_qkv[at, head * HD : (head + 1) * HD] = grad_in.astype(BF16)
+            if head == 2:
+                gain_k = gain_k + grad_gain
+            else:
+                gain_q = gain_q + grad_gain
+        grad_qkv[at, 384:] = grad_kv[:, HD:]
+        sums.put(0, off, dot_nt(grad_qkv[at, :], qkv_part[...]))
+
+        @pl.when(i >= 1)
+        def _():
+            last = back + 1
+            sums.pass_on(0, last + lax.div(last, 2) * (5 - 2 * last))
+
+        return gain_q, gain_k
+
+    nothing = jnp.zeros((1, HD), F32)
+    gain_q, gain_k = lax.fori_loop(0, 4, project_back, (nothing, nothing))
+
+    for j in range(16):
+        gains_column[rank, j : j + 1, :] = gains_grad[
+            j // 8 : j // 8 + 1, j % 8 * HD : (j % 8 + 1) * HD
+        ]
+    gains_column[rank, 16:17, :] = gain_q
+    gains_column[rank, 17:18, :] = gain_k
+    gains_column[rank, 18:24, :] = jnp.zeros((6, HD), F32)
+    gains_in.begin()
+
+    def qkv_rows(j, carry):
+        cols = pl.ds(pl.multiple_of(j * 256, 256), 256)
+        grads = dot_tn(all_tokens[:, :, cols].reshape(RANKS * ROWS, 256), grad_qkv[...])
+        qkv_lines[lax.div(j, 2), pl.ds(lax.rem(j, 2) * 8, 8)] = grads.astype(BF16).reshape(
+            8, 32, 512
+        )
+        return carry
+
+    lax.fori_loop(0, 4, qkv_rows, 0)
+    own_plane.start()
+    plane.begin()
+
+    gains_in.arrive()
+    gains_plane[here] = jnp.sum(gains_column[...], axis=0)
+    gains_over.begin()
+    token_grad[...] = grad_hidden[...] + sums.total(0)
+
+    own_plane.wait()
+    plane.arrive()
+    for row_zh in range(2):
+
+        def add_qkv(s, total):
+            return total + qkv_parts[s, row_zh].astype(F32)
+
+        total = lax.fori_loop(0, PLANE, add_qkv, jnp.zeros((32, 512), F32))
+        column_a[pl.ds(row_zh * 4, 4)] = total.reshape(4, 8, 512)
+    own_a.start()
+    to_a.begin()
+    gains_over.arrive()
+    gains_sum[...] = jnp.sum(gains_plane[...], axis=0)
+    to_b.arrive()
+    rows.arrive()
+    own_b.wait()
+    for j in (2, 1, 3, 0):
+        for k in (1, 3, 2):
+            stage_copy(j, k).wait_send()
+        if j:
+            kv_copy(j, False).wait_send()
+    sums.drain(0)
+    for exchange in (queries, rows, to_b, gains_in, gains_over, plane):
+        exchange.drain()
+    own_a.wait()
+    to_a.arrive()
+    to_a.drain()
+
+
+def end(number, *arrays):
+    anywhere = pl.BlockSpec(memory_space=pl.ANY)
+    vmem = pl.BlockSpec(memory_space=pltpu.VMEM)
+    dma = pltpu.SemaphoreType.DMA
+    struct = jax.ShapeDtypeStruct
+    block = (ROWS, D)
+    quarter_rows = (2, ROWS, 256)
+    return pl.pallas_call(
+        end_kernel,
+        out_shape=(
+            struct(block, F32),
+            struct((RANKS, 8, 512), F32),
+            struct((RANKS, 8, 768), F32),
+            struct((PLANE, 16, D), BF16),
+            struct((24, HD), F32),
+        ),
+        in_specs=[anywhere, anywhere] + [vmem] * 6 + [anywhere] + [vmem] * 3,
+        out_specs=(vmem, anywhere, anywhere, anywhere, vmem),
+        scratch_shapes=[
+            pltpu.VMEM((4,) + quarter_rows, BF16),
+            pltpu.VMEM((4, 4) + quarter_rows, BF16),
+            pltpu.VMEM((4,) + quarter_rows, BF16),
+            pltpu.VMEM((2, 4, ROWS, 256), BF16),
+            pltpu.VMEM((2, 4, ROWS, 256), BF16),
+            pltpu.VMEM((RANKS * ROWS, 512), BF16),
+            pltpu.VMEM((1, 4, 2) + block, BF16),
+            pltpu.VMEM((1, 4) + block, BF16),
+            pltpu.VMEM((1, 4) + block, BF16),
+            pltpu.VMEM((1, 4) + block, BF16),
+            pltpu.VMEM((2, PLANE, 32, 512), BF16),
+            pltpu.VMEM((PLANE, 2, 32, 512), BF16),
+            pltpu.VMEM((RANKS, 8, 512), F32),
+            pltpu.VMEM((RANKS, 8, 768), F32),
+            pltpu.VMEM((RANKS, 24, HD), F32),
+            pltpu.VMEM((PLANE, 24, HD), F32),
+        ]
+        + [dma((4, 4))] * 2
+        + [dma((4,))] * 4
+        + [dma((1, 4))] * 4
+        + [dma((PLANE,))] * 6
+        + [dma((RANKS,))] * 6
+        + [dma((8,))],
+        compiler_params=pltpu.CompilerParams(
+            collective_id=number, has_side_effects=True, vmem_limit_bytes=VMEM_LIMIT
+        ),
+        name="end",
+    )(*arrays)
 
 
 def adam_update(weight, gradient, mean_old, square_old, rate, decay):
@@ -1455,11 +1534,6 @@
 
 def by_rank(array, width):
     return array.reshape(array.shape[0], RANKS, width)
-
-
-def swap_owner(array):
-    pairs = [(a * 4 + b, b * 4 + a) for a in range(4) for b in range(4)]
-    return lax.ppermute(array, ("x", "zl", "co"), pairs)
 
 
 def body(
@@ -1534,7 +1608,6 @@
         output_weight.astype(BF16),
         jnp.concatenate([frequency, frequency])[None],
     )
-    all_tokens = all_tokens.reshape(RANKS * ROWS, D)
     gains_all = gains_low.reshape(-1, 8, HD)[:, 0, :18].reshape(-1).astype(F32)
     attn_gain = gains_all[:D]
     ffn_gain = gains_all[D : 2 * D]
@@ -1556,7 +1629,7 @@
         return ref.at[:, frm["x"]]
 
     result, grad_hidden, gains_grad, grad_mine, gateup_parts, down_parts, output_lines = middle(
-        5,
+        2,
         out_mine.reshape(4, 2, ROWS, 256),
         output_wide.reshape(256, D),
         gateup_low,
@@ -1568,114 +1641,34 @@
     dq_mine, dkv_mine = attend_back(
         query_blocks, key_blocks, q_mine, kv_mine, grad_mine.reshape(1024, 256), out_mine, lse
     )
-    dq, dkv_parts = push(
-        "attention_grad_out",
-        13,
-        [dq_mine.reshape(4, 2, ROWS, 256), dkv_mine.reshape(PLANE, 2, ROWS, 256)],
-        [((2, 4, ROWS, 256), BF16), ((4, 2, 4, ROWS, 256), BF16)],
-        [
-            (
-                1,
-                1,
-                SURFACE,
-                lambda ref, to: ref.at[flat_index(to, SURFACE)],
-                lambda ref, frm: ref.at[frm["y"], :, frm["x"]],
-            ),
-            (0, 0, ("x",), to_x, from_pack_x),
-        ],
-    )
-    dkv = jnp.sum(dkv_parts.astype(F32), axis=0).reshape(RANKS * ROWS, 256)
-    half = HD // 2
-    prepare = functools.partial(
-        head_prepare, cosine=cosine[:, None, :half], sine_part=sine[:, None, half:]
-    )
-    three = jnp.stack([head_gains[0], head_gains[0], head_gains[1]])
-    heads_use, heads_pull = jax.vjp(prepare, projected.reshape(-1, 3, HD), three)
-    grad_heads = jnp.concatenate([dq.reshape(RANKS * ROWS, 256).astype(F32), dkv[:, :HD]], axis=1)
-    grad_heads_in, grad_head_gains = heads_pull(grad_heads.reshape(-1, 3, HD))
-    grad_qkv = jnp.concatenate(
-        [grad_heads_in.reshape(-1, 384).astype(BF16), dkv[:, HD:].astype(BF16)], axis=1
-    )
-    qkv_grad = dot_tn(all_tokens, grad_qkv)
-    token_grad = grad_hidden + sum_column(
-        "grad_token_column",
-        14,
-        dot_nt(grad_qkv, qkv_part).astype(BF16).reshape(RANKS, ROWS, D),
-    )
-
-    gains_grad = jnp.concatenate(
-        [
-            gains_grad[0],
-            gains_grad[1],
-            grad_head_gains[0] + grad_head_gains[1],
-            grad_head_gains[2],
-        ]
-    )
-    gains_lines = jnp.pad(
-        gains_grad.reshape(2, PLANE, 4, 18).transpose(1, 0, 2, 3).reshape(PLANE, RANKS, 18),
-        ((0, 0), (0, 0), (0, HD - 18)),
-    )
-
-    def to_surface_inner(ref, to):
-        return ref.at[:, flat_index(to, SURFACE)]
-
-    def to_surface(ref, to):
-        return ref.at[flat_index(to, SURFACE)]
-
-    def to_surface_swapped(ref, to):
-        return ref.at[flat_index(to, ("y", "x"))]
-
-    qkv_lines = qkv_grad.astype(BF16).reshape(2, PLANE, 32, 512)
-    output_parts, qkv_parts, gains_parts = push(
-        "grads_plane",
-        15,
-        [output_lines, qkv_lines, gains_lines],
-        [
-            ((PLANE, 16, D), BF16),
-            ((PLANE, 2, 32, 512), BF16),
-            ((PLANE, RANKS, HD), F32),
-        ],
-        [
-            (0, 0, SURFACE, to_surface_swapped, to_surface),
-            (1, 1, SURFACE, to_surface_inner, to_surface),
-            (2, 2, SURFACE, to_surface, to_surface),
-        ],
-    )
+    token_grad, summed_a, summed_b, output_parts, gains_total = end(
+        3,
+        dq_mine.reshape(4, 2, ROWS, 256),
+        dkv_mine.reshape(PLANE, 2, ROWS, 256),
+        projected,
+        cosine,
+        sine,
+        head_gains,
+        all_tokens,
+        qkv_part,
+        output_lines,
+        gateup_parts,
+        grad_hidden,
+        gains_grad,
+    )
+    gains_sum = lax.dynamic_slice_in_dim(
+        gains_total.reshape(-1), lax.axis_index(AXES) * norm_gains.shape[0], norm_gains.shape[0]
+    )
+    output_sum = jnp.sum(output_parts.astype(F32), axis=0)
     down_wide = jnp.sum(down_parts.astype(F32), axis=0)
-    output_sum = swap_owner(jnp.sum(output_parts.astype(F32), axis=0))
     down_sum = jnp.concatenate([down_wide[:24], down_wide[24:]], axis=1)
-    gains_sums = jnp.sum(gains_parts, axis=0).reshape(RANKS, 1, HD)
-    column_sums = jnp.concatenate(
-        [
-            jnp.sum(qkv_parts.astype(F32), axis=0).reshape(RANKS, 8, 512),
-            jnp.pad(gains_sums, ((0, 0), (0, 7), (0, 0))),
-            jnp.sum(gateup_parts.astype(F32), axis=0).reshape(RANKS, 8, 768),
-        ],
-        axis=2,
-    )
-    (summed,) = push(
-        "grads_column",
-        16,
-        [column_sums],
-        [((RANKS, 8, 1408), F32)],
-        [
-            (
-                0,
-                0,
-                COLUMN,
-                lambda ref, to: ref.at[flat_index(to, COLUMN)],
-                lambda ref, frm: ref.at[flat_index(frm, COLUMN)],
-            )
-        ],
-    )
-    gains_sum = jnp.sum(summed[:, 0, 512 : 512 + 18], axis=0)
-    wide = summed.transpose(1, 0, 2)
-    query_sum = wide[:, :, :256].reshape(8, 2048)
+    wide_a, wide_b = summed_a.transpose(1, 0, 2), summed_b.transpose(1, 0, 2)
+    query_sum = wide_a[:, :, :256].reshape(8, 2048)
     keyval_sum = jnp.concatenate(
-        [wide[:, :, 256:384].reshape(8, KV), wide[:, :, 384:512].reshape(8, KV)], axis=1
+        [wide_a[:, :, 256:384].reshape(8, KV), wide_a[:, :, 384:].reshape(8, KV)], axis=1
     )
     gateup_sum = jnp.concatenate(
-        [wide[:, :, 640:1024].reshape(8, FF), wide[:, :, 1024:].reshape(8, FF)], axis=1
+        [wide_b[:, :, :384].reshape(8, FF), wide_b[:, :, 384:].reshape(8, FF)], axis=1
     )
 
     query_new, query_mean_new, query_square_new = adam_update(

time: 405 us -> 359 us (0.89); the launches traced: 402 us -> 360 us
  local copies, waits for them, and re-layouts: 22.2 us -> 8.01 us
  Pallas kernels: 350 us -> 341 us
  other arithmetic: 18.1 us -> 10.4 us
  matrix products: 5.23 us -> 0 us
  starting transfers between devices: 4.72 us -> 0 us
    pallas_call x4 -> x1, Pallas kernels: 92.6 us -> 77.2 us  [end(): pl.pallas_call(end_kernel, out_shape=(struct(block, F32), struct((RANKS,...]
    dot_general x2 -> x0, matrix products: 5.23 us -> none  [the longest x1 3.93 us: dot_tn(): lax.dot_general(a, b, (((0,), (0,)), ((), ())), preferred_element_type=F32)]
    reduce_sum x8 -> x1, other arithmetic: 5.16 us -> 0.08 us  [body(): output_sum = jnp.sum(output_parts.astype(F32), axis=0)]
    ppermute x1 -> x0, starting transfers between devices: 4.72 us -> none  [swap_owner(): return lax.ppermute(array, ('x', 'zl', 'co'), pairs)]
    unnamed x73 -> x45, local copies, waits for them, and re-layouts: 8.35 us -> 4.21 us
  transfers between devices with their start and end apart: 1 -> 0, of which waited for: 0 -> 0; matrix products, arithmetic and copies ran while one was open for 3% -> 0% of each run, Pallas kernels for 7% -> 0%
where the time goes in v3:
time: 359 us; the launch traced here: 360 us
  Pallas kernels  341 us (95%)
  other arithmetic  10.4 us (3%)
  local copies, waits for them, and re-layouts  8.01 us (2%)
    pallas_call x1, Pallas kernels, middle(): pl.pallas_call(middle_kernel, out_shape=(jax.ShapeDtypeStruct(block, BF16...  142 us
    pallas_call x1, Pallas kernels, end(): pl.pallas_call(end_kernel, out_shape=(struct(block, F32), struct((RANKS,...  77.2 us
    pallas_call x1, Pallas kernels, start(): pl.pallas_call(start_kernel, out_shape=(struct((4, 2, ROWS, 256), BF16),...  73.2 us
    pallas_call x1, Pallas kernels, attend_back(): pl.pallas_call(attend_back_kernel, out_shape=(jax.ShapeDtypeStruct(q.shap...  27.6 us
    pallas_call x1, Pallas kernels, attend(): pl.pallas_call(attend_kernel, out_shape=(jax.ShapeDtypeStruct(q.shape, BF...  20.9 us

profile of v3, /device:TPU:1, one launch (start us, length us, event | category | flops | bytes accessed | tf_op | source)
XLA Modules:
  0.0 360.2 jit_solution(11749356372823028543)
XLA Ops:
  0.7 0.8 add_reduce_fusion
  1.8 0.7 pad_bitcast_fusion
  2.6 0.8 slice_bitcast_fusion.3
  3.4 0.9 maximum_bitcast_fusion.1.sent_a
  4.3 1.0 fusion.15
  5.2 0.8 convert_element_type.35.output_rows
  6.2 1.0 copy-done
  7.1 73.2 %start.1 = (bf16[4,2,128,256]{3,2,1,0:T(8,128)(2,1)S(1)}, bf16[16,2,128,256]{3,2,1,0:T(8,128)(2,1)}, bf16[8,128,1024]{2,1,0:T(8,128)(2,1)}, bf16[16,16,1024]{2,1...) custom-call(f32[8,8,640]{2,1,0:T(8,128)S(1)} %maximum_bitcast_fusion, ...), custom_call_target="tpu_custom_call" | custom-call | tf_op jit(solution)/shard_map/start/pallas_call | solution.py:816
  80.8 0.2 copy.64
  81.3 1.6 copy-done.3
  82.9 20.9 %attend.1 = (bf16[1024,256]{1,0:T(8,128)(2,1)S(1)}, f32[16,128]{1,0:T(8,128)S(1)}) custom-call(s32[16]{0:T(128)S(1)} %reshape.135.q_blocks, s32[64]{0:T(128)S(1)} %reshape.136.k_blocks, bf16[1024,256]{1,0:T(8,128)(2,1)S(1)} %bitcast.75, bf16[4096,256]{1,0:T(8,128)(2,1)S(1)} %bitcast.74), custom_call_target="tpu_custom_call" | custom-call | flops 4000000000 | bytes 4000000 | tf_op jit(solution)/shard_map/attend/pallas_call | solution.py:152
  104.0 0.9 convert.7
  105.0 141.8 %middle.1 = (bf16[128,1024]{1,0:T(8,128)(2,1)S(1)}, f32[128,1024]{1,0:T(8,128)S(1)}, f32[2,1024]{1,0:T(2,128)S(1)}, bf16[4,2,128,256]{3,2,1,0:T(8,128)(2,1)S(1)}...) custom-call(bf16[4,2,128,256]{3,2,1,0:T(8,128)(2,1)S(1)} %bitcast.65, ...), custom_call_target="tpu_custom_call" | custom-call | tf_op jit(solution)/shard_map/middle/pallas_call | solution.py:1165
  246.8 1.3 convert_reduce_fusion
  248.1 1.8 multiply_subtract_fusion.1
  249.8 27.6 %attend_back.1 = (bf16[1024,256]{1,0:T(8,128)(2,1)S(1)}, bf16[4096,256]{1,0:T(8,128)(2,1)}) custom-call(s32[16]{0:T(128)S(1)} %reshape.135.q_blocks, s32[64]{0:T(128)S(1)} %reshape.136.k_blocks, bf16[1024,256]{1,0:T(8,128)(2,1)S(1)} %bitcast.76, bf16[4096,256]{1,0:T(8,128)(2,1)} %bitcast.73, bf16[1024,256]{1,0:T(8,128)(2,1)S(1)} %bitcast.77, ...), custom_call_target="tpu_custom_call" | custom-call | flops 10000000000 | bytes 8000000 | tf_op jit(solution)/shard_map/attend_back/pallas_call | solution.py:250
  277.4 77.2 %end.1 = (f32[128,1024]{1,0:T(8,128)S(1)}, f32[8,8,512]{2,1,0:T(8,128)S(1)}, f32[8,8,768]{2,1,0:T(8,128)S(1)}, bf16[16,16,1024]{2,1,0:T(8,128)(2,1)S(1)}, f32[24,128]{1,0:T(8,128)S(1)}) custom-call(bf16[4,2,128,256]{3,2,1,0:T(8,128)(2,1)S(1)} %bitcast.62, bf16[16,2,128,256]{3,2,1,0:T(8,128)(2,1)} %bitcast.78, f32[1024,384]{1,0:T(8,128)} %get-tuple-element.66.projected, ...), custom_call_target="tpu_custom_call" | custom-call | tf_op jit(solution)/shard_map/end/pallas_call | solution.py:1484
  354.9 0.9 multiply_subtract_fusion
  355.8 0.7 multiply_subtract_fusion.3
  356.6 0.7 multiply_subtract_fusion.4
  357.4 0.7 multiply_subtract_fusion.2
  358.1 0.6 multiply_subtract_fusion.5
  358.7 0.7 copy.73
  359.4 0.8 copy.74
  (72 shorter events, 1.8 us)
Async XLA Ops:
  6.2 1.0 copy-start
  81.3 1.6 copy-start.3
  82.9 22.1 %copy-start.1 = (bf16[1,128,1024]{2,1,0:T(8,128)(2,1)S(1)}, bf16[1,128,1024]{2,1,0:T(8,128)(2,1)}, u32[]{:S(2)}) copy-start(bf16[1,128,1024]{2,1,0:T(8,128)(2,1)} %param.22) | copy-start | bytes 786436
  82.9 22.1 %copy-start.2 = (bf16[1,128,1024]{2,1,0:T(8,128)(2,1)S(1)}, bf16[1,128,1024]{2,1,0:T(8,128)(2,1)}, u32[]{:S(2)}) copy-start(bf16[1,128,1024]{2,1,0:T(8,128)(2,1)} %param.23) | copy-start | bytes 786436
  277.4 77.4 %copy-start.4 = (f32[8,6144]{1,0:T(8,128)S(1)}, f32[8,6144]{1,0:T(8,128)}, u32[]{:S(2)}) copy-start(f32[8,6144]{1,0:T(8,128)} %param.29) | copy-start | bytes 589828
  277.4 77.4 %copy-start.10 = (f32[8,6144]{1,0:T(8,128)S(1)}, f32[8,6144]{1,0:T(8,128)}, u32[]{:S(2)}) copy-start(f32[8,6144]{1,0:T(8,128)} %param.35) | copy-start | bytes 589828
  277.4 77.4 %copy-start.11 = (f32[8,6144]{1,0:T(8,128)S(1)}, f32[8,6144]{1,0:T(8,128)}, u32[]{:S(2)}) copy-start(f32[8,6144]{1,0:T(8,128)} %param.41) | copy-start | bytes 589828
  354.7 1.1 copy-start.9
  354.7 1.1 copy-start.16
  354.7 1.1 copy-start.17
  354.7 1.8 copy-start.5
  354.7 1.8 copy-start.12
  354.7 1.8 copy-start.13
  354.7 2.6 copy-start.7
  354.8 2.6 copy-start.14
  354.8 2.6 copy-start.15
  354.8 3.3 copy-start.18
  354.8 3.3 copy-start.19
  354.8 3.3 copy-start.20
  356.5 3.7 %copy-start.8 = (f32[8,8,256]{2,0,1:T(8,128)}, f32[8,8,256]{2,0,1:T(8,128)S(1)}, u32[]{:S(2)}) copy-start(f32[8,8,256]{2,0,1:T(8,128)S(1)} %slice.80) | copy-start | bytes 196612
  357.4 2.8 copy-start.6

commit v4 on v3

--- a/solution.py
+++ b/solution.py
@@ -130,9 +130,16 @@
             mixed = mixed + dot_nn(values_t[c], weights.astype(BF16))
             return total, mixed
 
+        def two_chunks(j, state):
+            c = first + 2 * j
+            return one_chunk(c + 1, one_chunk(c, state, False), False)
+
+        first = first_chunk(block)
+        pairs = lax.div(last - first, 2)
         state = (jnp.zeros((1, 2 * BLOCK), F32), jnp.zeros((HD, 2 * BLOCK), F32))
+        state = lax.fori_loop(0, pairs, two_chunks, state)
         state = lax.fori_loop(
-            first_chunk(block), last, lambda c, s: one_chunk(c, s, False), state
+            first + 2 * pairs, last, lambda c, s: one_chunk(c, s, False), state
         )
         total, mixed = one_chunk(last, state, True)
         result = (mixed / total).T.astype(BF16)
@@ -220,12 +227,14 @@
             dk[rows, :] += dot_nn(grad_scores, query)
             return dq + dot_nn(keys_t[c], grad_scores)
 
-        dq = lax.fori_loop(
-            first_chunk(block),
-            last,
-            lambda c, s: one_chunk(c, s, False),
-            jnp.zeros((HD, 2 * BLOCK), F32),
-        )
+        def two_chunks(j, dq):
+            c = first + 2 * j
+            return one_chunk(c + 1, one_chunk(c, dq, False), False)
+
+        first = first_chunk(block)
+        pairs = lax.div(last - first, 2)
+        dq = lax.fori_loop(0, pairs, two_chunks, jnp.zeros((HD, 2 * BLOCK), F32))
+        dq = lax.fori_loop(first + 2 * pairs, last, lambda c, s: one_chunk(c, s, False), dq)
         dq = (one_chunk(last, dq, True) * SCALE).T.astype(BF16)
         rows = pl.ds(pl.multiple_of(tile * BLOCK, BLOCK), BLOCK)
         dq_ref[rows, :HD] = dq[:BLOCK]
@@ -275,10 +284,12 @@
         self.me, self.z, self.core = me, me["zh"] * 2 + me["zl"], me["co"]
         self.part, self.paired, self.sending, self.landed = part, paired, sending, landed
         self.near_sems, self.far_sems = (near_send, near_recv), (far_send, far_recv)
+        self.rows = part.shape[-2]
+        self.top, self.low = pl.ds(0, self.rows // 2), pl.ds(self.rows // 2, self.rows // 2)
 
     def near(self, phase, off):
         return pltpu.make_async_remote_copy(
-            src_ref=self.part.at[phase, off, 1 - self.core],
+            src_ref=self.part.at[phase, lax.rem(self.z + off, 4), 1 - self.core],
             dst_ref=self.paired.at[phase, off],
             send_sem=self.near_sems[0].at[phase, off],
             recv_sem=self.near_sems[1].at[phase, off],
@@ -286,39 +297,61 @@
             device_id_type=MESH,
         )
 
-    def far(self, phase, off):
+    def far(self, phase, which):
+        slot = which if which in (1, 3) else 2
+        src, dst = self.sending.at[phase, slot], self.landed.at[phase, slot]
+        if slot == 2:
+            half = self.top if which == 2 else self.low
+            src, dst = src.at[half], dst.at[half]
+        step = 1 if which in (1, 2) else 3
         return pltpu.make_async_remote_copy(
-            src_ref=self.sending.at[phase, off],
-            dst_ref=self.landed.at[phase, off],
-            send_sem=self.far_sems[0].at[phase, off],
-            recv_sem=self.far_sems[1].at[phase, off],
-            device_id=address(column_place(self.me, lax.rem(self.z + off, 4), self.core)),
+            src_ref=src,
+            dst_ref=dst,
+            send_sem=self.far_sems[0].at[phase, which],
+            recv_sem=self.far_sems[1].at[phase, which],
+            device_id=address(column_place(self.me, lax.rem(self.z + step, 4), self.core)),
             device_id_type=MESH,
         )
 
     def put(self, phase, off, terms):
-        self.part[phase, off] = terms.astype(BF16).reshape(2, ROWS, D)
+        self.part[phase, lax.rem(self.z + off, 4)] = terms.astype(BF16).reshape(2, self.rows, D)
         self.near(phase, off).start()
 
-    def pass_on(self, phase, off):
+    def put_all(self, phase, terms):
+        self.part[phase] = terms.astype(BF16).reshape(4, 2, self.rows, D)
+        for off in (2, 1, 3, 0):
+            self.near(phase, off).start()
+
+    def chip_sum(self, phase, off):
         self.near(phase, off).wait_recv()
-        both = self.part[phase, off, self.core].astype(F32) + self.paired[phase, off].astype(F32)
-        self.sending[phase, off] = both.astype(BF16)
-        self.far(phase, off).start()
+        mine = self.part[phase, lax.rem(self.z + off, 4), self.core].astype(F32)
+        return mine + self.paired[phase, off].astype(F32)
+
+    def first(self, phase):
+        self.sending[phase, 2] = self.chip_sum(phase, 2).astype(BF16)
+        self.far(phase, 2).start()
+        self.far(phase, 0).start()
+
+    def second(self, phase):
+        for which, by_way, half in ((1, 2, self.top), (3, 0, self.low)):
+            self.sending[phase, which] = self.chip_sum(phase, which).astype(BF16)
+            self.far(phase, by_way).wait_recv()
+            both = self.sending[phase, which, half].astype(F32)
+            both = both + self.landed[phase, 2, half].astype(F32)
+            self.sending[phase, which, half] = both.astype(BF16)
+            self.far(phase, which).start()
 
     def total(self, phase):
-        self.near(phase, 0).wait_recv()
-        total = self.part[phase, 0, self.core].astype(F32) + self.paired[phase, 0].astype(F32)
-        for off in (1, 3, 2):
-            self.far(phase, off).wait_recv()
-            total = total + self.landed[phase, off].astype(F32)
+        total = self.chip_sum(phase, 0)
+        for which in (1, 3):
+            self.far(phase, which).wait_recv()
+            total = total + self.landed[phase, which].astype(F32)
         return total
 
     def drain(self, phase):
         for off in range(4):
             self.near(phase, off).wait_send()
-            if off:
-                self.far(phase, off).wait_send()
+            self.far(phase, off).wait_send()
 
 
 class ColumnGathers:
@@ -326,16 +359,22 @@
         self.me, self.z, self.core = me, me["zh"] * 2 + me["zl"], me["co"]
         self.blocks = blocks
         self.near_sems, self.far_sems = (near_send, near_recv), (far_send, far_recv)
-
-    def far(self, phase, off, arriving):
-        z = lax.rem(self.z + 4 - off, 4) if arriving else self.z
-        block = self.blocks.at[phase, z * 2 + self.core]
+        self.rows = blocks.shape[-2]
+
+    def far(self, phase, which, arriving):
+        step = 1 if which in (1, 2) else 3
+        back = (step if which in (1, 3) else 2 * step) if arriving else (0 if which in (1, 3) else step)
+        block = self.blocks.at[phase, lax.rem(self.z + 4 * 2 - back, 4) * 2 + self.core]
+        if which == 2:
+            block = block.at[pl.ds(0, self.rows // 2)]
+        if which == 0:
+            block = block.at[pl.ds(self.rows // 2, self.rows // 2)]
         return pltpu.make_async_remote_copy(
             src_ref=block,
             dst_ref=block,
-            send_sem=self.far_sems[0].at[phase, off],
-            recv_sem=self.far_sems[1].at[phase, off],
-            device_id=address(column_place(self.me, lax.rem(self.z + off, 4), self.core)),
+            send_sem=self.far_sems[0].at[phase, which],
+            recv_sem=self.far_sems[1].at[phase, which],
+            device_id=address(column_place(self.me, lax.rem(self.z + step, 4), self.core)),
             device_id_type=MESH,
         )
 
@@ -353,32 +392,39 @@
 
     def begin(self, phase, rows):
         self.blocks[phase, self.z * 2 + self.core] = rows
-        for off in (1, 3, 2):
+        for off in (1, 3):
             self.far(phase, off, False).start()
         self.near(phase, 0, False).start()
 
+    def pass_on(self, phase):
+        for off, by_way in ((1, 2), (3, 0)):
+            self.far(phase, off, True).wait_recv()
+            self.far(phase, by_way, False).start()
+            self.near(phase, off, False).start()
+
     def await_chip(self, phase, i):
         off = i + lax.div(i, 2) * (5 - 2 * i)
 
-        @pl.when(i == 1)
-        def _():
-            for near_by in (1, 3):
-                self.far(phase, near_by, True).wait_recv()
-                self.near(phase, near_by, False).start()
-
         @pl.when(i == 3)
         def _():
-            self.far(phase, 2, True).wait_recv()
+            for by_way in (2, 0):
+                self.far(phase, by_way, True).wait_recv()
             self.near(phase, 2, False).start()
 
         self.near(phase, off, True).wait_recv()
         return off, lax.rem(self.z + 4 - off, 4)
+
+    def await_all(self, phase):
+        for by_way in (2, 0):
+            self.far(phase, by_way, True).wait_recv()
+        self.near(phase, 2, False).start()
+        for off in range(4):
+            self.near(phase, off, True).wait_recv()
 
     def drain(self, phase):
         for off in range(4):
             self.near(phase, off, False).wait_send()
-            if off:
-                self.far(phase, off, False).wait_send()
+            self.far(phase, off, False).wait_send()
 
 
 def norm_factor(values):
@@ -391,6 +437,10 @@
     inner = jnp.mean(values * scaled, axis=-1, keepdims=True)
     grad_gain = jnp.sum(grad * values * factor, axis=0, keepdims=True)
     return factor * scaled - values * (factor * factor * factor * inner), grad_gain
+
+
+def gray(i):
+    return i + lax.div(i, 2) * (5 - 2 * i)
 
 
 def quarter(place):
@@ -441,8 +491,15 @@
             greet(barrier, column_place(me, lax.rem(z + off, 4), me["co"]))
         greet(barrier, column_place(me, z, 1 - me["co"]))
         expected = expected + 4
-    if rows is not None:
-        at_home = me["x"] == quarter(me)
+    at_home = me["x"] == quarter(me)
+    if rows == "swap":
+
+        @pl.when(jnp.logical_not(at_home))
+        def _():
+            greet(barrier, swap_partner(me))
+
+        expected = expected + 1 - jnp.where(at_home, 1, 0)
+    elif rows is not None:
 
         def greet_rows(k, carry):
             @pl.when(jnp.logical_not(jnp.logical_and(k == 0, at_home)))
@@ -458,6 +515,44 @@
         count = PLANE - jnp.where(at_home, 1, 0)
         expected = expected + (2 * count if rows == "both" else count)
     pl.semaphore_wait(barrier, expected)
+
+
+def swap_partner(me):
+    return at_quarter(dict(me, x=quarter(me)), me["x"])
+
+
+class Swap:
+    def __init__(self, me, src, dst, own_dst, sems):
+        self.at_home = me["x"] == quarter(me)
+        self.remote = lambda: pltpu.make_async_remote_copy(
+            src_ref=src,
+            dst_ref=dst,
+            send_sem=sems.at[0],
+            recv_sem=sems.at[1],
+            device_id=address(swap_partner(me)),
+            device_id_type=MESH,
+        )
+        self.own = lambda: pltpu.make_async_copy(src, own_dst, sems.at[0])
+
+    def either(self, remote, own):
+        @pl.when(self.at_home)
+        def _():
+            own()
+
+        @pl.when(jnp.logical_not(self.at_home))
+        def _():
+            remote()
+
+    def begin(self):
+        self.either(lambda: self.remote().start(), lambda: self.own().start())
+
+    def finish(self):
+        def both():
+            copy = self.remote()
+            copy.wait_recv()
+            copy.wait_send()
+
+        self.either(both, lambda: self.own().wait())
 
 
 class RowCopies:
@@ -554,15 +649,116 @@
         self.each(lambda k: self.copy(k, False).wait_send())
 
 
+class PlaneGathers:
+    def __init__(self, me, views, first_send, first_recv, second_send, second_recv):
+        self.me, self.views = me, views
+        self.sems = ((first_send, first_recv), (second_send, second_recv))
+
+    def copy(self, turn, view, half, k, arriving):
+        axis = "xy"[half] if turn == 0 else "yx"[half]
+        to = shifted(self.me, (axis,), k, 1)
+        frm = shifted(self.me, (axis,), k, -1) if arriving else self.me
+        one, many = self.views[view]
+        block = one(half, frm["x"], frm["y"]) if turn == 0 else many(half, frm["yx"[half]])
+        return pltpu.make_async_remote_copy(
+            src_ref=block,
+            dst_ref=block,
+            send_sem=self.sems[turn][0].at[view, half, k],
+            recv_sem=self.sems[turn][1].at[view, half, k],
+            device_id=address(to),
+            device_id_type=MESH,
+        )
+
+    def each(self, view, act):
+        for half in range(2):
+            for k in (1, 3, 2):
+                act(half, k)
+
+    def begin(self, view):
+        self.each(view, lambda half, k: self.copy(0, view, half, k, False).start())
+
+    def pass_on(self, view):
+        for half in range(2):
+            for k in (1, 3, 2):
+                self.copy(0, view, half, k, True).wait_recv()
+            for k in (1, 3, 2):
+                self.copy(1, view, half, k, False).start()
+
+    def arrive(self, view):
+        self.each(view, lambda half, k: self.copy(1, view, half, k, True).wait_recv())
+
+    def drain(self):
+        for view in range(len(self.views)):
+            for turn in range(2):
+                self.each(
+                    view, lambda half, k: self.copy(turn, view, half, k, False).wait_send()
+                )
+
+
+class PlaneSums:
+    def __init__(self, me, lines, got, middle_sums, got_last, first_send, first_recv, last_send, last_recv):
+        self.me, self.lines, self.got, self.sums, self.got_last = me, lines, got, middle_sums, got_last
+        self.sems = ((first_send, first_recv), (last_send, last_recv))
+
+    def row(self, half, at):
+        return (half, at) if half == 0 else (half, slice(None), at)
+
+    def copy(self, turn, half, k):
+        axis = "xy"[half] if turn == 0 else "yx"[half]
+        to = shifted(self.me, (axis,), k, 1)
+        if turn == 0:
+            src, dst = self.lines.at[self.row(half, to[axis])], self.got.at[half, k]
+        else:
+            src, dst = self.sums.at[half, to[axis]], self.got_last.at[half, k]
+        return pltpu.make_async_remote_copy(
+            src_ref=src,
+            dst_ref=dst,
+            send_sem=self.sems[turn][0].at[half, k],
+            recv_sem=self.sems[turn][1].at[half, k],
+            device_id=address(to),
+            device_id_type=MESH,
+        )
+
+    def begin(self):
+        for half in range(2):
+            for k in (1, 3, 2):
+                self.copy(0, half, k).start()
+
+    def pass_on(self):
+        for half in range(2):
+            total = self.lines[self.row(half, self.me["xy"[half]])].astype(F32)
+            for k in (1, 3, 2):
+                self.copy(0, half, k).wait_recv()
+                total = total + self.got[half, k].astype(F32)
+            self.sums[half] = total.astype(BF16)
+            for k in (1, 3, 2):
+                self.copy(1, half, k).start()
+
+    def total(self, half):
+        total = self.sums[half, self.me["yx"[half]]].astype(F32)
+        for k in (1, 3, 2):
+            self.copy(1, half, k).wait_recv()
+            total = total + self.got_last[half, k].astype(F32)
+        return total
+
+    def drain(self):
+        for turn in range(2):
+            for half in range(2):
+                for k in (1, 3, 2):
+                    self.copy(turn, half, k).wait_send()
+
+
 def start_kernel(
     sent_a,
     sent_b,
     tokens,
     output_rows,
+    down_rows,
     frequency,
     q_mine,
     kv_mine,
     all_tokens,
+    down_low,
     output_wide,
     gateup_low,
     extra_out,
@@ -596,6 +792,7 @@
     kv_recv,
     relay_send,
     relay_recv,
+    swap_sems,
     own_sems,
 ):
     me = where_am_i()
@@ -618,29 +815,47 @@
         b_send,
         b_recv,
     )
-    spread = Exchange(
+    spread = PlaneGathers(
         me,
-        SURFACE,
-        lambda to: wide.at[:, here],
-        lambda frm: wide.at[:, flat_index(frm, SURFACE)],
+        (
+            (
+                lambda half, x, y: wide.at[half, x, y],
+                lambda half, at: wide.at[0, :, at] if half == 0 else wide.at[1, at],
+            ),
+            (
+                lambda half, x, y: output_wide.at[y, x, :, pl.ds(half * 512, 512)],
+                lambda half, at: (
+                    output_wide.at[at, :, :, pl.ds(0, 512)]
+                    if half == 0
+                    else output_wide.at[:, at, :, pl.ds(512, 512)]
+                ),
+            ),
+        ),
         w_send,
         w_recv,
-    )
-    rows = RowCopies(me, output_rows, output_wide, row_send, row_recv, False)
+        row_send,
+        row_recv,
+    )
+    output_swap = Swap(
+        me, output_rows, output_wide.at[y, quarter(me)], output_wide.at[y, x], swap_sems.at[0]
+    )
+    down_swap = Swap(me, down_rows, down_low, down_low, swap_sems.at[1])
     own_a = pltpu.make_async_copy(sent_a.at[rank], shares_a.at[rank], own_sems.at[0])
     own_b = pltpu.make_async_copy(sent_b.at[rank], shares_b.at[rank], own_sems.at[1])
     own_a.start()
     own_b.start()
-    greet_all(me, "all", "use")
+    greet_all(me, "all", "swap")
     to_a.begin()
+    output_swap.begin()
     gathers.begin(0, tokens[...])
-    rows.begin()
+    down_swap.begin()
     to_b.begin()
 
     own_a.wait()
     to_a.arrive()
-    wide[:, here] = shares_a[...].astype(BF16).reshape(2, 32, 640)
-    spread.begin()
+    wide[:, x, y] = shares_a[...].astype(BF16).reshape(2, 32, 640)
+    spread.begin(0)
+    output_swap.finish()
     extra_out[...] = shares_a[:, :, 512:]
 
     lanes = lax.broadcasted_iota(jnp.int32, (BLOCK, HD), 1)
@@ -657,11 +872,13 @@
         return carry
 
     lax.fori_loop(0, RANKS, tables, 0)
+    spread.pass_on(0)
+    spread.begin(1)
     own_b.wait()
     to_b.arrive()
     gateup_low[...] = shares_b[...].astype(BF16).reshape(2, 32, 768)
 
-    spread.arrive()
+    spread.arrive(0)
     qkv_part[...] = wide[..., :512].reshape(D, 512)
     extra = wide[..., 512:].reshape(D, HD)
     gains_out[...] = extra
@@ -703,16 +920,20 @@
             keyvals.at[row_zh, x], kv_mine.at[here, row_zh], own_sems.at[4 + row_zh]
         )
 
-    def relay(row_zh, from_x, k, arriving):
-        to_y = lax.rem(y + k, 4)
-        from_y = lax.rem(y + 4 - k, 4) if arriving else y
-        block = kv_mine.at[from_x * 4 + from_y, row_zh]
+    def relay(row_zh, from_x, which, arriving):
+        step = 1 if which in (1, 2) else 3
+        back = (step if which in (1, 3) else 2 * step) if arriving else (0 if which in (1, 3) else step)
+        block = kv_mine.at[from_x * 4 + lax.rem(y + 8 - back, 4), row_zh]
+        if which == 2:
+            block = block.at[pl.ds(0, BLOCK)]
+        if which == 0:
+            block = block.at[pl.ds(BLOCK, BLOCK)]
         return pltpu.make_async_remote_copy(
             src_ref=block,
             dst_ref=block,
-            send_sem=relay_send.at[row_zh, from_x, k],
-            recv_sem=relay_recv.at[row_zh, from_x, k],
-            device_id=address(dict(me, y=to_y)),
+            send_sem=relay_send.at[row_zh, from_x, which],
+            recv_sem=relay_recv.at[row_zh, from_x, which],
+            device_id=address(dict(me, y=lax.rem(y + step, 4))),
             device_id_type=MESH,
         )
 
@@ -754,14 +975,16 @@
 
         return carry
 
+    gathers.pass_on(0)
     lax.fori_loop(0, 4, project, 0)
+    spread.pass_on(1)
     for i in range(RANKS):
         slot = pltpu.make_async_copy(blocks.at[0, i], all_tokens.at[i], own_sems.at[6 + i])
         slot.start()
     for row_zh in range(2):
         kv_own(row_zh).wait()
-        for k in (2, 1, 3):
-            relay(row_zh, x, k, False).start()
+        for which in (1, 3):
+            relay(row_zh, x, which, False).start()
     for off in (1, 3, 2):
         from_x = lax.rem(x + 4 - off, 4)
         to_x = lax.rem(x + off, 4)
@@ -774,8 +997,18 @@
                 device_id=address(dict(me, x=to_x)),
                 device_id_type=MESH,
             ).wait_recv()
-            for k in (2, 1, 3):
-                relay(row_zh, from_x, k, False).start()
+            for which in (1, 3):
+                relay(row_zh, from_x, which, False).start()
+
+    def forward(j, carry):
+        off, row_zh = lax.div(j, 2), lax.rem(j, 2)
+        from_x = lax.rem(x + 4 - gray(off), 4)
+        for which, by_way in ((1, 2), (3, 0)):
+            relay(row_zh, from_x, which, True).wait_recv()
+            relay(row_zh, from_x, by_way, False).start()
+        return carry
+
+    lax.fori_loop(0, 8, forward, 0)
     for off in (1, 3, 2):
         from_x = lax.rem(x + 4 - off, 4)
         to_x = lax.rem(x + off, 4)
@@ -794,21 +1027,23 @@
 
     def finish(j, carry):
         row_zh, from_x = lax.div(j, 4), lax.rem(j, 4)
-        for k in (1, 3, 2):
-            relay(row_zh, from_x, k, False).wait_send()
-            relay(row_zh, from_x, k, True).wait_recv()
+        for which in range(4):
+            relay(row_zh, from_x, which, False).wait_send()
+        for which in (2, 0):
+            relay(row_zh, from_x, which, True).wait_recv()
         return carry
 
     lax.fori_loop(0, 8, finish, 0)
-    rows.arrive()
+    spread.arrive(1)
+    down_swap.finish()
     for i in range(RANKS):
         pltpu.make_async_copy(blocks.at[0, i], all_tokens.at[i], own_sems.at[6 + i]).wait()
-    for exchange in (to_a, to_b, spread, rows):
+    for exchange in (to_a, to_b, spread):
         exchange.drain()
     gathers.drain(0)
 
 
-def start(number, sent_a, sent_b, tokens, output_rows, frequency):
+def start(number, sent_a, sent_b, tokens, output_rows, down_rows, frequency):
     anywhere = pl.BlockSpec(memory_space=pl.ANY)
     vmem = pl.BlockSpec(memory_space=pltpu.VMEM)
     dma = pltpu.SemaphoreType.DMA
@@ -819,7 +1054,8 @@
             struct((4, 2, ROWS, 256), BF16),
             struct((PLANE, 2, ROWS, 256), BF16),
             struct((RANKS, ROWS, D), BF16),
-            struct((PLANE, 16, D), BF16),
+            struct((48, 512), BF16),
+            struct((4, 4, 16, D), BF16),
             struct((2, 32, 768), BF16),
             struct((RANKS, 8, HD), F32),
             struct((D, HD), BF16),
@@ -829,33 +1065,33 @@
             struct((RANKS * ROWS, HD), F32),
             struct((2, HD), F32),
         ),
-        in_specs=[anywhere, anywhere, vmem, anywhere, vmem],
-        out_specs=(anywhere, anywhere, anywhere, anywhere) + (vmem,) * 8,
+        in_specs=[anywhere, anywhere, vmem, anywhere, anywhere, vmem],
+        out_specs=(anywhere,) * 4 + (vmem,) * 9,
         scratch_shapes=[
             pltpu.VMEM((RANKS, 8, 640), F32),
             pltpu.VMEM((RANKS, 8, 768), F32),
-            pltpu.VMEM((2, PLANE, 32, 640), BF16),
+            pltpu.VMEM((2, 4, 4, 32, 640), BF16),
             pltpu.VMEM((1, RANKS, ROWS, D), BF16),
             pltpu.VMEM((2, 4, ROWS, 256), BF16),
             pltpu.VMEM((2, 4, ROWS, 256), BF16),
         ]
         + [dma((RANKS,))] * 4
-        + [dma((PLANE,))] * 4
+        + [dma((2, 2, 4))] * 4
         + [dma((1, 4))] * 4
         + [dma((2, 4))] * 4
-        + [dma((2, 4, 4)), dma((2, 4, 4)), dma((6 + RANKS,))],
+        + [dma((2, 4, 4)), dma((2, 4, 4)), dma((2, 2)), dma((6 + RANKS,))],
         compiler_params=pltpu.CompilerParams(
             collective_id=number, has_side_effects=True, vmem_limit_bytes=VMEM_LIMIT
         ),
         name="start",
-    )(sent_a, sent_b, tokens, output_rows, frequency)
+    )(sent_a, sent_b, tokens, output_rows, down_rows, frequency)
 
 
 def middle_kernel(
     out_mine,
     wo,
     gateup_low,
-    down_rows_low,
+    down_rows,
     inputs,
     upstream,
     gains,
@@ -863,7 +1099,7 @@
     grad_hidden,
     gains_grad,
     grad_mine,
-    gateup_parts,
+    gateup_sum,
     down_parts,
     output_lines,
     attended,
@@ -882,8 +1118,11 @@
     branch,
     hidden,
     wgu,
+    wd,
     down_wide,
-    wd,
+    got,
+    plane_sums,
+    got_last,
     near_send,
     near_recv,
     far_send,
@@ -898,6 +1137,8 @@
     back_recv,
     plane_send,
     plane_recv,
+    last_send,
+    last_recv,
     w_send,
     w_recv,
     row_send,
@@ -913,163 +1154,159 @@
         me, part, paired, sending, landed, near_send, near_recv, far_send, far_recv
     )
     gathers = ColumnGathers(me, blocks, gnear_send, gnear_recv, gfar_send, gfar_recv)
-    own = pltpu.make_async_copy(out_mine.at[x], attended.at[:, x], own_sems.at[0])
-    own.start()
-    own_wgu = pltpu.make_async_copy(gateup_low, wgu.at[:, here], own_sems.at[2])
+    own_wgu = pltpu.make_async_copy(gateup_low, wgu.at[:, x, me["y"]], own_sems.at[0])
     own_wgu.start()
-    spread = Exchange(
+    own_down = pltpu.make_async_copy(down_rows, down_wide.at[me["y"], x], own_sems.at[1])
+    own_down.start()
+    spread = PlaneGathers(
         me,
-        SURFACE,
-        lambda to: gateup_low,
-        lambda frm: wgu.at[:, flat_index(frm, SURFACE)],
+        (
+            (
+                lambda half, x, y: wgu.at[half, x, y],
+                lambda half, at: wgu.at[0, :, at] if half == 0 else wgu.at[1, at],
+            ),
+            (
+                lambda half, x, y: down_wide.at[y, x, :, pl.ds(half * 256, 256)],
+                lambda half, at: (
+                    down_wide.at[at, :, :, pl.ds(0, 256)]
+                    if half == 0
+                    else down_wide.at[:, at, :, pl.ds(256, 256)]
+                ),
+            ),
+        ),
         w_send,
         w_recv,
-    )
-    rows_in = RowCopies(me, down_rows_low, down_wide, row_send, row_recv, False)
+        row_send,
+        row_recv,
+    )
     rows_back = RowCopies(me, down_lines, down_parts, down_send, down_recv, True)
-    gateup_back = Exchange(
-        me,
-        SURFACE,
-        lambda to: gateup_lines.at[:, flat_index(to, SURFACE)],
-        lambda frm: gateup_parts.at[flat_index(frm, SURFACE)],
-        plane_send,
-        plane_recv,
-    )
-    own_gateup = pltpu.make_async_copy(
-        gateup_lines.at[:, here], gateup_parts.at[here], own_sems.at[1]
-    )
-    greet_all(me, "some", "both")
-
-    def attention_out(k, arriving):
+    gateup_back = PlaneSums(
+        me, gateup_lines, got, plane_sums, got_last, plane_send, plane_recv, last_send, last_recv
+    )
+
+    def half_rows(half):
+        return pl.ds(half * BLOCK, BLOCK)
+
+    def own_out(half):
+        return pltpu.make_async_copy(
+            out_mine.at[x, :, half_rows(half)], attended.at[half, :, x], own_sems.at[2 + half]
+        )
+
+    def attention_out(half, k, arriving):
         frm = shifted(me, ("x",), k, -1) if arriving else me
         to = shifted(me, ("x",), k, 1)
         return pltpu.make_async_remote_copy(
-            src_ref=out_mine.at[to["x"]],
-            dst_ref=attended.at[:, frm["x"]],
-            send_sem=att_send.at[k],
-            recv_sem=att_recv.at[k],
+            src_ref=out_mine.at[to["x"], :, half_rows(half)],
+            dst_ref=attended.at[half, :, frm["x"]],
+            send_sem=att_send.at[half, k],
+            recv_sem=att_recv.at[half, k],
             device_id=address(to),
             device_id_type=MESH,
         )
 
-    for k in (2, 1, 3):
-        attention_out(k, False).start()
-    spread.begin()
-    rows_in.begin()
-    own.wait()
-    for k in (1, 3, 2):
-        attention_out(k, True).wait_recv()
-
-    def project_out(i, carry):
-        back = 3 - i
-        off = back + lax.div(back, 2) * (5 - 2 * back)
-        to_z = lax.rem(z + off, 4)
-        rows = attended[lax.div(to_z, 2), pl.ds(lax.rem(to_z, 2) * 2, 2)].reshape(2 * ROWS, 256)
-        sums.put(0, off, dot_nn(rows, wo[...]))
-
-        @pl.when(i >= 1)
-        def _():
-            last = back + 1
-            sums.pass_on(0, last + lax.div(last, 2) * (5 - 2 * last))
-
-        return carry
-
-    lax.fori_loop(0, 4, project_out, 0)
-    branch[...] = sums.total(0)
-    normed = branch[...] * norm_factor(branch[...]) * gains[0:1, :]
-    hidden[...] = inputs[...].astype(F32) + normed
-    gathers.begin(0, hidden[...].astype(BF16))
-
-    def chip_rows(phase, at_z):
-        return blocks[phase, pl.ds(at_z * 2, 2)].reshape(2 * ROWS, D)
-
-    def pass_on_last(phase, i):
-        @pl.when(i >= 2)
-        def _():
-            last = i - 1
-            sums.pass_on(phase, last + lax.div(last, 2) * (5 - 2 * last))
-
-    def at_rows(at_z):
-        return pl.ds(pl.multiple_of(at_z * 2 * ROWS, 2 * ROWS), 2 * ROWS)
-
+    for half in range(2):
+        own_out(half).start()
+    greet_all(me, "some", "own")
+    for half in range(2):
+        for k in (2, 1, 3):
+            attention_out(half, k, False).start()
     own_wgu.wait()
-    spread.arrive()
-    rows_in.arrive()
+    own_down.wait()
+    spread.begin(0)
+    spread.begin(1)
 
     def down_line_in(j, carry):
         at = pl.ds(pl.multiple_of(j * 48, 16), 48)
-        pair = down_wide[pl.ds(2 * j, 2)].astype(F32)
-        for half in range(2):
-            part = pair[:, half * 24 : half * 24 + 24].reshape(48, 512)
-            wd[at, half * 512 : half * 512 + 512] = part.astype(BF16)
+        pair = down_wide[lax.div(j, 2), pl.ds(lax.rem(j, 2) * 2, 2)].astype(F32)
+        for side in range(2):
+            rows = pair[:, side * 24 : side * 24 + 24].reshape(48, 512)
+            wd[at, side * 512 : side * 512 + 512] = rows.astype(BF16)
         return carry
 
-    lax.fori_loop(0, PLANE // 2, down_line_in, 0)
-
-    def feed_forward(i, carry):
-        off, at_z = gathers.await_chip(0, i)
-        both = dot_nn(chip_rows(0, at_z), wgu[...].reshape(D, 768))
-        gate_up[at_rows(at_z), :] = both
+    def project_out(half):
+        own_out(half).wait()
+        for k in (1, 3, 2):
+            attention_out(half, k, True).wait_recv()
+
+        rows = attended[half].reshape(RANKS * BLOCK, 256)
+        sums.put_all(half, dot_nn(rows, wo[...]))
+
+    def block_rows(phase):
+        return blocks[phase].reshape(RANKS * BLOCK, D)
+
+    def at_half(half):
+        return slice(half * RANKS * BLOCK, (half + 1) * RANKS * BLOCK)
+
+    def attention_norm(half):
+        at = half_rows(half)
+        total = sums.total(half)
+        branch[at, :] = total
+        both = inputs[at, :].astype(F32) + total * norm_factor(total) * gains[0:1, :]
+        hidden[at, :] = both
+        gathers.begin(half, both.astype(BF16))
+
+    def feed_forward(half):
+        at = at_half(half)
+        both = dot_nn(block_rows(half), wgu[...].reshape(D, 768))
+        gate_up[at, :] = both
         gate, up = both[:, :384], both[:, 384:]
         acts = (gate * (1.0 / (1.0 + jnp.exp(-gate))) * up).astype(BF16)
-        activated[at_rows(at_z), :] = acts
-        sums.put(1, lax.rem(4 - off, 4), dot_nn(acts, wd[...]))
-
-        @pl.when(i >= 2)
-        def _():
-            last = i - 1
-            sums.pass_on(1, 4 - (last + lax.div(last, 2) * (5 - 2 * last)))
-
-        return carry
-
-    lax.fori_loop(0, 4, feed_forward, 0)
-    sums.pass_on(1, 2)
-    ffn_out = sums.total(1)
-    grad = upstream[...].astype(F32)
-    result[...] = (hidden[...] + ffn_out * norm_factor(ffn_out) * gains[1:2, :]).astype(BF16)
-    grad_ffn, grad_ffn_gain = norm_back(ffn_out, gains[1:2, :], grad)
-    gathers.begin(1, grad_ffn.astype(BF16))
-    gains_grad[1:2, :] = grad_ffn_gain
-
-    def feed_forward_back(i, carry):
-        off, at_z = gathers.await_chip(1, i)
-        grad_act = dot_nt(chip_rows(1, at_z), wd[...])
-        gate, up = gate_up[at_rows(at_z), :384], gate_up[at_rows(at_z), 384:]
+        activated[at, :] = acts
+        sums.put_all(2 + half, dot_nn(acts, wd[...]))
+
+    def feed_forward_norm(half):
+        at = half_rows(half)
+        ffn_out = sums.total(2 + half)
+        gain = gains[1:2, :]
+        result[at, :] = (hidden[at, :] + ffn_out * norm_factor(ffn_out) * gain).astype(BF16)
+        grad_ffn, grad_gain = norm_back(ffn_out, gain, upstream[at, :].astype(F32))
+        gathers.begin(2 + half, grad_ffn.astype(BF16))
+        return grad_gain
+
+    def feed_forward_back(half):
+        at = at_half(half)
+        grad_act = dot_nt(block_rows(2 + half), wd[...])
+        gate, up = gate_up[at, :384], gate_up[at, 384:]
         sig = 1.0 / (1.0 + jnp.exp(-gate))
-        grad_gate[at_rows(at_z), :384] = (
-            grad_act * up * (sig * (1.0 + gate * (1.0 - sig)))
-        ).astype(BF16)
-        grad_gate[at_rows(at_z), 384:] = (grad_act * (gate * sig)).astype(BF16)
-        sums.put(2, lax.rem(4 - off, 4), dot_nt(grad_gate[at_rows(at_z), :], wgu[...].reshape(D, 768)))
-
-        @pl.when(i >= 2)
-        def _():
-            last = i - 1
-            sums.pass_on(2, 4 - (last + lax.div(last, 2) * (5 - 2 * last)))
-
-        return carry
-
-    lax.fori_loop(0, 4, feed_forward_back, 0)
-    sums.pass_on(2, 2)
-
-    def gateup_rows(j, carry):
-        cols = pl.ds(pl.multiple_of(j * 256, 256), 256)
-        grads = dot_tn(blocks[0, :, :, cols].reshape(RANKS * ROWS, 256), grad_gate[...])
-        gateup_lines[lax.div(j, 2), pl.ds(lax.rem(j, 2) * 8, 8)] = grads.astype(BF16).reshape(
-            8, 32, 768
-        )
-        return carry
-
-    lax.fori_loop(0, 4, gateup_rows, 0)
-    own_gateup.start()
-    gateup_back.begin()
-
-    def down_rows(j, carry):
-        cols = pl.ds(pl.multiple_of(j * 128, 128), 128)
-        down_grad[cols, :] = dot_tn(activated[:, cols], blocks[1].reshape(RANKS * ROWS, D))
-        return carry
-
-    lax.fori_loop(0, 3, down_rows, 0)
+        grad_gate[at, :384] = (grad_act * up * (sig * (1.0 + gate * (1.0 - sig)))).astype(BF16)
+        grad_gate[at, 384:] = (grad_act * (gate * sig)).astype(BF16)
+        sums.put_all(4 + half, dot_nt(grad_gate[at, :], wgu[...].reshape(D, 768)))
+
+    def attention_norm_back(half):
+        at = half_rows(half)
+        total = upstream[at, :].astype(F32) + sums.total(4 + half)
+        grad_hidden[at, :] = total
+        grad_branch, grad_gain = norm_back(branch[at, :], gains[0:1, :], total)
+        gathers.begin(4 + half, grad_branch.astype(BF16))
+        return grad_gain
+
+    def to_attention(half, row_zh, pack):
+        return pltpu.make_async_remote_copy(
+            src_ref=grad_attended.at[half, row_zh, pack],
+            dst_ref=grad_mine.at[x, row_zh, half_rows(half)],
+            send_sem=back_send.at[half, row_zh, pack],
+            recv_sem=back_recv.at[half, row_zh, x],
+            device_id=address(dict(me, x=pack)),
+            device_id_type=MESH,
+        )
+
+    def own_attention(half, row_zh):
+        return pltpu.make_async_copy(
+            grad_attended.at[half, row_zh, x],
+            grad_mine.at[x, row_zh, half_rows(half)],
+            own_sems.at[4 + 2 * half + row_zh],
+        )
+
+    def project_out_back(half):
+        grads = dot_nt(block_rows(4 + half), wo[...]).astype(BF16)
+        grad_attended[half] = grads.reshape(2, 4, BLOCK, 256)
+        for row_zh in range(2):
+            own_attention(half, row_zh).start()
+            for k in (1, 3, 2):
+                to_attention(half, row_zh, lax.rem(x + k, 4)).start()
+
+    def all_rows(phase):
+        return blocks[phase : phase + 2].reshape(RANKS * ROWS, D)
 
     def down_line(s, carry):
         rows = down_grad[pl.ds(pl.multiple_of(s * 24, 8), 24), :].astype(BF16)
@@ -1077,90 +1314,88 @@
         down_lines[s, 24:48, :] = rows[:, 512:]
         return carry
 
-    lax.fori_loop(0, PLANE, down_line, 0)
-    rows_back.begin()
-
-    total = grad + sums.total(2)
-    grad_hidden[...] = total
-    grad_branch, grad_attn_gain = norm_back(branch[...], gains[0:1, :], total)
-    gathers.begin(2, grad_branch.astype(BF16))
-    gains_grad[0:1, :] = grad_attn_gain
-
-    def to_attention(row_zh, pack):
-        return pltpu.make_async_remote_copy(
-            src_ref=grad_attended.at[row_zh, pack],
-            dst_ref=grad_mine.at[x, row_zh],
-            send_sem=back_send.at[row_zh, pack],
-            recv_sem=back_recv.at[row_zh, x],
-            device_id=address(dict(me, x=pack)),
-            device_id_type=MESH,
-        )
-
-    def own_attention(row_zh):
-        return pltpu.make_async_copy(
-            grad_attended.at[row_zh, x], grad_mine.at[x, row_zh], own_sems.at[3 + row_zh]
-        )
-
-    def project_out_back(i, carry):
-        off, at_z = gathers.await_chip(2, i)
-        grads = dot_nt(chip_rows(2, at_z), wo[...]).astype(BF16).reshape(2, ROWS, 256)
-        row_zh = lax.div(at_z, 2)
-        for at_core in range(2):
-            pack = lax.rem(at_z, 2) * 2 + at_core
-            grad_attended[row_zh, pack] = grads[at_core]
-
-            @pl.when(pack != x)
-            def _():
-                to_attention(row_zh, pack).start()
-
-            @pl.when(pack == x)
-            def _():
-                own_attention(row_zh).start()
-
-        return carry
-
-    lax.fori_loop(0, 4, project_out_back, 0)
-
-    def output_rows(j, carry):
-        cols = pl.ds(pl.multiple_of(j * 128, 128), 128)
-        grads = dot_tn(
-            attended[:, :, :, cols].reshape(RANKS * ROWS, 128), blocks[2].reshape(RANKS * ROWS, D)
-        )
-        output_lines[pl.ds(j * 8, 8)] = grads.astype(BF16).reshape(8, 16, D)
-        return carry
-
-    lax.fori_loop(0, 2, output_rows, 0)
-
-    for k in (1, 3, 2):
-        attention_out(k, False).wait_send()
-        frm_x = lax.rem(x + 4 - k, 4)
-        to_x = lax.rem(x + k, 4)
+    def send_down():
+        down_grad[...] = dot_tn(activated[...], all_rows(2))
+        lax.fori_loop(0, PLANE, down_line, 0)
+        rows_back.begin()
+
+    def send_gateup():
+        grads = dot_tn(all_rows(0), grad_gate[...])
+        gateup_lines[...] = grads.astype(BF16).reshape(2, 4, 4, 32, 768)
+        gateup_back.begin()
+
+    works = (project_out, feed_forward, feed_forward_back, project_out_back)
+    thens = (attention_norm, feed_forward_norm, attention_norm_back)
+    gain_grads = [None, None, None]
+    works[0](0)
+    sums.first(0)
+    works[0](1)
+    spread.pass_on(0)
+    spread.pass_on(1)
+    sums.second(0)
+    for stage in range(3):
+        phase = 2 * stage
+        if stage == 2:
+            send_down()
+        gain_grads[stage] = thens[stage](0)
+        if stage > 0:
+            works[stage](1)
+        sums.first(phase + 1)
+        gathers.pass_on(phase)
+        sums.second(phase + 1)
+        if stage == 2:
+            send_gateup()
+        gathers.await_all(phase)
+        if stage == 0:
+            spread.arrive(0)
+            spread.arrive(1)
+            lax.fori_loop(0, PLANE // 2, down_line_in, 0)
+        works[stage + 1](0)
+        other = thens[stage](1)
+        if stage > 0:
+            gains_grad[2 - stage : 3 - stage, :] = gain_grads[stage] + other
+        if stage < 2:
+            sums.first(phase + 2)
+        gathers.pass_on(phase + 1)
+        if stage < 2:
+            sums.second(phase + 2)
+        gathers.await_all(phase + 1)
+    works[3](1)
+    gateup_back.pass_on()
+    grads = dot_tn(attended[...].reshape(RANKS * ROWS, 256), all_rows(4))
+    output_lines[...] = grads.astype(BF16).reshape(PLANE, 16, D)
+
+    for half in range(2):
+        for k in (1, 3, 2):
+            attention_out(half, k, False).wait_send()
+            frm_x = lax.rem(x + 4 - k, 4)
+            to_x = lax.rem(x + k, 4)
+            for row_zh in range(2):
+                to_attention(half, row_zh, to_x).wait_send()
+                pltpu.make_async_remote_copy(
+                    src_ref=grad_attended.at[half, row_zh, to_x],
+                    dst_ref=grad_mine.at[frm_x, row_zh, half_rows(half)],
+                    send_sem=back_send.at[half, row_zh, to_x],
+                    recv_sem=back_recv.at[half, row_zh, frm_x],
+                    device_id=address(dict(me, x=to_x)),
+                    device_id_type=MESH,
+                ).wait_recv()
         for row_zh in range(2):
-            to_attention(row_zh, to_x).wait_send()
-            pltpu.make_async_remote_copy(
-                src_ref=grad_attended.at[row_zh, to_x],
-                dst_ref=grad_mine.at[frm_x, row_zh],
-                send_sem=back_send.at[row_zh, to_x],
-                recv_sem=back_recv.at[row_zh, frm_x],
-                device_id=address(dict(me, x=to_x)),
-                device_id_type=MESH,
-            ).wait_recv()
-    for row_zh in range(2):
-        own_attention(row_zh).wait()
-    for phase in range(3):
+            own_attention(half, row_zh).wait()
+    for phase in range(6):
         sums.drain(phase)
         gathers.drain(phase)
-    own_gateup.wait()
-    gateup_back.arrive()
+    for half in range(2):
+        gateup_sum[half] = gateup_back.total(half)
     rows_back.arrive()
-    for exchange in (spread, rows_in, gateup_back, rows_back):
+    for exchange in (spread, gateup_back, rows_back):
         exchange.drain()
 
 
 def middle(number, out_mine, wo, gateup_low, down_rows, inputs, upstream, gains):
     anywhere = pl.BlockSpec(memory_space=pl.ANY)
     vmem = pl.BlockSpec(memory_space=pltpu.VMEM)
-    block = (ROWS, D)
+    block, half = (ROWS, D), (BLOCK, D)
     dma = pltpu.SemaphoreType.DMA
     return pl.pallas_call(
         middle_kernel,
@@ -1169,36 +1404,41 @@
             jax.ShapeDtypeStruct(block, F32),
             jax.ShapeDtypeStruct((2, D), F32),
             jax.ShapeDtypeStruct((4, 2, ROWS, 256), BF16),
-            jax.ShapeDtypeStruct((PLANE, 2, 32, 768), BF16),
+            jax.ShapeDtypeStruct((2, 32, 768), F32),
             jax.ShapeDtypeStruct((PLANE, 48, 512), BF16),
             jax.ShapeDtypeStruct((PLANE, 16, D), BF16),
         ),
         in_specs=[anywhere, vmem, anywhere, anywhere, vmem, vmem, vmem],
-        out_specs=(vmem, vmem, vmem, anywhere, anywhere, anywhere, vmem),
+        out_specs=(vmem, vmem, vmem, anywhere, vmem, anywhere, vmem),
         scratch_shapes=[
-            pltpu.VMEM((2, 4, ROWS, 256), BF16),
-            pltpu.VMEM((3, RANKS) + block, BF16),
-            pltpu.VMEM((3, 4, 2) + block, BF16),
-            pltpu.VMEM((3, 4) + block, BF16),
-            pltpu.VMEM((3, 4) + block, BF16),
-            pltpu.VMEM((3, 4) + block, BF16),
+            pltpu.VMEM((2, 2, 4, BLOCK, 256), BF16),
+            pltpu.VMEM((6, RANKS) + half, BF16),
+            pltpu.VMEM((6, 4, 2) + half, BF16),
+            pltpu.VMEM((6, 4) + half, BF16),
+            pltpu.VMEM((6, 4) + half, BF16),
+            pltpu.VMEM((6, 4) + half, BF16),
             pltpu.VMEM((RANKS * ROWS, 768), F32),
             pltpu.VMEM((RANKS * ROWS, 384), BF16),
             pltpu.VMEM((RANKS * ROWS, 768), BF16),
-            pltpu.VMEM((2, 4, ROWS, 256), BF16),
-            pltpu.VMEM((2, PLANE, 32, 768), BF16),
+            pltpu.VMEM((2, 2, 4, BLOCK, 256), BF16),
+            pltpu.VMEM((2, 4, 4, 32, 768), BF16),
             pltpu.VMEM((384, D), F32),
             pltpu.VMEM((PLANE, 48, 512), BF16),
             pltpu.VMEM(block, F32),
             pltpu.VMEM(block, F32),
-            pltpu.VMEM((2, PLANE, 32, 768), BF16),
-            pltpu.VMEM((PLANE, 48, 512), BF16),
+            pltpu.VMEM((2, 4, 4, 32, 768), BF16),
             pltpu.VMEM((384, D), BF16),
+            pltpu.VMEM((4, 4, 48, 512), BF16),
+            pltpu.VMEM((2, 4, 4, 32, 768), BF16),
+            pltpu.VMEM((2, 4, 32, 768), BF16),
+            pltpu.VMEM((2, 4, 32, 768), BF16),
         ]
-        + [dma((3, 4))] * 8
-        + [dma((4,)), dma((4,)), dma((2, 4)), dma((2, 4))]
-        + [dma((PLANE,))] * 8
-        + [dma((5,))],
+        + [dma((6, 4))] * 8
+        + [dma((2, 4)), dma((2, 4)), dma((2, 2, 4)), dma((2, 2, 4))]
+        + [dma((2, 4))] * 4
+        + [dma((2, 2, 4))] * 4
+        + [dma((PLANE,))] * 2
+        + [dma((8,))],
         compiler_params=pltpu.CompilerParams(
             collective_id=number, has_side_effects=True, vmem_limit_bytes=VMEM_LIMIT
         ),
@@ -1216,7 +1456,7 @@
     all_tokens,
     qkv_part,
     output_lines,
-    gateup_parts,
+    column_b,
     grad_hidden,
     gains_grad,
     token_grad,
@@ -1224,8 +1464,9 @@
     summed_b,
     output_parts,
     gains_sum,
-    own_kv,
-    stage,
+    across,
+    besides,
+    landed_kv,
     passing,
     dq_all,
     dkv_all,
@@ -1237,11 +1478,10 @@
     qkv_lines,
     qkv_parts,
     column_a,
-    column_b,
     gains_column,
     gains_plane,
-    stage_send,
-    stage_recv,
+    ring_send,
+    ring_recv,
     kv_send,
     kv_recv,
     dq_send,
@@ -1321,18 +1561,20 @@
     own_a = pltpu.make_async_copy(column_a.at[rank], summed_a.at[rank], own_sems.at[6])
     own_b = pltpu.make_async_copy(column_b.at[rank], summed_b.at[rank], own_sems.at[7])
 
-    def own_copy(j):
+    def ring(j, which):
         to_x = lax.rem(x + j, 4)
-        return pltpu.make_async_copy(dkv_mine.at[to_x * 4 + y], own_kv.at[j], own_sems.at[j])
-
-    def stage_copy(j, k):
-        to_x, to_y = lax.rem(x + j, 4), lax.rem(y + k, 4)
+        step = 1 if which in (1, 2) else 3
+        if which in (1, 3):
+            src, dst = besides.at[j, which // 2], landed_kv.at[j, which // 2]
+        else:
+            row_zh = 0 if which == 2 else 1
+            src, dst = dkv_mine.at[to_x * 4 + lax.rem(y + 2, 4), row_zh], across.at[j, row_zh]
         return pltpu.make_async_remote_copy(
-            src_ref=dkv_mine.at[to_x * 4 + to_y],
-            dst_ref=stage.at[k, j],
-            send_sem=stage_send.at[k, j],
-            recv_sem=stage_recv.at[k, j],
-            device_id=address(dict(me, y=to_y)),
+            src_ref=src,
+            dst_ref=dst,
+            send_sem=ring_send.at[j, which],
+            recv_sem=ring_recv.at[j, which],
+            device_id=address(dict(me, y=lax.rem(y + step, 4))),
             device_id_type=MESH,
         )
 
@@ -1348,36 +1590,36 @@
         )
 
     own_dq.start()
-    for j in (2, 1, 3, 0):
-        own_copy(j).start()
     greet_all(me, "all", "own")
     for j in (2, 1, 3, 0):
-        for k in (1, 3, 2):
-            stage_copy(j, k).start()
+        for which in (2, 0):
+            ring(j, which).start()
     queries.begin()
-    rows.begin()
-
-    for row_zh in range(2):
-
-        def add_part(s, total):
-            return total + gateup_parts[s, row_zh].astype(F32)
-
-        total = lax.fori_loop(0, PLANE, add_part, jnp.zeros((32, 768), F32))
-        column_b[pl.ds(row_zh * 4, 4)] = total.reshape(4, 8, 768)
+    for j in (2, 1, 3, 0):
+        to_x = lax.rem(x + j, 4)
+        for which, by_way, step in ((1, 2, 1), (3, 0, 3)):
+            row_zh, other = (0, 1) if by_way == 2 else (1, 0)
+            own_block = to_x * 4 + lax.rem(y + step, 4)
+            besides[j, which // 2, other] = dkv_mine[own_block, other]
+            ring(j, by_way).wait_recv()
+            both = dkv_mine[own_block, row_zh].astype(F32) + across[j, row_zh].astype(F32)
+            besides[j, which // 2, row_zh] = both.astype(BF16)
+            ring(j, which).start()
+
     own_b.start()
     to_b.begin()
 
     for j in (2, 1, 3, 0):
-        own_copy(j).wait()
-        total = own_kv[j].astype(F32)
-        for k in (1, 3, 2):
-            stage_copy(j, k).wait_recv()
-            total = total + stage[k, j].astype(F32)
+        total = dkv_mine[lax.rem(x + j, 4) * 4 + y].astype(F32)
+        for which in (1, 3):
+            ring(j, which).wait_recv()
+            total = total + landed_kv[j, which // 2].astype(F32)
         if j:
             passing[j] = total.astype(BF16)
             kv_copy(j, False).start()
         else:
             dkv_all[:, x] = total.astype(BF16)
+    rows.begin()
     own_dq.wait()
     queries.arrive()
     for j in (2, 1, 3):
@@ -1385,8 +1627,7 @@
 
     def project_back(i, carry):
         gain_q, gain_k = carry
-        back = 3 - i
-        off = back + lax.div(back, 2) * (5 - 2 * back)
+        off = gray(3 - i)
         to_z = lax.rem(z + off, 4)
         at = pl.ds(pl.multiple_of(to_z * 2 * ROWS, 2 * ROWS), 2 * ROWS)
         row_zh, first = lax.div(to_z, 2), lax.rem(to_z, 2) * 2
@@ -1409,10 +1650,9 @@
         grad_qkv[at, 384:] = grad_kv[:, HD:]
         sums.put(0, off, dot_nt(grad_qkv[at, :], qkv_part[...]))
 
-        @pl.when(i >= 1)
+        @pl.when(i == 1)
         def _():
-            last = back + 1
-            sums.pass_on(0, last + lax.div(last, 2) * (5 - 2 * last))
+            sums.first(0)
 
         return gain_q, gain_k
 
@@ -1427,6 +1667,7 @@
     gains_column[rank, 17:18, :] = gain_k
     gains_column[rank, 18:24, :] = jnp.zeros((6, HD), F32)
     gains_in.begin()
+    sums.second(0)
 
     def qkv_rows(j, carry):
         cols = pl.ds(pl.multiple_of(j * 256, 256), 256)
@@ -1462,8 +1703,8 @@
     rows.arrive()
     own_b.wait()
     for j in (2, 1, 3, 0):
-        for k in (1, 3, 2):
-            stage_copy(j, k).wait_send()
+        for which in range(4):
+            ring(j, which).wait_send()
         if j:
             kv_copy(j, False).wait_send()
     sums.drain(0)
@@ -1490,11 +1731,12 @@
             struct((PLANE, 16, D), BF16),
             struct((24, HD), F32),
         ),
-        in_specs=[anywhere, anywhere] + [vmem] * 6 + [anywhere] + [vmem] * 3,
+        in_specs=[anywhere, vmem] + [vmem] * 6 + [anywhere, anywhere] + [vmem] * 2,
         out_specs=(vmem, anywhere, anywhere, anywhere, vmem),
         scratch_shapes=[
             pltpu.VMEM((4,) + quarter_rows, BF16),
-            pltpu.VMEM((4, 4) + quarter_rows, BF16),
+            pltpu.VMEM((4, 2) + quarter_rows, BF16),
+            pltpu.VMEM((4, 2) + quarter_rows, BF16),
             pltpu.VMEM((4,) + quarter_rows, BF16),
             pltpu.VMEM((2, 4, ROWS, 256), BF16),
             pltpu.VMEM((2, 4, ROWS, 256), BF16),
@@ -1506,7 +1748,6 @@
             pltpu.VMEM((2, PLANE, 32, 512), BF16),
             pltpu.VMEM((PLANE, 2, 32, 512), BF16),
             pltpu.VMEM((RANKS, 8, 512), F32),
-            pltpu.VMEM((RANKS, 8, 768), F32),
             pltpu.VMEM((RANKS, 24, HD), F32),
             pltpu.VMEM((PLANE, 24, HD), F32),
         ]
@@ -1591,6 +1832,7 @@
         q_mine,
         kv_mine,
         all_tokens,
+        down_low,
         output_wide,
         gateup_low,
         extras,
@@ -1606,6 +1848,7 @@
         sent_b,
         inputs,
         output_weight.astype(BF16),
+        jnp.concatenate([down_weight[:, :512], down_weight[:, 512:]], axis=0).astype(BF16),
         jnp.concatenate([frequency, frequency])[None],
     )
     gains_all = gains_low.reshape(-1, 8, HD)[:, 0, :18].reshape(-1).astype(F32)
@@ -1628,12 +1871,12 @@
     def from_pack_x(ref, frm):
         return ref.at[:, frm["x"]]
 
-    result, grad_hidden, gains_grad, grad_mine, gateup_parts, down_parts, output_lines = middle(
+    result, grad_hidden, gains_grad, grad_mine, gateup_sum, down_parts, output_lines = middle(
         2,
         out_mine.reshape(4, 2, ROWS, 256),
         output_wide.reshape(256, D),
         gateup_low,
-        jnp.concatenate([down_weight[:, :512], down_weight[:, 512:]], axis=0).astype(BF16),
+        down_low,
         inputs,
         cotangent[0],
         jnp.stack([attn_gain, ffn_gain]),
@@ -1652,7 +1895,7 @@
         all_tokens,
         qkv_part,
         output_lines,
-        gateup_parts,
+        gateup_sum.reshape(RANKS, 8, 768),
         grad_hidden,
         gains_grad,
     )
@@ -1660,14 +1903,14 @@
         gains_total.reshape(-1), lax.axis_index(AXES) * norm_gains.shape[0], norm_gains.shape[0]
     )
     output_sum = jnp.sum(output_parts.astype(F32), axis=0)
-    down_wide = jnp.sum(down_parts.astype(F32), axis=0)
-    down_sum = jnp.concatenate([down_wide[:24], down_wide[24:]], axis=1)
+    down_sides = jnp.sum(down_parts.astype(F32), axis=0)
+    down_sum = jnp.concatenate([down_sides[:24], down_sides[24:]], axis=1)
     wide_a, wide_b = summed_a.transpose(1, 0, 2), summed_b.transpose(1, 0, 2)
     query_sum = wide_a[:, :, :256].reshape(8, 2048)
     keyval_sum = jnp.concatenate(
         [wide_a[:, :, 256:384].reshape(8, KV), wide_a[:, :, 384:].reshape(8, KV)], axis=1
     )
-    gateup_sum = jnp.concatenate(
+    gateup_total = jnp.concatenate(
         [wide_b[:, :, :384].reshape(8, FF), wide_b[:, :, 384:].reshape(8, FF)], axis=1
     )
 
@@ -1681,7 +1924,7 @@
         output_weight, output_sum, output_mean, output_square, RATE_MATRIX, DECAY
     )
     gateup_new, gateup_mean_new, gateup_square_new = adam_update(
-        gateup_weight, gateup_sum, gateup_mean, gateup_square, RATE_MATRIX, DECAY
+        gateup_weight, gateup_total, gateup_mean, gateup_square, RATE_MATRIX, DECAY
     )
     down_new, down_mean_new, down_square_new = adam_update(
         down_weight, down_sum, down_mean, down_square, RATE_MATRIX, DECAY
@@ -1695,7 +1938,7 @@
         query_sum,
         keyval_sum,
         output_sum,
-        gateup_sum,
+        gateup_total,
         down_sum,
         gains_sum,
         query_new,

time: 359 us -> 328 us (0.914)
  Pallas kernels: 341 us -> 306 us
    pallas_call x1, Pallas kernels: 142 us -> 121 us  [middle(): pl.pallas_call(middle_kernel, out_shape=(jax.ShapeDtypeStruct(block, BF16...]
    pallas_call x1, Pallas kernels: 73.2 us -> 61.6 us  [start(): pl.pallas_call(start_kernel, out_shape=(struct((4, 2, ROWS, 256), BF16),...]
    pallas_call x1, Pallas kernels: 77.2 us -> 66.2 us  [end(): pl.pallas_call(end_kernel, out_shape=(struct(block, F32), struct((RANKS,...]
    pallas_call x1, Pallas kernels: 27.6 us -> 31.7 us  [attend_back(): pl.pallas_call(attend_back_kernel, out_shape=(jax.ShapeDtypeStruct(q.shap...]
    pallas_call x1, Pallas kernels: 20.9 us -> 24.9 us  [attend(): pl.pallas_call(attend_kernel, out_shape=(jax.ShapeDtypeStruct(q.shape, BF...]
where the time goes in v4:
time: 328 us; the launch traced here: 327 us
  Pallas kernels  306 us (93%)
  local copies, waits for them, and re-layouts  10.7 us (3%)
  other arithmetic  9.47 us (3%)
    pallas_call x1, Pallas kernels, middle(): pl.pallas_call(middle_kernel, out_shape=(jax.ShapeDtypeStruct(block, BF16...  121 us
    pallas_call x1, Pallas kernels, end(): pl.pallas_call(end_kernel, out_shape=(struct(block, F32), struct((RANKS,...  66.2 us
    pallas_call x1, Pallas kernels, start(): pl.pallas_call(start_kernel, out_shape=(struct((4, 2, ROWS, 256), BF16),...  61.6 us
    pallas_call x1, Pallas kernels, attend_back(): pl.pallas_call(attend_back_kernel, out_shape=(jax.ShapeDtypeStruct(q.shap...  31.7 us
    pallas_call x1, Pallas kernels, attend(): pl.pallas_call(attend_kernel, out_shape=(jax.ShapeDtypeStruct(q.shape, BF...  24.9 us
    unnamed x57, local copies, waits for them, and re-layouts  6.94 us

profile of v4, /device:TPU:1, one launch (start us, length us, event | category | flops | bytes accessed | tf_op | source)
XLA Modules:
  0.0 327.0 jit_solution(9567221085861984888)
XLA Ops:
  0.7 0.8 add_reduce_fusion
  2.7 0.8 slice_bitcast_fusion.3
  3.5 0.9 maximum_bitcast_fusion.1.sent_a
  4.3 1.0 fusion.15
  5.3 0.9 convert.7
  6.2 0.8 convert_element_type.35.output_rows
  7.2 61.6 %start.1 = (bf16[4,2,128,256]{3,2,1,0:T(8,128)(2,1)S(1)}, bf16[16,2,128,256]{3,2,1,0:T(8,128)(2,1)}, bf16[8,128,1024]{2,1,0:T(8,128)(2,1)}, bf16[48,512]{1,0:T(8...) custom-call(f32[8,8,640]{2,1,0:T(8,128)S(1)} %maximum_bitcast_fusion, ...), custom_call_target="tpu_custom_call" | custom-call | tf_op jit(solution)/shard_map/start/pallas_call | solution.py:1051
  68.7 0.8 copy-done.4
  70.5 1.6 copy-done.3
  72.1 1.0 copy-done.5
  73.1 24.9 %attend.1 = (bf16[1024,256]{1,0:T(8,128)(2,1)S(1)}, f32[16,128]{1,0:T(8,128)S(1)}) custom-call(s32[16]{0:T(128)S(1)} %reshape.138.q_blocks, s32[64]{0:T(128)S(1)} %reshape.139.k_blocks, bf16[1024,256]{1,0:T(8,128)(2,1)S(1)} %bitcast.77, bf16[4096,256]{1,0:T(8,128)(2,1)S(1)} %bitcast.76), custom_call_target="tpu_custom_call" | custom-call | flops 4000000000 | bytes 4000000 | tf_op jit(solution)/shard_map/attend/pallas_call | solution.py:159
  98.3 121.3 %middle.1 = (bf16[128,1024]{1,0:T(8,128)(2,1)S(1)}, f32[128,1024]{1,0:T(8,128)S(1)}, f32[2,1024]{1,0:T(2,128)S(1)}, bf16[4,2,128,256]{3,2,1,0:T(8,128)(2,1)S(1)}...) custom-call(bf16[4,2,128,256]{3,2,1,0:T(8,128)(2,1)S(1)} %bitcast.66, ...), custom_call_target="tpu_custom_call" | custom-call | tf_op jit(solution)/shard_map/middle/pallas_call | solution.py:1400
  219.6 0.8 copy-done.1
  220.4 1.3 convert_reduce_fusion
  221.7 0.8 multiply_subtract_fusion.1
  222.4 1.0 copy-done.6
  223.5 31.7 %attend_back.1 = (bf16[1024,256]{1,0:T(8,128)(2,1)S(1)}, bf16[4096,256]{1,0:T(8,128)(2,1)}) custom-call(s32[16]{0:T(128)S(1)} %reshape.138.q_blocks, s32[64]{0:T(128)S(1)} %reshape.139.k_blocks, bf16[1024,256]{1,0:T(8,128)(2,1)S(1)} %bitcast.78, bf16[4096,256]{1,0:T(8,128)(2,1)} %bitcast.75, bf16[1024,256]{1,0:T(8,128)(2,1)S(1)} %bitcast.79, ...), custom_call_target="tpu_custom_call" | custom-call | flops 10000000000 | bytes 8000000 | tf_op jit(solution)/shard_map/attend_back/pallas_call | solution.py:259
  255.2 66.2 %end.1 = (f32[128,1024]{1,0:T(8,128)S(1)}, f32[8,8,512]{2,1,0:T(8,128)S(1)}, f32[8,8,768]{2,1,0:T(8,128)S(1)}, bf16[16,16,1024]{2,1,0:T(8,128)(2,1)S(1)}, f32[24,128]{1,0:T(8,128)S(1)}) custom-call(bf16[4,2,128,256]{3,2,1,0:T(8,128)(2,1)S(1)} %bitcast.63, bf16[16,2,128,256]{3,2,1,0:T(8,128)(2,1)} %bitcast.80, f32[1024,384]{1,0:T(8,128)} %get-tuple-element.68.projected, ...), custom_call_target="tpu_custom_call" | custom-call | tf_op jit(solution)/shard_map/end/pallas_call | solution.py:1725
  321.6 0.9 multiply_subtract_fusion
  322.5 0.7 multiply_subtract_fusion.3
  323.3 0.7 multiply_subtract_fusion.4
  324.1 0.7 multiply_subtract_fusion.2
  325.5 0.7 copy.73
  326.2 0.8 copy.74
  (84 shorter events, 3.3 us)
Async XLA Ops:
  0.7 6.5 %copy-start = (bf16[1,128,1024]{2,1,0:T(8,128)(2,1)S(1)}, bf16[1,128,1024]{2,1,0:T(8,128)(2,1)}, u32[]{:S(2)}) copy-start(bf16[1,128,1024]{2,1,0:T(8,128)(2,1)} %param.22) | copy-start | bytes 786436
  70.5 1.6 copy-start.3
  72.1 1.0 copy-start.5
  73.1 25.1 %copy-start.2 = (bf16[1,128,1024]{2,1,0:T(8,128)(2,1)S(1)}, bf16[1,128,1024]{2,1,0:T(8,128)(2,1)}, u32[]{:S(2)}) copy-start(bf16[1,128,1024]{2,1,0:T(8,128)(2,1)} %param.23) | copy-start | bytes 786436
  98.0 123.6 %copy-start.8 = (f32[24,1024]{1,0:T(8,128)S(1)}, f32[24,1024]{1,0:T(8,128)}, u32[]{:S(2)}) copy-start(f32[24,1024]{1,0:T(8,128)} %param.30) | copy-start | bytes 294916
  98.0 123.6 %copy-start.16 = (f32[24,1024]{1,0:T(8,128)S(1)}, f32[24,1024]{1,0:T(8,128)}, u32[]{:S(2)}) copy-start(f32[24,1024]{1,0:T(8,128)} %param.36) | copy-start | bytes 294916
  98.0 123.6 %copy-start.17 = (f32[24,1024]{1,0:T(8,128)S(1)}, f32[24,1024]{1,0:T(8,128)}, u32[]{:S(2)}) copy-start(f32[24,1024]{1,0:T(8,128)} %param.42) | copy-start | bytes 294916
  255.2 66.4 %copy-start.7 = (f32[8,6144]{1,0:T(8,128)S(1)}, f32[8,6144]{1,0:T(8,128)}, u32[]{:S(2)}) copy-start(f32[8,6144]{1,0:T(8,128)} %param.29) | copy-start | bytes 589828
  255.2 66.4 %copy-start.14 = (f32[8,6144]{1,0:T(8,128)S(1)}, f32[8,6144]{1,0:T(8,128)}, u32[]{:S(2)}) copy-start(f32[8,6144]{1,0:T(8,128)} %param.35) | copy-start | bytes 589828
  255.2 66.4 %copy-start.15 = (f32[8,6144]{1,0:T(8,128)S(1)}, f32[8,6144]{1,0:T(8,128)}, u32[]{:S(2)}) copy-start(f32[8,6144]{1,0:T(8,128)} %param.41) | copy-start | bytes 589828
  321.4 1.1 copy-start.13
  321.4 1.1 copy-start.22
  321.4 1.1 copy-start.23
  321.4 1.8 copy-start.9
  321.4 1.8 copy-start.18
  321.5 1.8 copy-start.19
  321.5 2.6 copy-start.11
  321.5 2.6 copy-start.20
  321.5 2.6 copy-start.21
  321.5 3.3 %copy-start.24 = (f32[18]{0:T(128)S(1)}, f32[18]{0:T(128)}, u32[]{:S(2)}) copy-start(f32[18]{0:T(128)} %param.31) | copy-start | bytes 220
  321.5 3.3 %copy-start.25 = (f32[18]{0:T(128)S(1)}, f32[18]{0:T(128)}, u32[]{:S(2)}) copy-start(f32[18]{0:T(128)} %param.37) | copy-start | bytes 220
  321.5 3.3 %copy-start.26 = (f32[18]{0:T(128)S(1)}, f32[18]{0:T(128)}, u32[]{:S(2)}) copy-start(f32[18]{0:T(128)} %param.43) | copy-start | bytes 220
  323.3 3.7 %copy-start.12 = (f32[8,8,256]{2,0,1:T(8,128)}, f32[8,8,256]{2,0,1:T(8,128)S(1)}, u32[]{:S(2)}) copy-start(f32[8,8,256]{2,0,1:T(8,128)S(1)} %slice.80) | copy-start | bytes 196612
  324.1 2.8 copy-start.10
  (3 other events, 2.6 us)

commit v5 on v4

--- a/solution.py
+++ b/solution.py
@@ -451,25 +451,11 @@
     return dict(place, zl=lax.div(t, 2), co=lax.rem(t, 2))
 
 
-def row_user(me, k):
-    return at_quarter(shifted(me, SURFACE, k, 1), me["x"])
-
-
-def row_owner(me, k):
-    y, t = lax.div(k, 4), lax.rem(k, 4)
-    to = dict(me, x=quarter(me), y=lax.rem(me["y"] + y, 4))
-    return at_quarter(to, lax.rem(quarter(me) + t, 4))
-
-
-def row_slot(owner):
-    return owner["y"] * 4 + quarter(owner)
-
-
 def greet(barrier, place):
     pl.semaphore_signal(barrier, inc=1, device_id=address(place), device_id_type=MESH)
 
 
-def greet_all(me, column, rows):
+def greet_all(me, column, swap):
     barrier = pltpu.get_barrier_semaphore()
 
     def greet_surface(k, carry):
@@ -491,29 +477,14 @@
             greet(barrier, column_place(me, lax.rem(z + off, 4), me["co"]))
         greet(barrier, column_place(me, z, 1 - me["co"]))
         expected = expected + 4
-    at_home = me["x"] == quarter(me)
-    if rows == "swap":
+    if swap:
+        at_home = me["x"] == quarter(me)
 
         @pl.when(jnp.logical_not(at_home))
         def _():
             greet(barrier, swap_partner(me))
 
         expected = expected + 1 - jnp.where(at_home, 1, 0)
-    elif rows is not None:
-
-        def greet_rows(k, carry):
-            @pl.when(jnp.logical_not(jnp.logical_and(k == 0, at_home)))
-            def _():
-                if rows != "own":
-                    greet(barrier, row_owner(me, k))
-                if rows != "use":
-                    greet(barrier, row_user(me, k))
-
-            return carry
-
-        lax.fori_loop(0, PLANE, greet_rows, 0)
-        count = PLANE - jnp.where(at_home, 1, 0)
-        expected = expected + (2 * count if rows == "both" else count)
     pl.semaphore_wait(barrier, expected)
 
 
@@ -553,65 +524,6 @@
             copy.wait_send()
 
         self.either(both, lambda: self.own().wait())
-
-
-class RowCopies:
-    def __init__(self, me, src, dst, send, recv, back):
-        self.me, self.src, self.dst, self.send, self.recv, self.back = me, src, dst, send, recv, back
-        self.at_home = me["x"] == quarter(me)
-
-    def copy(self, k, arriving):
-        me = self.me
-        if self.back:
-            to = row_owner(me, k)
-            frm = row_user(me, k) if arriving else me
-            src, slot = self.src.at[row_slot(to)], flat_index(frm, SURFACE)
-        else:
-            to = row_user(me, k)
-            frm = row_owner(me, k) if arriving else me
-            src, slot = self.src, row_slot(frm)
-        return pltpu.make_async_remote_copy(
-            src_ref=src,
-            dst_ref=self.dst.at[slot],
-            send_sem=self.send.at[k],
-            recv_sem=self.recv.at[slot],
-            device_id=address(to),
-            device_id_type=MESH,
-        )
-
-    def own(self):
-        me = self.me
-        if self.back:
-            src, slot = self.src.at[row_slot(me)], flat_index(me, SURFACE)
-        else:
-            src, slot = self.src, row_slot(me)
-        return pltpu.make_async_copy(src, self.dst.at[slot], self.recv.at[slot])
-
-    def each(self, remote, own):
-        def one(j, carry):
-            k = lax.rem(j * 7, PLANE)
-            itself = jnp.logical_and(k == 0, self.at_home)
-
-            @pl.when(itself)
-            def _():
-                own()
-
-            @pl.when(jnp.logical_not(itself))
-            def _():
-                remote(k)
-
-            return carry
-
-        lax.fori_loop(0, PLANE, one, 0)
-
-    def begin(self):
-        self.each(lambda k: self.copy(k, False).start(), lambda: self.own().start())
-
-    def arrive(self):
-        self.each(lambda k: self.copy(k, True).wait_recv(), lambda: self.own().wait())
-
-    def drain(self):
-        self.each(lambda k: self.copy(k, False).wait_send(), lambda: None)
 
 
 class Exchange:
@@ -844,7 +756,7 @@
     own_b = pltpu.make_async_copy(sent_b.at[rank], shares_b.at[rank], own_sems.at[1])
     own_a.start()
     own_b.start()
-    greet_all(me, "all", "swap")
+    greet_all(me, "all", True)
     to_a.begin()
     output_swap.begin()
     gathers.begin(0, tokens[...])
@@ -1100,7 +1012,7 @@
     gains_grad,
     grad_mine,
     gateup_sum,
-    down_parts,
+    down_sum,
     output_lines,
     attended,
     blocks,
@@ -1123,6 +1035,9 @@
     got,
     plane_sums,
     got_last,
+    d_got,
+    d_sums,
+    d_got_last,
     near_send,
     near_recv,
     far_send,
@@ -1145,10 +1060,12 @@
     row_recv,
     down_send,
     down_recv,
+    dlast_send,
+    dlast_recv,
     own_sems,
 ):
     me = where_am_i()
-    x, here = me["x"], flat_index(me, SURFACE)
+    x = me["x"]
     z = me["zh"] * 2 + me["zl"]
     sums = ColumnSums(
         me, part, paired, sending, landed, near_send, near_recv, far_send, far_recv
@@ -1179,7 +1096,9 @@
         row_send,
         row_recv,
     )
-    rows_back = RowCopies(me, down_lines, down_parts, down_send, down_recv, True)
+    down_back = PlaneSums(
+        me, down_lines, d_got, d_sums, d_got_last, down_send, down_recv, dlast_send, dlast_recv
+    )
     gateup_back = PlaneSums(
         me, gateup_lines, got, plane_sums, got_last, plane_send, plane_recv, last_send, last_recv
     )
@@ -1206,7 +1125,7 @@
 
     for half in range(2):
         own_out(half).start()
-    greet_all(me, "some", "own")
+    greet_all(me, "some", False)
     for half in range(2):
         for k in (2, 1, 3):
             attention_out(half, k, False).start()
@@ -1310,14 +1229,17 @@
 
     def down_line(s, carry):
         rows = down_grad[pl.ds(pl.multiple_of(s * 24, 8), 24), :].astype(BF16)
-        down_lines[s, 0:24, :] = rows[:, :512]
-        down_lines[s, 24:48, :] = rows[:, 512:]
+        at_y, at_x = lax.div(s, 4), lax.rem(s, 4)
+        for half in range(2):
+            for side in range(2):
+                cols = slice(side * 512 + half * 256, side * 512 + half * 256 + 256)
+                down_lines[half, at_x, at_y, side * 24 : side * 24 + 24, :] = rows[:, cols]
         return carry
 
     def send_down():
         down_grad[...] = dot_tn(activated[...], all_rows(2))
         lax.fori_loop(0, PLANE, down_line, 0)
-        rows_back.begin()
+        down_back.begin()
 
     def send_gateup():
         grads = dot_tn(all_rows(0), grad_gate[...])
@@ -1344,6 +1266,7 @@
         gathers.pass_on(phase)
         sums.second(phase + 1)
         if stage == 2:
+            down_back.pass_on()
             send_gateup()
         gathers.await_all(phase)
         if stage == 0:
@@ -1359,11 +1282,15 @@
         gathers.pass_on(phase + 1)
         if stage < 2:
             sums.second(phase + 2)
+        if stage == 2:
+            gateup_back.pass_on()
         gathers.await_all(phase + 1)
     works[3](1)
-    gateup_back.pass_on()
     grads = dot_tn(attended[...].reshape(RANKS * ROWS, 256), all_rows(4))
-    output_lines[...] = grads.astype(BF16).reshape(PLANE, 16, D)
+    for line in range(PLANE):
+        rows = grads[line * 16 : line * 16 + 16].astype(BF16)
+        for half in range(2):
+            output_lines[half, line % 4, line // 4] = rows[:, half * 512 : half * 512 + 512]
 
     for half in range(2):
         for k in (1, 3, 2):
@@ -1386,9 +1313,9 @@
         sums.drain(phase)
         gathers.drain(phase)
     for half in range(2):
+        down_sum[:, half * 256 : half * 256 + 256] = down_back.total(half)
         gateup_sum[half] = gateup_back.total(half)
-    rows_back.arrive()
-    for exchange in (spread, gateup_back, rows_back):
+    for exchange in (spread, gateup_back, down_back):
         exchange.drain()
 
 
@@ -1405,11 +1332,11 @@
             jax.ShapeDtypeStruct((2, D), F32),
             jax.ShapeDtypeStruct((4, 2, ROWS, 256), BF16),
             jax.ShapeDtypeStruct((2, 32, 768), F32),
-            jax.ShapeDtypeStruct((PLANE, 48, 512), BF16),
-            jax.ShapeDtypeStruct((PLANE, 16, D), BF16),
+            jax.ShapeDtypeStruct((48, 512), F32),
+            jax.ShapeDtypeStruct((2, 4, 4, 16, 512), BF16),
         ),
         in_specs=[anywhere, vmem, anywhere, anywhere, vmem, vmem, vmem],
-        out_specs=(vmem, vmem, vmem, anywhere, vmem, anywhere, vmem),
+        out_specs=(vmem, vmem, vmem, anywhere, vmem, vmem, vmem),
         scratch_shapes=[
             pltpu.VMEM((2, 2, 4, BLOCK, 256), BF16),
             pltpu.VMEM((6, RANKS) + half, BF16),
@@ -1423,7 +1350,7 @@
             pltpu.VMEM((2, 2, 4, BLOCK, 256), BF16),
             pltpu.VMEM((2, 4, 4, 32, 768), BF16),
             pltpu.VMEM((384, D), F32),
-            pltpu.VMEM((PLANE, 48, 512), BF16),
+            pltpu.VMEM((2, 4, 4, 48, 256), BF16),
             pltpu.VMEM(block, F32),
             pltpu.VMEM(block, F32),
             pltpu.VMEM((2, 4, 4, 32, 768), BF16),
@@ -1432,12 +1359,15 @@
             pltpu.VMEM((2, 4, 4, 32, 768), BF16),
             pltpu.VMEM((2, 4, 32, 768), BF16),
             pltpu.VMEM((2, 4, 32, 768), BF16),
+            pltpu.VMEM((2, 4, 4, 48, 256), BF16),
+            pltpu.VMEM((2, 4, 48, 256), BF16),
+            pltpu.VMEM((2, 4, 48, 256), BF16),
         ]
         + [dma((6, 4))] * 8
         + [dma((2, 4)), dma((2, 4)), dma((2, 2, 4)), dma((2, 2, 4))]
         + [dma((2, 4))] * 4
         + [dma((2, 2, 4))] * 4
-        + [dma((PLANE,))] * 2
+        + [dma((2, 4))] * 4
         + [dma((8,))],
         compiler_params=pltpu.CompilerParams(
             collective_id=number, has_side_effects=True, vmem_limit_bytes=VMEM_LIMIT
@@ -1456,13 +1386,15 @@
     all_tokens,
     qkv_part,
     output_lines,
+    down_total,
     column_b,
     grad_hidden,
     gains_grad,
     token_grad,
     summed_a,
     summed_b,
-    output_parts,
+    output_sum,
+    down_sum,
     gains_sum,
     across,
     besides,
@@ -1476,7 +1408,13 @@
     sending,
     landed,
     qkv_lines,
-    qkv_parts,
+    q_got,
+    q_sums,
+    q_got_last,
+    o_got,
+    o_sums,
+    o_got_last,
+    output_total,
     column_a,
     gains_column,
     gains_plane,
@@ -1492,10 +1430,15 @@
     far_recv,
     plane_send,
     plane_recv,
+    qlast_send,
+    qlast_recv,
+    row_send,
+    row_recv,
+    olast_send,
+    olast_recv,
     gplane_send,
     gplane_recv,
-    row_send,
-    row_recv,
+    swap_sems,
     a_send,
     a_recv,
     b_send,
@@ -1539,13 +1482,8 @@
         gplane_send,
         gplane_recv,
     )
-    plane = Exchange(
-        me,
-        SURFACE,
-        lambda to: qkv_lines.at[:, flat_index(to, SURFACE)],
-        lambda frm: qkv_parts.at[flat_index(frm, SURFACE)],
-        plane_send,
-        plane_recv,
+    qkv_back = PlaneSums(
+        me, qkv_lines, q_got, q_sums, q_got_last, plane_send, plane_recv, qlast_send, qlast_recv
     )
     queries = Exchange(
         me,
@@ -1555,9 +1493,12 @@
         dq_send,
         dq_recv,
     )
-    rows = RowCopies(me, output_lines, output_parts, row_send, row_recv, True)
+    output_back = PlaneSums(
+        me, output_lines, o_got, o_sums, o_got_last, row_send, row_recv, olast_send, olast_recv
+    )
+    output_swap = Swap(me, output_total, output_sum, output_sum, swap_sems.at[0])
+    down_swap = Swap(me, down_total, down_sum, down_sum, swap_sems.at[1])
     own_dq = pltpu.make_async_copy(dq_mine.at[x], dq_all.at[:, x], own_sems.at[4])
-    own_plane = pltpu.make_async_copy(qkv_lines.at[:, here], qkv_parts.at[here], own_sems.at[5])
     own_a = pltpu.make_async_copy(column_a.at[rank], summed_a.at[rank], own_sems.at[6])
     own_b = pltpu.make_async_copy(column_b.at[rank], summed_b.at[rank], own_sems.at[7])
 
@@ -1590,11 +1531,12 @@
         )
 
     own_dq.start()
-    greet_all(me, "all", "own")
+    greet_all(me, "all", True)
     for j in (2, 1, 3, 0):
         for which in (2, 0):
             ring(j, which).start()
     queries.begin()
+    down_swap.begin()
     for j in (2, 1, 3, 0):
         to_x = lax.rem(x + j, 4)
         for which, by_way, step in ((1, 2, 1), (3, 0, 3)):
@@ -1619,7 +1561,7 @@
             kv_copy(j, False).start()
         else:
             dkv_all[:, x] = total.astype(BF16)
-    rows.begin()
+    output_back.begin()
     own_dq.wait()
     queries.arrive()
     for j in (2, 1, 3):
@@ -1668,39 +1610,37 @@
     gains_column[rank, 18:24, :] = jnp.zeros((6, HD), F32)
     gains_in.begin()
     sums.second(0)
+    output_back.pass_on()
 
     def qkv_rows(j, carry):
         cols = pl.ds(pl.multiple_of(j * 256, 256), 256)
         grads = dot_tn(all_tokens[:, :, cols].reshape(RANKS * ROWS, 256), grad_qkv[...])
-        qkv_lines[lax.div(j, 2), pl.ds(lax.rem(j, 2) * 8, 8)] = grads.astype(BF16).reshape(
-            8, 32, 512
+        qkv_lines[lax.div(j, 2), pl.ds(lax.rem(j, 2) * 2, 2)] = grads.astype(BF16).reshape(
+            2, 4, 32, 512
         )
         return carry
 
     lax.fori_loop(0, 4, qkv_rows, 0)
-    own_plane.start()
-    plane.begin()
+    qkv_back.begin()
 
     gains_in.arrive()
     gains_plane[here] = jnp.sum(gains_column[...], axis=0)
     gains_over.begin()
     token_grad[...] = grad_hidden[...] + sums.total(0)
-
-    own_plane.wait()
-    plane.arrive()
-    for row_zh in range(2):
-
-        def add_qkv(s, total):
-            return total + qkv_parts[s, row_zh].astype(F32)
-
-        total = lax.fori_loop(0, PLANE, add_qkv, jnp.zeros((32, 512), F32))
-        column_a[pl.ds(row_zh * 4, 4)] = total.reshape(4, 8, 512)
+    qkv_back.pass_on()
+    for half in range(2):
+        output_total[:, half * 512 : half * 512 + 512] = output_back.total(half)
+    output_swap.begin()
+
+    for half in range(2):
+        column_a[pl.ds(half * 4, 4)] = qkv_back.total(half).reshape(4, 8, 512)
     own_a.start()
     to_a.begin()
     gains_over.arrive()
     gains_sum[...] = jnp.sum(gains_plane[...], axis=0)
     to_b.arrive()
-    rows.arrive()
+    output_swap.finish()
+    down_swap.finish()
     own_b.wait()
     for j in (2, 1, 3, 0):
         for which in range(4):
@@ -1708,7 +1648,7 @@
         if j:
             kv_copy(j, False).wait_send()
     sums.drain(0)
-    for exchange in (queries, rows, to_b, gains_in, gains_over, plane):
+    for exchange in (queries, output_back, to_b, gains_in, gains_over, qkv_back):
         exchange.drain()
     own_a.wait()
     to_a.arrive()
@@ -1728,11 +1668,12 @@
             struct(block, F32),
             struct((RANKS, 8, 512), F32),
             struct((RANKS, 8, 768), F32),
-            struct((PLANE, 16, D), BF16),
+            struct((16, D), F32),
+            struct((48, 512), F32),
             struct((24, HD), F32),
         ),
-        in_specs=[anywhere, vmem] + [vmem] * 6 + [anywhere, anywhere] + [vmem] * 2,
-        out_specs=(vmem, anywhere, anywhere, anywhere, vmem),
+        in_specs=[anywhere, vmem] + [vmem] * 6 + [vmem, anywhere, anywhere] + [vmem] * 2,
+        out_specs=(vmem, anywhere, anywhere, anywhere, anywhere, vmem),
         scratch_shapes=[
             pltpu.VMEM((4,) + quarter_rows, BF16),
             pltpu.VMEM((4, 2) + quarter_rows, BF16),
@@ -1745,8 +1686,14 @@
             pltpu.VMEM((1, 4) + block, BF16),
             pltpu.VMEM((1, 4) + block, BF16),
             pltpu.VMEM((1, 4) + block, BF16),
-            pltpu.VMEM((2, PLANE, 32, 512), BF16),
-            pltpu.VMEM((PLANE, 2, 32, 512), BF16),
+            pltpu.VMEM((2, 4, 4, 32, 512), BF16),
+            pltpu.VMEM((2, 4, 4, 32, 512), BF16),
+            pltpu.VMEM((2, 4, 32, 512), BF16),
+            pltpu.VMEM((2, 4, 32, 512), BF16),
+            pltpu.VMEM((2, 4, 4, 16, 512), BF16),
+            pltpu.VMEM((2, 4, 16, 512), BF16),
+            pltpu.VMEM((2, 4, 16, 512), BF16),
+            pltpu.VMEM((16, D), F32),
             pltpu.VMEM((RANKS, 8, 512), F32),
             pltpu.VMEM((RANKS, 24, HD), F32),
             pltpu.VMEM((PLANE, 24, HD), F32),
@@ -1754,7 +1701,9 @@
         + [dma((4, 4))] * 2
         + [dma((4,))] * 4
         + [dma((1, 4))] * 4
-        + [dma((PLANE,))] * 6
+        + [dma((2, 4))] * 8
+        + [dma((PLANE,))] * 2
+        + [dma((2, 2))]
         + [dma((RANKS,))] * 6
         + [dma((8,))],
         compiler_params=pltpu.CompilerParams(
@@ -1871,7 +1820,7 @@
     def from_pack_x(ref, frm):
         return ref.at[:, frm["x"]]
 
-    result, grad_hidden, gains_grad, grad_mine, gateup_sum, down_parts, output_lines = middle(
+    result, grad_hidden, gains_grad, grad_mine, gateup_sum, down_total, output_lines = middle(
         2,
         out_mine.reshape(4, 2, ROWS, 256),
         output_wide.reshape(256, D),
@@ -1884,7 +1833,7 @@
     dq_mine, dkv_mine = attend_back(
         query_blocks, key_blocks, q_mine, kv_mine, grad_mine.reshape(1024, 256), out_mine, lse
     )
-    token_grad, summed_a, summed_b, output_parts, gains_total = end(
+    token_grad, summed_a, summed_b, output_sum, down_sides, gains_total = end(
         3,
         dq_mine.reshape(4, 2, ROWS, 256),
         dkv_mine.reshape(PLANE, 2, ROWS, 256),
@@ -1895,6 +1844,7 @@
         all_tokens,
         qkv_part,
         output_lines,
+        down_total,
         gateup_sum.reshape(RANKS, 8, 768),
         grad_hidden,
         gains_grad,
@@ -1902,8 +1852,6 @@
     gains_sum = lax.dynamic_slice_in_dim(
         gains_total.reshape(-1), lax.axis_index(AXES) * norm_gains.shape[0], norm_gains.shape[0]
     )
-    output_sum = jnp.sum(output_parts.astype(F32), axis=0)
-    down_sides = jnp.sum(down_parts.astype(F32), axis=0)
     down_sum = jnp.concatenate([down_sides[:24], down_sides[24:]], axis=1)
     wide_a, wide_b = summed_a.transpose(1, 0, 2), summed_b.transpose(1, 0, 2)
     query_sum = wide_a[:, :, :256].reshape(8, 2048)

time: 328 us -> 298 us (0.909)
  Pallas kernels: 306 us -> 280 us
    pallas_call x1, Pallas kernels: 121 us -> 106 us  [middle(): pl.pallas_call(middle_kernel, out_shape=(jax.ShapeDtypeStruct(block, BF16...]
    pallas_call x1, Pallas kernels: 66.2 us -> 59.8 us  [end(): pl.pallas_call(end_kernel, out_shape=(struct(block, F32), struct((RANKS,...]
    unnamed x57 -> x48, local copies, waits for them, and re-layouts: 6.94 us -> 3.9 us
where the time goes in v5:
time: 298 us; the launch traced here: 297 us
  Pallas kernels  280 us (94%)
  other arithmetic  8.09 us (3%)
  local copies, waits for them, and re-layouts  7.7 us (3%)
    pallas_call x1, Pallas kernels, middle(): pl.pallas_call(middle_kernel, out_shape=(jax.ShapeDtypeStruct(block, BF16...  106 us
    pallas_call x1, Pallas kernels, start(): pl.pallas_call(start_kernel, out_shape=(struct((4, 2, ROWS, 256), BF16),...  61.6 us
    pallas_call x1, Pallas kernels, end(): pl.pallas_call(end_kernel, out_shape=(struct(block, F32), struct((RANKS,...  59.8 us
    pallas_call x1, Pallas kernels, attend_back(): pl.pallas_call(attend_back_kernel, out_shape=(jax.ShapeDtypeStruct(q.shap...  29.8 us
    pallas_call x1, Pallas kernels, attend(): pl.pallas_call(attend_kernel, out_shape=(jax.ShapeDtypeStruct(q.shape, BF...  23 us

profile of v5, /device:TPU:1, one launch (start us, length us, event | category | flops | bytes accessed | tf_op | source)
XLA Modules:
  0.0 296.6 jit_solution(4608320481852390981)
XLA Ops:
  0.9 0.8 add_reduce_fusion
  2.0 0.7 pad_bitcast_fusion
  2.7 0.8 convert_element_type.29.output_rows
  3.6 0.9 convert.7
  4.5 0.8 slice_bitcast_fusion.3
  5.3 0.9 maximum_bitcast_fusion.1.sent_a
  6.1 1.0 fusion.15
  7.1 61.6 %start.1 = (bf16[4,2,128,256]{3,2,1,0:T(8,128)(2,1)S(1)}, bf16[16,2,128,256]{3,2,1,0:T(8,128)(2,1)}, bf16[8,128,1024]{2,1,0:T(8,128)(2,1)}, bf16[48,512]{1,0:T(8...) custom-call(f32[8,8,640]{2,1,0:T(8,128)S(1)} %maximum_bitcast_fusion, ...), custom_call_target="tpu_custom_call" | custom-call | tf_op jit(solution)/shard_map/start/pallas_call | solution.py:963
  69.0 0.1 copy.67
  69.2 0.2 copy.64
  70.0 1.6 copy-done.2
  71.6 23.0 %attend.1 = (bf16[1024,256]{1,0:T(8,128)(2,1)S(1)}, f32[16,128]{1,0:T(8,128)S(1)}) custom-call(s32[16]{0:T(128)S(1)} %reshape.138.q_blocks, s32[64]{0:T(128)S(1)} %reshape.139.k_blocks, bf16[1024,256]{1,0:T(8,128)(2,1)S(1)} %bitcast.77, bf16[4096,256]{1,0:T(8,128)(2,1)S(1)} %bitcast.76), custom_call_target="tpu_custom_call" | custom-call | flops 4000000000 | bytes 4000000 | tf_op jit(solution)/shard_map/attend/pallas_call | solution.py:159
  94.6 105.5 %middle.1 = (bf16[128,1024]{1,0:T(8,128)(2,1)S(1)}, f32[128,1024]{1,0:T(8,128)S(1)}, f32[2,1024]{1,0:T(2,128)S(1)}, bf16[4,2,128,256]{3,2,1,0:T(8,128)(2,1)S(1)}...) custom-call(bf16[4,2,128,256]{3,2,1,0:T(8,128)(2,1)S(1)} %bitcast.66, ...), custom_call_target="tpu_custom_call" | custom-call | tf_op jit(solution)/shard_map/middle/pallas_call | solution.py:1327
  200.1 29.8 %attend_back.1 = (bf16[1024,256]{1,0:T(8,128)(2,1)S(1)}, bf16[4096,256]{1,0:T(8,128)(2,1)}) custom-call(s32[16]{0:T(128)S(1)} %reshape.138.q_blocks, s32[64]{0:T(128)S(1)} %reshape.139.k_blocks, bf16[1024,256]{1,0:T(8,128)(2,1)S(1)} %bitcast.78, bf16[4096,256]{1,0:T(8,128)(2,1)} %bitcast.75, bf16[1024,256]{1,0:T(8,128)(2,1)S(1)} %bitcast.79, ...), custom_call_target="tpu_custom_call" | custom-call | flops 10000000000 | bytes 8000000 | tf_op jit(solution)/shard_map/attend_back/pallas_call | solution.py:259
  230.0 59.8 %end.1 = (f32[128,1024]{1,0:T(8,128)S(1)}, f32[8,8,512]{2,1,0:T(8,128)S(1)}, f32[8,8,768]{2,1,0:T(8,128)S(1)}, f32[16,1024]{1,0:T(8,128)S(1)}, f32[48,512]{1,0:T(8,128)S(1)}, /*index=5*/f32[24,128]{1,0:T(8,128)S(1)}) custom-call(bf16[4,2,128,256]{3,2,1,0:T(8,128)(2,1)S(1)} %bitcast.63, bf16[16,2,128,256]{3,2,1,0:T(8,128)(2,1)} %bitcast.80, ...), custom_call_target="tpu_custom_call" | custom-call | tf_op jit(solution)/shard_map/end/pallas_call | solution.py:1665
  289.9 0.6 multiply_subtract_fusion.5
  290.6 0.7 multiply_subtract_fusion.2
  291.3 0.7 multiply_subtract_fusion.3
  292.0 0.7 multiply_subtract_fusion.4
  292.8 0.8 multiply_subtract_fusion.1
  293.6 0.9 multiply_subtract_fusion
  294.5 0.7 copy.74
  295.2 0.8 copy.75
  296.0 0.6 copy.76
  (73 shorter events, 1.6 us)
Async XLA Ops:
  0.7 6.5 %copy-start = (bf16[1,128,1024]{2,1,0:T(8,128)(2,1)S(1)}, bf16[1,128,1024]{2,1,0:T(8,128)(2,1)}, u32[]{:S(2)}) copy-start(bf16[1,128,1024]{2,1,0:T(8,128)(2,1)} %param.22) | copy-start | bytes 786436
  70.0 1.6 copy-start.2
  71.6 23.0 %copy-start.1 = (bf16[1,128,1024]{2,1,0:T(8,128)(2,1)S(1)}, bf16[1,128,1024]{2,1,0:T(8,128)(2,1)}, u32[]{:S(2)}) copy-start(bf16[1,128,1024]{2,1,0:T(8,128)(2,1)} %param.23) | copy-start | bytes 786436
  229.9 60.0 %copy-start.19 = (f32[18]{0:T(128)S(1)}, f32[18]{0:T(128)}, u32[]{:S(2)}) copy-start(f32[18]{0:T(128)} %param.31) | copy-start | bytes 220
  229.9 60.0 %copy-start.20 = (f32[18]{0:T(128)S(1)}, f32[18]{0:T(128)}, u32[]{:S(2)}) copy-start(f32[18]{0:T(128)} %param.37) | copy-start | bytes 220
  229.9 60.0 %copy-start.21 = (f32[18]{0:T(128)S(1)}, f32[18]{0:T(128)}, u32[]{:S(2)}) copy-start(f32[18]{0:T(128)} %param.43) | copy-start | bytes 220
  229.9 60.7 %copy-start.6 = (f32[16,1024]{1,0:T(8,128)S(1)}, f32[16,1024]{1,0:T(8,128)}, u32[]{:S(2)}) copy-start(f32[16,1024]{1,0:T(8,128)} %param.28) | copy-start | bytes 196612
  229.9 60.7 %copy-start.13 = (f32[16,1024]{1,0:T(8,128)S(1)}, f32[16,1024]{1,0:T(8,128)}, u32[]{:S(2)}) copy-start(f32[16,1024]{1,0:T(8,128)} %param.34) | copy-start | bytes 196612
  229.9 60.7 %copy-start.14 = (f32[16,1024]{1,0:T(8,128)S(1)}, f32[16,1024]{1,0:T(8,128)}, u32[]{:S(2)}) copy-start(f32[16,1024]{1,0:T(8,128)} %param.40) | copy-start | bytes 196612
  229.9 61.4 %copy-start.8 = (f32[8,2048]{1,0:T(8,128)S(1)}, f32[8,2048]{1,0:T(8,128)}, u32[]{:S(2)}) copy-start(f32[8,2048]{1,0:T(8,128)} %param.27) | copy-start | bytes 196612
  229.9 61.4 %copy-start.17 = (f32[8,2048]{1,0:T(8,128)S(1)}, f32[8,2048]{1,0:T(8,128)}, u32[]{:S(2)}) copy-start(f32[8,2048]{1,0:T(8,128)} %param.33) | copy-start | bytes 196612
  230.0 61.4 %copy-start.18 = (f32[8,2048]{1,0:T(8,128)S(1)}, f32[8,2048]{1,0:T(8,128)}, u32[]{:S(2)}) copy-start(f32[8,2048]{1,0:T(8,128)} %param.39) | copy-start | bytes 196612
  230.0 62.1 %copy-start.5 = (f32[8,2048]{1,0:T(8,128)S(1)}, f32[8,2048]{1,0:T(8,128)}, u32[]{:S(2)}) copy-start(f32[8,2048]{1,0:T(8,128)} %param.26) | copy-start | bytes 196612
  230.0 62.1 %copy-start.15 = (f32[8,2048]{1,0:T(8,128)S(1)}, f32[8,2048]{1,0:T(8,128)}, u32[]{:S(2)}) copy-start(f32[8,2048]{1,0:T(8,128)} %param.32) | copy-start | bytes 196612
  230.0 62.0 %copy-start.16 = (f32[8,2048]{1,0:T(8,128)S(1)}, f32[8,2048]{1,0:T(8,128)}, u32[]{:S(2)}) copy-start(f32[8,2048]{1,0:T(8,128)} %param.38) | copy-start | bytes 196612
  289.8 2.9 copy-start.4
  289.8 2.9 copy-start.11
  289.8 2.9 copy-start.12
  289.9 3.7 %copy-start.3 = (f32[8,6144]{1,0:T(8,128)S(1)}, f32[8,6144]{1,0:T(8,128)}, u32[]{:S(2)}) copy-start(f32[8,6144]{1,0:T(8,128)} %param.29) | copy-start | bytes 589828
  289.9 3.7 %copy-start.9 = (f32[8,6144]{1,0:T(8,128)S(1)}, f32[8,6144]{1,0:T(8,128)}, u32[]{:S(2)}) copy-start(f32[8,6144]{1,0:T(8,128)} %param.35) | copy-start | bytes 589828
  289.9 3.7 %copy-start.10 = (f32[8,6144]{1,0:T(8,128)S(1)}, f32[8,6144]{1,0:T(8,128)}, u32[]{:S(2)}) copy-start(f32[8,6144]{1,0:T(8,128)} %param.41) | copy-start | bytes 589828
  290.5 3.9 %copy-start.7 = (f32[8,8,256]{2,0,1:T(8,128)}, f32[8,8,256]{2,0,1:T(8,128)S(1)}, u32[]{:S(2)}) copy-start(f32[8,8,256]{2,0,1:T(8,128)S(1)} %slice.80) | copy-start | bytes 196612

commit v6 on v5

--- a/solution.py
+++ b/solution.py
@@ -19,7 +19,8 @@
 LONG = 3072
 ROWS = 128
 BLOCK = 64
-CHUNK = 512
+CHUNK = 1024
+TOGETHER = 4
 PACK_TOK = 4096
 RANKS = 8
 PLANE = 16
@@ -115,41 +116,50 @@
         part = values[c * CHUNK : (c + 1) * CHUNK, :].astype(F32)
         values_t[c] = part.T.astype(BF16)
 
-    def one_tile(tile, carry):
-        block = q_blocks[tile]
-        query = stacked_heads(q_ref, tile)
-        last = lax.div(block, CHUNK // BLOCK)
-
-        def one_chunk(c, state, masked):
-            total, mixed = state
-            chunk_keys = keys[pl.ds(pl.multiple_of(c * CHUNK, CHUNK), CHUNK), :]
-            weights = jnp.exp2(dot_nt(chunk_keys, query) * (SCALE * LOG2E))
-            if masked:
-                weights = jnp.where(allowed_keys(block, c), weights, 0.0)
-            total = total + jnp.sum(weights, axis=0, keepdims=True)
-            mixed = mixed + dot_nn(values_t[c], weights.astype(BF16))
-            return total, mixed
-
-        def two_chunks(j, state):
-            c = first + 2 * j
-            return one_chunk(c + 1, one_chunk(c, state, False), False)
-
-        first = first_chunk(block)
-        pairs = lax.div(last - first, 2)
-        state = (jnp.zeros((1, 2 * BLOCK), F32), jnp.zeros((HD, 2 * BLOCK), F32))
-        state = lax.fori_loop(0, pairs, two_chunks, state)
-        state = lax.fori_loop(
-            first + 2 * pairs, last, lambda c, s: one_chunk(c, s, False), state
-        )
-        total, mixed = one_chunk(last, state, True)
-        result = (mixed / total).T.astype(BF16)
-        rows = pl.ds(pl.multiple_of(tile * BLOCK, BLOCK), BLOCK)
-        out_ref[rows, :HD] = result[:BLOCK]
-        out_ref[rows, HD:] = result[BLOCK:]
-        lse_ref[pl.ds(tile, 1), :] = jnp.log2(total)
+    def one_chunk(query, block, c, state, masked):
+        total, mixed = state
+        chunk_keys = keys[pl.ds(pl.multiple_of(c * CHUNK, CHUNK), CHUNK), :]
+        weights = jnp.exp2(dot_nt(chunk_keys, query) * (SCALE * LOG2E))
+        if masked:
+            weights = jnp.where(allowed_keys(block, c), weights, 0.0)
+        total = total + jnp.sum(weights, axis=0, keepdims=True)
+        mixed = mixed + dot_nn(values_t[c], weights.astype(BF16))
+        return total, mixed
+
+    def some_tiles(group, carry):
+        tiles = [TOGETHER * group + u for u in range(TOGETHER)]
+        blocks = [q_blocks[tile] for tile in tiles]
+        queries = [stacked_heads(q_ref, tile) for tile in tiles]
+        firsts = [first_chunk(block) for block in blocks]
+        lasts = [lax.div(block, CHUNK // BLOCK) for block in blocks]
+        full = [last - first for first, last in zip(firsts, lasts)]
+        common = functools.reduce(jnp.minimum, full)
+
+        def step(u, j, state):
+            return one_chunk(queries[u], blocks[u], firsts[u] + j, state, False)
+
+        empty = (jnp.zeros((1, 2 * BLOCK), F32), jnp.zeros((HD, 2 * BLOCK), F32))
+        states = lax.fori_loop(
+            0,
+            common,
+            lambda j, s: tuple(step(u, j, s[u]) for u in range(TOGETHER)),
+            (empty,) * TOGETHER,
+        )
+        states = [
+            lax.fori_loop(common, full[u], functools.partial(step, u), states[u]) for u in range(TOGETHER)
+        ]
+        states = [
+            one_chunk(queries[u], blocks[u], lasts[u], states[u], True) for u in range(TOGETHER)
+        ]
+        for tile, (total, mixed) in zip(tiles, states):
+            result = (mixed / total).T.astype(BF16)
+            rows = pl.ds(pl.multiple_of(tile * BLOCK, BLOCK), BLOCK)
+            out_ref[rows, :HD] = result[:BLOCK]
+            out_ref[rows, HD:] = result[BLOCK:]
+            lse_ref[pl.ds(tile, 1), :] = jnp.log2(total)
         return carry
 
-    lax.fori_loop(0, q_ref.shape[0] // BLOCK, one_tile, 0)
+    lax.fori_loop(0, q_ref.shape[0] // BLOCK // TOGETHER, some_tiles, 0)
 
 
 def attend(q_blocks, k_blocks, q, kv):
@@ -207,41 +217,56 @@
     dk[...] = jnp.zeros_like(dk)
     dv[...] = jnp.zeros_like(dv)
 
-    def one_tile(tile, carry):
-        block = q_blocks[tile]
-        query = stacked_heads(q_ref, tile)
-        grad = stacked_heads(grad_ref, tile)
-        out = stacked_heads(out_ref, tile)
-        inner = jnp.sum((grad.astype(F32) * out.astype(F32)).T, axis=0, keepdims=True)
-        lse = lse_ref[pl.ds(tile, 1), :]
-        last = lax.div(block, CHUNK // BLOCK)
-
-        def one_chunk(c, dq, masked):
-            rows = pl.ds(pl.multiple_of(c * CHUNK, CHUNK), CHUNK)
-            probs = jnp.exp2(dot_nt(keys[rows, :], query) * (SCALE * LOG2E) - lse)
-            if masked:
-                probs = jnp.where(allowed_keys(block, c), probs, 0.0)
-            grad_probs = dot_nt(values[rows, :], grad)
-            grad_scores = (probs * (grad_probs - inner)).astype(BF16)
-            dv[rows, :] += dot_nn(probs.astype(BF16), grad)
-            dk[rows, :] += dot_nn(grad_scores, query)
-            return dq + dot_nn(keys_t[c], grad_scores)
-
-        def two_chunks(j, dq):
-            c = first + 2 * j
-            return one_chunk(c + 1, one_chunk(c, dq, False), False)
-
-        first = first_chunk(block)
-        pairs = lax.div(last - first, 2)
-        dq = lax.fori_loop(0, pairs, two_chunks, jnp.zeros((HD, 2 * BLOCK), F32))
-        dq = lax.fori_loop(first + 2 * pairs, last, lambda c, s: one_chunk(c, s, False), dq)
-        dq = (one_chunk(last, dq, True) * SCALE).T.astype(BF16)
-        rows = pl.ds(pl.multiple_of(tile * BLOCK, BLOCK), BLOCK)
-        dq_ref[rows, :HD] = dq[:BLOCK]
-        dq_ref[rows, HD:] = dq[BLOCK:]
+    def one_chunk(given, block, c, dq, masked):
+        query, grad, inner, lse = given
+        rows = pl.ds(pl.multiple_of(c * CHUNK, CHUNK), CHUNK)
+        probs = jnp.exp2(dot_nt(keys[rows, :], query) * (SCALE * LOG2E) - lse)
+        if masked:
+            probs = jnp.where(allowed_keys(block, c), probs, 0.0)
+        grad_probs = dot_nt(values[rows, :], grad)
+        grad_scores = (probs * (grad_probs - inner)).astype(BF16)
+        dv[rows, :] += dot_nn(probs.astype(BF16), grad)
+        dk[rows, :] += dot_nn(grad_scores, query)
+        return dq + dot_nn(keys_t[c], grad_scores)
+
+    def some_tiles(group, carry):
+        tiles = [TOGETHER * group + u for u in range(TOGETHER)]
+        blocks = [q_blocks[tile] for tile in tiles]
+        given = []
+        for tile in tiles:
+            query, grad = stacked_heads(q_ref, tile), stacked_heads(grad_ref, tile)
+            out = stacked_heads(out_ref, tile)
+            inner = jnp.sum((grad.astype(F32) * out.astype(F32)).T, axis=0, keepdims=True)
+            given.append((query, grad, inner, lse_ref[pl.ds(tile, 1), :]))
+        firsts = [first_chunk(block) for block in blocks]
+        lasts = [lax.div(block, CHUNK // BLOCK) for block in blocks]
+        full = [last - first for first, last in zip(firsts, lasts)]
+        common = functools.reduce(jnp.minimum, full)
+
+        def step(u, j, dq):
+            return one_chunk(given[u], blocks[u], firsts[u] + j, dq, False)
+
+        empty = jnp.zeros((HD, 2 * BLOCK), F32)
+        dqs = lax.fori_loop(
+            0,
+            common,
+            lambda j, s: tuple(step(u, j, s[u]) for u in range(TOGETHER)),
+            (empty,) * TOGETHER,
+        )
+        dqs = [
+            lax.fori_loop(common, full[u], functools.partial(step, u), dqs[u]) for u in range(TOGETHER)
+        ]
+        dqs = [
+            one_chunk(given[u], blocks[u], lasts[u], dqs[u], True) for u in range(TOGETHER)
+        ]
+        for tile, dq in zip(tiles, dqs):
+            dq = (dq * SCALE).T.astype(BF16)
+            rows = pl.ds(pl.multiple_of(tile * BLOCK, BLOCK), BLOCK)
+            dq_ref[rows, :HD] = dq[:BLOCK]
+            dq_ref[rows, HD:] = dq[BLOCK:]
         return carry
 
-    lax.fori_loop(0, q_ref.shape[0] // BLOCK, one_tile, 0)
+    lax.fori_loop(0, q_ref.shape[0] // BLOCK // TOGETHER, some_tiles, 0)
 
     def unsort(i, carry):
         at = pl.multiple_of(k_blocks[i] * BLOCK, BLOCK)

time: 298 us -> 278 us (0.933)
  Pallas kernels: 280 us -> 260 us
    pallas_call x1, Pallas kernels: 23 us -> 11.5 us  [attend(): pl.pallas_call(attend_kernel, out_shape=(jax.ShapeDtypeStruct(q.shape, BF...]
    pallas_call x1, Pallas kernels: 29.8 us -> 19.3 us  [attend_back(): pl.pallas_call(attend_back_kernel, out_shape=(jax.ShapeDtypeStruct(q.shap...]
where the time goes in v6:
time: 278 us; the launch traced here: 277 us
  Pallas kernels  260 us (94%)
  other arithmetic  8.09 us (3%)
  local copies, waits for them, and re-layouts  7.7 us (3%)
    pallas_call x1, Pallas kernels, middle(): pl.pallas_call(middle_kernel, out_shape=(jax.ShapeDtypeStruct(block, BF16...  106 us
    pallas_call x1, Pallas kernels, end(): pl.pallas_call(end_kernel, out_shape=(struct(block, F32), struct((RANKS,...  61.8 us
    pallas_call x1, Pallas kernels, start(): pl.pallas_call(start_kernel, out_shape=(struct((4, 2, ROWS, 256), BF16),...  61.6 us
    pallas_call x1, Pallas kernels, attend_back(): pl.pallas_call(attend_back_kernel, out_shape=(jax.ShapeDtypeStruct(q.shap...  19.3 us
    pallas_call x1, Pallas kernels, attend(): pl.pallas_call(attend_kernel, out_shape=(jax.ShapeDtypeStruct(q.shape, BF...  11.5 us

profile of v6, /device:TPU:1, one launch (start us, length us, event | category | flops | bytes accessed | tf_op | source)
XLA Modules:
  0.0 276.7 jit_solution(2533796579882446834)
XLA Ops:
  0.9 0.8 add_reduce_fusion
  2.0 0.7 pad_bitcast_fusion
  2.7 0.8 convert_element_type.29.output_rows
  3.6 0.9 convert.7
  4.5 0.8 slice_bitcast_fusion.3
  5.3 0.9 maximum_bitcast_fusion.1.sent_a
  6.1 1.0 fusion.15
  7.1 61.6 %start.1 = (bf16[4,2,128,256]{3,2,1,0:T(8,128)(2,1)S(1)}, bf16[16,2,128,256]{3,2,1,0:T(8,128)(2,1)}, bf16[8,128,1024]{2,1,0:T(8,128)(2,1)}, bf16[48,512]{1,0:T(8...) custom-call(f32[8,8,640]{2,1,0:T(8,128)S(1)} %maximum_bitcast_fusion, ...), custom_call_target="tpu_custom_call" | custom-call | tf_op jit(solution)/shard_map/start/pallas_call | solution.py:988
  69.0 0.1 copy.67
  69.2 0.2 copy.64
  70.0 1.6 copy-done.2
  71.6 11.5 %attend.1 = (bf16[1024,256]{1,0:T(8,128)(2,1)S(1)}, f32[16,128]{1,0:T(8,128)S(1)}) custom-call(s32[16]{0:T(128)S(1)} %reshape.138.q_blocks, s32[64]{0:T(128)S(1)} %reshape.139.k_blocks, bf16[1024,256]{1,0:T(8,128)(2,1)S(1)} %bitcast.77, bf16[4096,256]{1,0:T(8,128)(2,1)S(1)} %bitcast.76), custom_call_target="tpu_custom_call" | custom-call | flops 4000000000 | bytes 4000000 | tf_op jit(solution)/shard_map/attend/pallas_call | solution.py:169
  83.1 105.6 %middle.1 = (bf16[128,1024]{1,0:T(8,128)(2,1)S(1)}, f32[128,1024]{1,0:T(8,128)S(1)}, f32[2,1024]{1,0:T(2,128)S(1)}, bf16[4,2,128,256]{3,2,1,0:T(8,128)(2,1)S(1)}...) custom-call(bf16[4,2,128,256]{3,2,1,0:T(8,128)(2,1)S(1)} %bitcast.66, ...), custom_call_target="tpu_custom_call" | custom-call | tf_op jit(solution)/shard_map/middle/pallas_call | solution.py:1352
  188.7 19.3 %attend_back.1 = (bf16[1024,256]{1,0:T(8,128)(2,1)S(1)}, bf16[4096,256]{1,0:T(8,128)(2,1)}) custom-call(s32[16]{0:T(128)S(1)} %reshape.138.q_blocks, s32[64]{0:T(128)S(1)} %reshape.139.k_blocks, bf16[1024,256]{1,0:T(8,128)(2,1)S(1)} %bitcast.78, bf16[4096,256]{1,0:T(8,128)(2,1)} %bitcast.75, bf16[1024,256]{1,0:T(8,128)(2,1)S(1)} %bitcast.79, ...), custom_call_target="tpu_custom_call" | custom-call | flops 10000000000 | bytes 8000000 | tf_op jit(solution)/shard_map/attend_back/pallas_call | solution.py:284
  208.1 61.8 %end.1 = (f32[128,1024]{1,0:T(8,128)S(1)}, f32[8,8,512]{2,1,0:T(8,128)S(1)}, f32[8,8,768]{2,1,0:T(8,128)S(1)}, f32[16,1024]{1,0:T(8,128)S(1)}, f32[48,512]{1,0:T(8,128)S(1)}, /*index=5*/f32[24,128]{1,0:T(8,128)S(1)}) custom-call(bf16[4,2,128,256]{3,2,1,0:T(8,128)(2,1)S(1)} %bitcast.63, bf16[16,2,128,256]{3,2,1,0:T(8,128)(2,1)} %bitcast.80, ...), custom_call_target="tpu_custom_call" | custom-call | tf_op jit(solution)/shard_map/end/pallas_call | solution.py:1690
  270.0 0.6 multiply_subtract_fusion.5
  270.7 0.7 multiply_subtract_fusion.2
  271.4 0.7 multiply_subtract_fusion.3
  272.1 0.7 multiply_subtract_fusion.4
  272.9 0.8 multiply_subtract_fusion.1
  273.7 0.9 multiply_subtract_fusion
  274.6 0.7 copy.74
  275.3 0.8 copy.75
  276.1 0.6 copy.76
  (73 shorter events, 1.6 us)
Async XLA Ops:
  0.7 6.5 %copy-start = (bf16[1,128,1024]{2,1,0:T(8,128)(2,1)S(1)}, bf16[1,128,1024]{2,1,0:T(8,128)(2,1)}, u32[]{:S(2)}) copy-start(bf16[1,128,1024]{2,1,0:T(8,128)(2,1)} %param.22) | copy-start | bytes 786436
  70.0 1.6 copy-start.2
  71.6 11.5 %copy-start.1 = (bf16[1,128,1024]{2,1,0:T(8,128)(2,1)S(1)}, bf16[1,128,1024]{2,1,0:T(8,128)(2,1)}, u32[]{:S(2)}) copy-start(bf16[1,128,1024]{2,1,0:T(8,128)(2,1)} %param.23) | copy-start | bytes 786436
  208.0 62.0 %copy-start.19 = (f32[18]{0:T(128)S(1)}, f32[18]{0:T(128)}, u32[]{:S(2)}) copy-start(f32[18]{0:T(128)} %param.31) | copy-start | bytes 220
  208.0 62.0 %copy-start.20 = (f32[18]{0:T(128)S(1)}, f32[18]{0:T(128)}, u32[]{:S(2)}) copy-start(f32[18]{0:T(128)} %param.37) | copy-start | bytes 220
  208.0 62.0 %copy-start.21 = (f32[18]{0:T(128)S(1)}, f32[18]{0:T(128)}, u32[]{:S(2)}) copy-start(f32[18]{0:T(128)} %param.43) | copy-start | bytes 220
  208.0 62.7 %copy-start.6 = (f32[16,1024]{1,0:T(8,128)S(1)}, f32[16,1024]{1,0:T(8,128)}, u32[]{:S(2)}) copy-start(f32[16,1024]{1,0:T(8,128)} %param.28) | copy-start | bytes 196612
  208.0 62.7 %copy-start.13 = (f32[16,1024]{1,0:T(8,128)S(1)}, f32[16,1024]{1,0:T(8,128)}, u32[]{:S(2)}) copy-start(f32[16,1024]{1,0:T(8,128)} %param.34) | copy-start | bytes 196612
  208.0 62.7 %copy-start.14 = (f32[16,1024]{1,0:T(8,128)S(1)}, f32[16,1024]{1,0:T(8,128)}, u32[]{:S(2)}) copy-start(f32[16,1024]{1,0:T(8,128)} %param.40) | copy-start | bytes 196612
  208.0 63.4 %copy-start.8 = (f32[8,2048]{1,0:T(8,128)S(1)}, f32[8,2048]{1,0:T(8,128)}, u32[]{:S(2)}) copy-start(f32[8,2048]{1,0:T(8,128)} %param.27) | copy-start | bytes 196612
  208.1 63.4 %copy-start.17 = (f32[8,2048]{1,0:T(8,128)S(1)}, f32[8,2048]{1,0:T(8,128)}, u32[]{:S(2)}) copy-start(f32[8,2048]{1,0:T(8,128)} %param.33) | copy-start | bytes 196612
  208.1 63.3 %copy-start.18 = (f32[8,2048]{1,0:T(8,128)S(1)}, f32[8,2048]{1,0:T(8,128)}, u32[]{:S(2)}) copy-start(f32[8,2048]{1,0:T(8,128)} %param.39) | copy-start | bytes 196612
  208.1 64.0 %copy-start.5 = (f32[8,2048]{1,0:T(8,128)S(1)}, f32[8,2048]{1,0:T(8,128)}, u32[]{:S(2)}) copy-start(f32[8,2048]{1,0:T(8,128)} %param.26) | copy-start | bytes 196612
  208.1 64.0 %copy-start.15 = (f32[8,2048]{1,0:T(8,128)S(1)}, f32[8,2048]{1,0:T(8,128)}, u32[]{:S(2)}) copy-start(f32[8,2048]{1,0:T(8,128)} %param.32) | copy-start | bytes 196612
  208.1 64.0 %copy-start.16 = (f32[8,2048]{1,0:T(8,128)S(1)}, f32[8,2048]{1,0:T(8,128)}, u32[]{:S(2)}) copy-start(f32[8,2048]{1,0:T(8,128)} %param.38) | copy-start | bytes 196612
  269.9 2.9 %copy-start.4 = (f32[24,1024]{1,0:T(8,128)S(1)}, f32[24,1024]{1,0:T(8,128)}, u32[]{:S(2)}) copy-start(f32[24,1024]{1,0:T(8,128)} %param.30) | copy-start | bytes 294916
  269.9 2.9 %copy-start.11 = (f32[24,1024]{1,0:T(8,128)S(1)}, f32[24,1024]{1,0:T(8,128)}, u32[]{:S(2)}) copy-start(f32[24,1024]{1,0:T(8,128)} %param.36) | copy-start | bytes 294916
  269.9 2.9 %copy-start.12 = (f32[24,1024]{1,0:T(8,128)S(1)}, f32[24,1024]{1,0:T(8,128)}, u32[]{:S(2)}) copy-start(f32[24,1024]{1,0:T(8,128)} %param.42) | copy-start | bytes 294916
  270.0 3.7 %copy-start.3 = (f32[8,6144]{1,0:T(8,128)S(1)}, f32[8,6144]{1,0:T(8,128)}, u32[]{:S(2)}) copy-start(f32[8,6144]{1,0:T(8,128)} %param.29) | copy-start | bytes 589828
  270.0 3.7 %copy-start.9 = (f32[8,6144]{1,0:T(8,128)S(1)}, f32[8,6144]{1,0:T(8,128)}, u32[]{:S(2)}) copy-start(f32[8,6144]{1,0:T(8,128)} %param.35) | copy-start | bytes 589828
  270.0 3.7 %copy-start.10 = (f32[8,6144]{1,0:T(8,128)S(1)}, f32[8,6144]{1,0:T(8,128)}, u32[]{:S(2)}) copy-start(f32[8,6144]{1,0:T(8,128)} %param.41) | copy-start | bytes 589828
  270.6 3.9 %copy-start.7 = (f32[8,8,256]{2,0,1:T(8,128)}, f32[8,8,256]{2,0,1:T(8,128)S(1)}, u32[]{:S(2)}) copy-start(f32[8,8,256]{2,0,1:T(8,128)S(1)} %slice.80) | copy-start | bytes 196612

commit v7 on v6

--- a/solution.py
+++ b/solution.py
@@ -1615,17 +1615,35 @@
             else:
                 gain_q = gain_q + grad_gain
         grad_qkv[at, 384:] = grad_kv[:, HD:]
+        return gain_q, gain_k
+
+    nothing = jnp.zeros((1, HD), F32)
+    gain_q, gain_k = lax.fori_loop(0, 4, project_back, (nothing, nothing))
+
+    def qkv_rows(j, carry):
+        cols = pl.ds(pl.multiple_of(j * 256, 256), 256)
+        grads = dot_tn(all_tokens[:, :, cols].reshape(RANKS * ROWS, 256), grad_qkv[...])
+        qkv_lines[lax.div(j, 2), pl.ds(lax.rem(j, 2) * 2, 2)] = grads.astype(BF16).reshape(
+            2, 4, 32, 512
+        )
+        return carry
+
+    lax.fori_loop(0, 4, qkv_rows, 0)
+    qkv_back.begin()
+
+    def put_tokens(i, carry):
+        off = gray(3 - i)
+        to_z = lax.rem(z + off, 4)
+        at = pl.ds(pl.multiple_of(to_z * 2 * ROWS, 2 * ROWS), 2 * ROWS)
         sums.put(0, off, dot_nt(grad_qkv[at, :], qkv_part[...]))
 
         @pl.when(i == 1)
         def _():
             sums.first(0)
 
-        return gain_q, gain_k
-
-    nothing = jnp.zeros((1, HD), F32)
-    gain_q, gain_k = lax.fori_loop(0, 4, project_back, (nothing, nothing))
-
+        return carry
+
+    lax.fori_loop(0, 4, put_tokens, 0)
     for j in range(16):
         gains_column[rank, j : j + 1, :] = gains_grad[
             j // 8 : j // 8 + 1, j % 8 * HD : (j % 8 + 1) * HD
@@ -1635,32 +1653,20 @@
     gains_column[rank, 18:24, :] = jnp.zeros((6, HD), F32)
     gains_in.begin()
     sums.second(0)
+    qkv_back.pass_on()
     output_back.pass_on()
-
-    def qkv_rows(j, carry):
-        cols = pl.ds(pl.multiple_of(j * 256, 256), 256)
-        grads = dot_tn(all_tokens[:, :, cols].reshape(RANKS * ROWS, 256), grad_qkv[...])
-        qkv_lines[lax.div(j, 2), pl.ds(lax.rem(j, 2) * 2, 2)] = grads.astype(BF16).reshape(
-            2, 4, 32, 512
-        )
-        return carry
-
-    lax.fori_loop(0, 4, qkv_rows, 0)
-    qkv_back.begin()
-
     gains_in.arrive()
     gains_plane[here] = jnp.sum(gains_column[...], axis=0)
     gains_over.begin()
     token_grad[...] = grad_hidden[...] + sums.total(0)
-    qkv_back.pass_on()
-    for half in range(2):
-        output_total[:, half * 512 : half * 512 + 512] = output_back.total(half)
-    output_swap.begin()
 
     for half in range(2):
         column_a[pl.ds(half * 4, 4)] = qkv_back.total(half).reshape(4, 8, 512)
     own_a.start()
     to_a.begin()
+    for half in range(2):
+        output_total[:, half * 512 : half * 512 + 512] = output_back.total(half)
+    output_swap.begin()
     gains_over.arrive()
     gains_sum[...] = jnp.sum(gains_plane[...], axis=0)
     to_b.arrive()

time: 278 us -> 272 us (0.978)
  Pallas kernels: 260 us -> 254 us
    pallas_call x1, Pallas kernels: 61.8 us -> 53.8 us  [end(): pl.pallas_call(end_kernel, out_shape=(struct(block, F32), struct((RANKS,...]
where the time goes in v7:
time: 272 us; the launch traced here: 271 us
  Pallas kernels  254 us (93%)
  other arithmetic  8.09 us (3%)
  local copies, waits for them, and re-layouts  7.7 us (3%)
    pallas_call x1, Pallas kernels, middle(): pl.pallas_call(middle_kernel, out_shape=(jax.ShapeDtypeStruct(block, BF16...  105 us
    pallas_call x1, Pallas kernels, start(): pl.pallas_call(start_kernel, out_shape=(struct((4, 2, ROWS, 256), BF16),...  61.6 us
    pallas_call x1, Pallas kernels, end(): pl.pallas_call(end_kernel, out_shape=(struct(block, F32), struct((RANKS,...  53.8 us
    pallas_call x1, Pallas kernels, attend_back(): pl.pallas_call(attend_back_kernel, out_shape=(jax.ShapeDtypeStruct(q.shap...  20.8 us
    pallas_call x1, Pallas kernels, attend(): pl.pallas_call(attend_kernel, out_shape=(jax.ShapeDtypeStruct(q.shape, BF...  12.9 us

profile of v7, /device:TPU:1, one launch (start us, length us, event | category | flops | bytes accessed | tf_op | source)
XLA Modules:
  0.0 271.4 jit_solution(764600521140024522)
XLA Ops:
  0.9 0.8 add_reduce_fusion
  2.0 0.7 pad_bitcast_fusion
  2.7 0.8 convert_element_type.29.output_rows
  3.6 0.9 convert.7
  4.5 0.8 slice_bitcast_fusion.3
  5.3 0.9 maximum_bitcast_fusion.1.sent_a
  6.1 1.0 fusion.15
  7.1 61.6 %start.1 = (bf16[4,2,128,256]{3,2,1,0:T(8,128)(2,1)S(1)}, bf16[16,2,128,256]{3,2,1,0:T(8,128)(2,1)}, bf16[8,128,1024]{2,1,0:T(8,128)(2,1)}, bf16[48,512]{1,0:T(8...) custom-call(f32[8,8,640]{2,1,0:T(8,128)S(1)} %maximum_bitcast_fusion, ...), custom_call_target="tpu_custom_call" | custom-call | tf_op jit(solution)/shard_map/start/pallas_call | solution.py:988
  69.0 0.1 copy.67
  69.2 0.2 copy.64
  70.0 1.6 copy-done.2
  71.6 12.9 %attend.1 = (bf16[1024,256]{1,0:T(8,128)(2,1)S(1)}, f32[16,128]{1,0:T(8,128)S(1)}) custom-call(s32[16]{0:T(128)S(1)} %reshape.138.q_blocks, s32[64]{0:T(128)S(1)} %reshape.139.k_blocks, bf16[1024,256]{1,0:T(8,128)(2,1)S(1)} %bitcast.77, bf16[4096,256]{1,0:T(8,128)(2,1)S(1)} %bitcast.76), custom_call_target="tpu_custom_call" | custom-call | flops 4000000000 | bytes 4000000 | tf_op jit(solution)/shard_map/attend/pallas_call | solution.py:169
  84.5 105.3 %middle.1 = (bf16[128,1024]{1,0:T(8,128)(2,1)S(1)}, f32[128,1024]{1,0:T(8,128)S(1)}, f32[2,1024]{1,0:T(2,128)S(1)}, bf16[4,2,128,256]{3,2,1,0:T(8,128)(2,1)S(1)}...) custom-call(bf16[4,2,128,256]{3,2,1,0:T(8,128)(2,1)S(1)} %bitcast.66, ...), custom_call_target="tpu_custom_call" | custom-call | tf_op jit(solution)/shard_map/middle/pallas_call | solution.py:1352
  189.8 20.8 %attend_back.1 = (bf16[1024,256]{1,0:T(8,128)(2,1)S(1)}, bf16[4096,256]{1,0:T(8,128)(2,1)}) custom-call(s32[16]{0:T(128)S(1)} %reshape.138.q_blocks, s32[64]{0:T(128)S(1)} %reshape.139.k_blocks, bf16[1024,256]{1,0:T(8,128)(2,1)S(1)} %bitcast.78, bf16[4096,256]{1,0:T(8,128)(2,1)} %bitcast.75, bf16[1024,256]{1,0:T(8,128)(2,1)S(1)} %bitcast.79, ...), custom_call_target="tpu_custom_call" | custom-call | flops 10000000000 | bytes 8000000 | tf_op jit(solution)/shard_map/attend_back/pallas_call | solution.py:284
  210.7 53.8 %end.1 = (f32[128,1024]{1,0:T(8,128)S(1)}, f32[8,8,512]{2,1,0:T(8,128)S(1)}, f32[8,8,768]{2,1,0:T(8,128)S(1)}, f32[16,1024]{1,0:T(8,128)S(1)}, f32[48,512]{1,0:T(8,128)S(1)}, /*index=5*/f32[24,128]{1,0:T(8,128)S(1)}) custom-call(bf16[4,2,128,256]{3,2,1,0:T(8,128)(2,1)S(1)} %bitcast.63, bf16[16,2,128,256]{3,2,1,0:T(8,128)(2,1)} %bitcast.80, ...), custom_call_target="tpu_custom_call" | custom-call | tf_op jit(solution)/shard_map/end/pallas_call | solution.py:1696
  264.7 0.6 multiply_subtract_fusion.5
  265.4 0.7 multiply_subtract_fusion.2
  266.1 0.7 multiply_subtract_fusion.3
  266.8 0.7 multiply_subtract_fusion.4
  267.5 0.8 multiply_subtract_fusion.1
  268.3 0.9 multiply_subtract_fusion
  269.2 0.7 copy.74
  269.9 0.8 copy.75
  270.7 0.6 copy.76
  (73 shorter events, 1.6 us)
Async XLA Ops:
  0.7 6.5 %copy-start = (bf16[1,128,1024]{2,1,0:T(8,128)(2,1)S(1)}, bf16[1,128,1024]{2,1,0:T(8,128)(2,1)}, u32[]{:S(2)}) copy-start(bf16[1,128,1024]{2,1,0:T(8,128)(2,1)} %param.22) | copy-start | bytes 786436
  70.0 1.6 copy-start.2
  71.6 12.9 %copy-start.1 = (bf16[1,128,1024]{2,1,0:T(8,128)(2,1)S(1)}, bf16[1,128,1024]{2,1,0:T(8,128)(2,1)}, u32[]{:S(2)}) copy-start(bf16[1,128,1024]{2,1,0:T(8,128)(2,1)} %param.23) | copy-start | bytes 786436
  210.6 54.0 %copy-start.19 = (f32[18]{0:T(128)S(1)}, f32[18]{0:T(128)}, u32[]{:S(2)}) copy-start(f32[18]{0:T(128)} %param.31) | copy-start | bytes 220
  210.6 54.0 %copy-start.20 = (f32[18]{0:T(128)S(1)}, f32[18]{0:T(128)}, u32[]{:S(2)}) copy-start(f32[18]{0:T(128)} %param.37) | copy-start | bytes 220
  210.6 54.0 %copy-start.21 = (f32[18]{0:T(128)S(1)}, f32[18]{0:T(128)}, u32[]{:S(2)}) copy-start(f32[18]{0:T(128)} %param.43) | copy-start | bytes 220
  210.6 54.7 %copy-start.6 = (f32[16,1024]{1,0:T(8,128)S(1)}, f32[16,1024]{1,0:T(8,128)}, u32[]{:S(2)}) copy-start(f32[16,1024]{1,0:T(8,128)} %param.28) | copy-start | bytes 196612
  210.6 54.7 %copy-start.13 = (f32[16,1024]{1,0:T(8,128)S(1)}, f32[16,1024]{1,0:T(8,128)}, u32[]{:S(2)}) copy-start(f32[16,1024]{1,0:T(8,128)} %param.34) | copy-start | bytes 196612
  210.7 54.7 %copy-start.14 = (f32[16,1024]{1,0:T(8,128)S(1)}, f32[16,1024]{1,0:T(8,128)}, u32[]{:S(2)}) copy-start(f32[16,1024]{1,0:T(8,128)} %param.40) | copy-start | bytes 196612
  210.7 55.4 %copy-start.8 = (f32[8,2048]{1,0:T(8,128)S(1)}, f32[8,2048]{1,0:T(8,128)}, u32[]{:S(2)}) copy-start(f32[8,2048]{1,0:T(8,128)} %param.27) | copy-start | bytes 196612
  210.7 55.4 %copy-start.17 = (f32[8,2048]{1,0:T(8,128)S(1)}, f32[8,2048]{1,0:T(8,128)}, u32[]{:S(2)}) copy-start(f32[8,2048]{1,0:T(8,128)} %param.33) | copy-start | bytes 196612
  210.7 55.4 %copy-start.18 = (f32[8,2048]{1,0:T(8,128)S(1)}, f32[8,2048]{1,0:T(8,128)}, u32[]{:S(2)}) copy-start(f32[8,2048]{1,0:T(8,128)} %param.39) | copy-start | bytes 196612
  210.7 56.1 %copy-start.5 = (f32[8,2048]{1,0:T(8,128)S(1)}, f32[8,2048]{1,0:T(8,128)}, u32[]{:S(2)}) copy-start(f32[8,2048]{1,0:T(8,128)} %param.26) | copy-start | bytes 196612
  210.7 56.1 %copy-start.15 = (f32[8,2048]{1,0:T(8,128)S(1)}, f32[8,2048]{1,0:T(8,128)}, u32[]{:S(2)}) copy-start(f32[8,2048]{1,0:T(8,128)} %param.32) | copy-start | bytes 196612
  210.7 56.1 %copy-start.16 = (f32[8,2048]{1,0:T(8,128)S(1)}, f32[8,2048]{1,0:T(8,128)}, u32[]{:S(2)}) copy-start(f32[8,2048]{1,0:T(8,128)} %param.38) | copy-start | bytes 196612
  264.6 2.9 %copy-start.4 = (f32[24,1024]{1,0:T(8,128)S(1)}, f32[24,1024]{1,0:T(8,128)}, u32[]{:S(2)}) copy-start(f32[24,1024]{1,0:T(8,128)} %param.30) | copy-start | bytes 294916
  264.6 2.9 %copy-start.11 = (f32[24,1024]{1,0:T(8,128)S(1)}, f32[24,1024]{1,0:T(8,128)}, u32[]{:S(2)}) copy-start(f32[24,1024]{1,0:T(8,128)} %param.36) | copy-start | bytes 294916
  264.6 2.9 %copy-start.12 = (f32[24,1024]{1,0:T(8,128)S(1)}, f32[24,1024]{1,0:T(8,128)}, u32[]{:S(2)}) copy-start(f32[24,1024]{1,0:T(8,128)} %param.42) | copy-start | bytes 294916
  264.6 3.7 %copy-start.3 = (f32[8,6144]{1,0:T(8,128)S(1)}, f32[8,6144]{1,0:T(8,128)}, u32[]{:S(2)}) copy-start(f32[8,6144]{1,0:T(8,128)} %param.29) | copy-start | bytes 589828
  264.6 3.7 %copy-start.9 = (f32[8,6144]{1,0:T(8,128)S(1)}, f32[8,6144]{1,0:T(8,128)}, u32[]{:S(2)}) copy-start(f32[8,6144]{1,0:T(8,128)} %param.35) | copy-start | bytes 589828
  264.6 3.7 %copy-start.10 = (f32[8,6144]{1,0:T(8,128)S(1)}, f32[8,6144]{1,0:T(8,128)}, u32[]{:S(2)}) copy-start(f32[8,6144]{1,0:T(8,128)} %param.41) | copy-start | bytes 589828
  265.3 3.9 %copy-start.7 = (f32[8,8,256]{2,0,1:T(8,128)}, f32[8,8,256]{2,0,1:T(8,128)S(1)}, u32[]{:S(2)}) copy-start(f32[8,8,256]{2,0,1:T(8,128)S(1)} %slice.80) | copy-start | bytes 196612
